TPU v7x, 512 devices: a whole 4x4x16 slice. The times are simulated.
512 devices in a mesh: enc: 128 (over y, z, core), agg: 4 (over x).
Axes of the slice: x: 4, y: 4, z: 16, core: 2. Of those that a mesh axis runs over, the one named last changes fastest.
Arguments:
- features: bfloat16 [18432, 4, 2048], P('enc'), may hold values from -6 to 6
- tile_slide: int32 [18432, 1], P('enc'), may hold values from 0 to 127; in each aligned block of 144 rows (0 to 143, 144 to 287, ...) at most 2 rows name the same one
- tile_pos: int32 [18432], P('enc'), may hold values from 0 to 255
- slide_owner: int32 [128], replicated, may hold values from 0 to 127, each once
- slide_label: int32 [128], replicated, may hold values from 0 to 31
- enc_weight: bfloat16 [2048, 768], P(None, 'agg'), may hold values from -0.125 to 0.125
- enc_bias: float32 [768], P('agg'), may hold values from -3 to 3
- norm_gain: float32 [768], replicated, may hold values from 0.1 to 1.9
- qkv_weight: bfloat16 [768, 2304], P('enc'), may hold values from -0.21875 to 0.21875
- out_weight: bfloat16 [768, 768], P('enc'), may hold values from -0.21875 to 0.21875
- cls_weight: float32 [768, 32], replicated, may hold values from -0.6 to 0.6
Outputs:
- owner_logits: float32 [128, 32], P('enc')
- enc_grad: float32 [2048, 768], P(None, 'agg')
- bias_grad: float32 [768], P('agg')
Inputs may be any that keep to these rules, and one draw needn't show every extreme that they name: `tile_slide`: in each aligned block of 144 tiles (the tiles of one index of enc) no slide has more than 2 tiles, and some slide has exactly that many in some block; every slide has a tile. `slide_owner`: each index of enc owns exactly one slide.
All inputs are finite; a program needn't handle non-finite values.
Results may differ from a plain program's by a relative error of at most 0.012.
Values may be sent and summed in bfloat16 or wider, within the bound.
No kernel may reach another device: no remote copies, remote signals or barrier semaphores. Data moves between devices by JAX's collectives and lax.ppermute only.
A program may use at most 64 MiB of HBM per device.

v0:
```python
import jax
import jax.numpy as jnp
from jax import lax
from jax.sharding import PartitionSpec as P

CH = 2048
POS = 4
EMB = 768
HEADS = 12
CLASSES = 32
HD = 64


eps = 1e-05


def dilation_table():
    head_ids = jnp.arange(HEADS, dtype=jnp.int32)
    group_ids = head_ids % 3
    segment_len = jnp.left_shift(jnp.int32(64), group_ids)
    stride_len = jnp.left_shift(jnp.int32(1), group_ids)
    return (segment_len, stride_len)


def visible_mask(query_pos, key_pos, segment_len, stride_len):
    seg_col = segment_len[:, None, None]
    str_col = stride_len[:, None, None]
    same_seg = query_pos[None, :, None] // seg_col == key_pos[None, None, :] // seg_col
    same_res = query_pos[None, :, None] % str_col == key_pos[None, None, :] % str_col
    return same_seg & same_res


def layer_norm(row_values, norm_gain):
    centred = row_values - jnp.mean(row_values, axis=-1, keepdims=True)
    variance = jnp.mean(centred * centred, axis=-1, keepdims=True)
    inv_std = lax.rsqrt(variance + eps)
    normed = centred * inv_std
    return (normed, inv_std, (normed * norm_gain).astype(jnp.bfloat16))


def norm_backward(grad_normed, normed, inv_std, norm_gain):
    scaled = grad_normed * norm_gain
    return inv_std * (
        scaled
        - jnp.mean(scaled, axis=-1, keepdims=True)
        - normed * jnp.mean(scaled * normed, axis=-1, keepdims=True)
    )


def attention_weights(query_heads, query_place, query_live, key_heads, key_place, key_live):
    segment_len, stride_len = dilation_table()
    visible = (
        visible_mask(query_place, key_place, segment_len, stride_len)
        & key_live[None, None, :]
        & query_live[None, :, None]
    )
    scores = jnp.einsum("qhd,khd->hqk", query_heads, key_heads, preferred_element_type=jnp.float32)
    masked = jnp.where(visible, scores, -1e30)
    row_max = jnp.max(masked, axis=-1, keepdims=True)
    weights = jnp.where(visible, jnp.exp(masked - row_max), 0.0)
    row_total = jnp.sum(weights, axis=-1, keepdims=True)
    return weights / jnp.where(row_total > 0, row_total, 1.0)


def on_device(
    features,
    tile_slide,
    tile_pos,
    slide_owner,
    slide_label,
    enc_weight,
    enc_bias,
    norm_gain,
    qkv_weight,
    out_weight,
    cls_weight,
):
    enc_count = lax.axis_size("enc")
    tile_count = features.shape[0]
    local_cols = enc_weight.shape[1]
    slide_count = slide_owner.shape[0]
    send_slots = max(2, 2 * tile_count // enc_count)
    slot_total = enc_count * send_slots
    flattened = features.reshape(tile_count * POS, CH)
    preact = (
        jnp.dot(flattened, enc_weight, preferred_element_type=jnp.float32).reshape(
            tile_count, POS, local_cols
        )
        + enc_bias
    )
    tile_rows = jnp.mean(jnp.maximum(preact, 0.0), axis=1).astype(jnp.bfloat16)
    slide_ids = tile_slide[:, 0]
    slide_range = jnp.arange(slide_count, dtype=jnp.int32)
    owners = jnp.sum(
        jnp.where(slide_ids[:, None] == slide_range[None, :], slide_owner[None, :], 0), axis=1
    )
    tile_range = jnp.arange(tile_count, dtype=jnp.int32)
    earlier = tile_range[None, :] < tile_range[:, None]
    slot_rank = jnp.sum(((owners[:, None] == owners[None, :]) & earlier).astype(jnp.int32), axis=1)
    target = owners * send_slots + slot_rank
    placing = (jnp.arange(slot_total, dtype=jnp.int32)[:, None] == target[None, :]).astype(
        jnp.bfloat16
    )
    send_rows = (
        jnp.dot(placing, tile_rows, preferred_element_type=jnp.float32)
        .astype(jnp.bfloat16)
        .reshape(enc_count, send_slots, local_cols)
    )
    cell_tags = (tile_pos + 1).astype(jnp.bfloat16)
    send_tags = (
        jnp.dot(placing, cell_tags, preferred_element_type=jnp.float32)
        .astype(jnp.bfloat16)
        .reshape(enc_count, send_slots, 1)
    )
    slot_rows, slot_tags = (
        lax.all_to_all(
            lax.all_to_all(send_rows, "enc", split_axis=0, concat_axis=0, tiled=True),
            "agg",
            split_axis=0,
            concat_axis=2,
            tiled=True,
        ),
        lax.all_to_all(
            lax.all_to_all(send_tags, "enc", split_axis=0, concat_axis=0, tiled=True),
            "agg",
            split_axis=0,
            concat_axis=2,
            tiled=True,
        ),
    )
    local_slots = slot_rows.shape[0] * send_slots
    rows_in = slot_rows.reshape(local_slots, EMB)
    tags = slot_tags[:, :, 0].reshape(local_slots)
    row_values = rows_in.astype(jnp.float32)
    live = tags > 0
    live_values = live.astype(jnp.float32)
    normed, inv_std, normed_in = layer_norm(row_values, norm_gain)
    full_qkv, full_out = (
        lax.all_gather(qkv_weight, "enc", axis=0, tiled=True),
        lax.all_gather(out_weight, "enc", axis=0, tiled=True),
    )
    qkv_all = jnp.dot(normed_in, full_qkv, preferred_element_type=jnp.float32)
    score_scale = HD ** (-0.5)
    queries = (qkv_all[:, :EMB] * score_scale).astype(jnp.bfloat16)
    key_rows = qkv_all[:, EMB : 2 * EMB].astype(jnp.bfloat16)
    value_rows = qkv_all[:, 2 * EMB :].astype(jnp.bfloat16)
    all_keys, all_values, all_tags = (
        lax.all_gather(key_rows, "agg", axis=0, tiled=True),
        lax.all_gather(value_rows, "agg", axis=0, tiled=True),
        lax.all_gather(tags, "agg", axis=0, tiled=True),
    )
    key_total = all_keys.shape[0]
    query_pos = tags.astype(jnp.int32) - 1
    key_pos = all_tags.astype(jnp.int32) - 1
    key_live = all_tags > 0
    query_heads = queries.reshape(local_slots, HEADS, HD)
    key_heads = all_keys.reshape(key_total, HEADS, HD)
    value_heads = all_values.reshape(key_total, HEADS, HD)
    weights = attention_weights(query_heads, query_pos, live, key_heads, key_pos, key_live)
    probs_in = weights.astype(jnp.bfloat16)
    mixed = (
        jnp.einsum("hqk,khd->qhd", probs_in, value_heads, preferred_element_type=jnp.float32)
        .reshape(local_slots, EMB)
        .astype(jnp.bfloat16)
    )
    projected = jnp.dot(mixed, full_out, preferred_element_type=jnp.float32)
    outputs = row_values + projected
    partial_total = jnp.sum(outputs * live_values[:, None], axis=0)
    slide_total = lax.psum(partial_total, "agg")
    tile_number = jnp.sum(key_live.astype(jnp.float32))
    pooled = slide_total / tile_number
    owner_index = lax.axis_index("enc")
    my_label = jnp.sum(jnp.where(slide_owner == owner_index, slide_label, 0))
    logits = jnp.dot(pooled, cls_weight, precision=lax.Precision.HIGHEST)
    class_probs = jax.nn.softmax(logits)
    grad_logits = class_probs - (jnp.arange(CLASSES, dtype=jnp.int32) == my_label).astype(
        jnp.float32
    )
    grad_pooled = jnp.dot(cls_weight, grad_logits, precision=lax.Precision.HIGHEST) / tile_number
    pooled_in = grad_pooled.astype(jnp.bfloat16)
    grad_mixed_row = jnp.dot(full_out, pooled_in, preferred_element_type=jnp.float32).astype(
        jnp.bfloat16
    )
    grad_mixed = jnp.where(live[:, None], grad_mixed_row[None, :], jnp.zeros((), jnp.bfloat16))
    grad_heads = grad_mixed.reshape(local_slots, HEADS, HD)
    grad_att = jnp.einsum(
        "qhd,khd->hqk", grad_heads, value_heads, preferred_element_type=jnp.float32
    )
    grad_scores = (
        weights * (grad_att - jnp.sum(weights * grad_att, axis=-1, keepdims=True))
    ).astype(jnp.bfloat16)
    grad_query = (
        jnp.einsum("hqk,khd->qhd", grad_scores, key_heads, preferred_element_type=jnp.float32)
        * score_scale
    )
    key_part = jnp.einsum(
        "hqk,qhd->khd", grad_scores, query_heads, preferred_element_type=jnp.float32
    ).reshape(key_total, EMB)
    value_part = jnp.einsum(
        "hqk,qhd->khd", probs_in, grad_heads, preferred_element_type=jnp.float32
    ).reshape(key_total, EMB)
    grad_key, grad_value = (
        lax.psum_scatter(key_part, "agg", scatter_dimension=0, tiled=True),
        lax.psum_scatter(value_part, "agg", scatter_dimension=0, tiled=True),
    )
    grad_qkv = jnp.concatenate(
        [grad_query.reshape(local_slots, EMB), grad_key, grad_value], axis=1
    ).astype(jnp.bfloat16)
    grad_normed = lax.dot_general(
        grad_qkv, full_qkv, (((1,), (1,)), ((), ())), preferred_element_type=jnp.float32
    )
    grad_rows = (
        live_values[:, None] * grad_pooled[None, :]
        + norm_backward(grad_normed, normed, inv_std, norm_gain)
    ).astype(jnp.bfloat16)
    back_rows = lax.all_to_all(
        lax.all_to_all(
            grad_rows.reshape(local_slots // send_slots, send_slots, EMB),
            "agg",
            split_axis=2,
            concat_axis=0,
            tiled=True,
        ),
        "enc",
        split_axis=0,
        concat_axis=0,
        tiled=True,
    )
    back_flat = back_rows.reshape(slot_total, local_cols)
    tile_grads = lax.dot_general(
        placing, back_flat, (((0,), (0,)), ((), ())), preferred_element_type=jnp.float32
    )
    grad_preact = jnp.where(preact > 0, tile_grads[:, None, :] / POS, 0.0).astype(jnp.bfloat16)
    weight_part = lax.dot_general(
        flattened,
        grad_preact.reshape(tile_count * POS, local_cols),
        (((0,), (0,)), ((), ())),
        preferred_element_type=jnp.float32,
    )
    bias_part = jnp.sum(grad_preact.astype(jnp.float32), axis=(0, 1))
    enc_grad, bias_grad = lax.psum((weight_part, bias_part), "enc")
    return (logits[None, :], enc_grad, bias_grad)


def solution(mesh):
    return jax.shard_map(
        on_device,
        mesh=mesh,
        in_specs=(
            P("enc", None, None),
            P("enc", None),
            P("enc"),
            P(),
            P(),
            P(None, "agg"),
            P("agg"),
            P(),
            P("enc", None),
            P("enc", None),
            P(),
        ),
        out_specs=(P("enc", None), P(None, "agg"), P("agg")),
        check_vma=False,
    )
```

profile of v0, /device:TPU:1, one launch (start us, length us, event | category | flops | bytes accessed | tf_op | source)
XLA Modules:
  0.0 814.0 jit_solution(135959976760046860)
XLA Ops:
  11.5 21.0 %all-to-all-start.2 = ((bf16[128,2,1]{1,2,0:T(2,128)(2,1)}), bf16[128,2,1]{1,2,0:T(2,128)(2,1)}, u32[]{:S(2)}, u32[]{:S(2)}) async-start(bf16[128,2,1]{1,2,0:T(2,128)(2,1)} %reshape.536), calls=%async_computation.2 | async-start | bytes 131072 | tf_op jit(solution)/shard_map/all_to_all | solution.py:124
  33.9 5.2 maximum_reduce_fusion
  39.4 7.6 all-to-all-done.2
  47.0 4.0 all-to-all-start.3
  55.5 10.4 %all-to-all-start = ((bf16[128,2,192]{2,1,0:T(2,128)(2,1)}), bf16[128,2,192]{2,1,0:T(2,128)(2,1)}, u32[]{:S(2)}, u32[]{:S(2)}) async-start(bf16[128,2,192]{2,1,0:T(2,128)(2,1)} %reshape.504), calls=%async_computation | async-start | bytes 262144 | tf_op jit(solution)/shard_map/all_to_all | solution.py:117
  66.6 7.7 all-reduce
  77.2 5.5 all-to-all-done
  86.8 4.1 all-to-all-done.1
  92.3 63.9 %all-gather.7.cloned.1.call-done = bf16[128,6,768]{2,1,0:T(8,128)(2,1)} async-done(((bf16[1,6,768]{2,1,0:T(8,128)(2,1)}), bf16[128,6,768]{2,1,0:T(8,128)(2,1)}) %all-gather.7.cloned.1.call-update) | async-done | bytes 1179664 | tf_op jit(solution)/shard_map/all_gather | solution.py:140
  158.5 139.8 %all-gather.5.cloned.1.call-done = bf16[128,6,2304]{2,1,0:T(8,128)(2,1)} async-done(((bf16[1,6,2304]{2,1,0:T(8,128)(2,1)}), bf16[128,6,2304]{2,1,0:T(8,128)(2,1)}) %all-gather.5.cloned.1.call-update) | async-done | bytes 3538960 | tf_op jit(solution)/shard_map/all_gather | solution.py:139
  298.3 6.6 reshape.521
  307.9 10.6 %all_gather.18 = bf16[256,768]{1,0:T(8,128)(2,1)S(1)} all-gather(bf16[64,768]{1,0:T(8,128)(2,1)S(1)} %get-tuple-element.7), channel_id=1, replica_groups=mesh['enc'=128,'agg'=4] {'agg'}, dimensions={0}, use_global_device_ids=true | all-gather | bytes 491520 | tf_op jit(solution)/shard_map/all_gather | solution.py:148
  318.7 9.8 %all_gather.16 = bf16[256,768]{1,0:T(8,128)(2,1)S(1)} all-gather(bf16[64,768]{1,0:T(8,128)(2,1)S(1)} %get-tuple-element.8), channel_id=1, replica_groups=mesh['enc'=128,'agg'=4] {'agg'}, dimensions={0}, use_global_device_ids=true | all-gather | bytes 491520 | tf_op jit(solution)/shard_map/all_gather | solution.py:149
  329.5 3.4 fusion.78
  335.3 7.9 psum.21
  357.0 25.9 %reduce-scatter.9.cloned.1.call-done = f32[64,768]{1,0:T(8,128)} async-done(((f32[256,768]{1,0:T(8,128)}), f32[64,768]{1,0:T(8,128)}) %reduce-scatter.9.cloned.1.call-update) | async-done | bytes 196624
  384.0 31.5 %reduce-scatter.7.cloned.1.call-done = f32[64,768]{1,0:T(8,128)} async-done(((f32[256,768]{1,0:T(8,128)}), f32[64,768]{1,0:T(8,128)}) %reduce-scatter.7.cloned.1.call-update) | async-done | bytes 196624
  416.7 3.3 fusion.74
  421.1 7.0 all_to_all.60
  429.6 19.0 %all-to-all-start.5 = ((bf16[128,2,192]{2,1,0:T(2,128)(2,1)}), bf16[128,2,192]{2,1,0:T(2,128)(2,1)S(1)}, u32[]{:S(2)}, u32[]{:S(2)}) async-start(bf16[128,2,192]{2,1,0:T(2,128)(2,1)} %copy.90), calls=%async_computation.5 | async-start | bytes 262144 | tf_op jit(solution)/shard_map/all_to_all | solution.py:216
  449.0 17.0 %all-to-all-done.5 = bf16[128,2,192]{2,1,0:T(2,128)(2,1)S(1)} async-done(((bf16[128,2,192]{2,1,0:T(2,128)(2,1)}), bf16[128,2,192]{2,1,0:T(2,128)(2,1)S(1)}, u32[]{:S(2)}, u32[]{:S(2)}) %all-to-all-start.5) | async-done | bytes 98336 | tf_op jit(solution)/shard_map/all_to_all | solution.py:216
  466.4 5.7 convolution_bitcast_fusion
  472.3 248.6 %psum.23 = f32[192]{0:T(256)} all-reduce(f32[192]{0:T(256)S(1)} %convert_reduce_fusion), channel_id=1, replica_groups=mesh['enc'=128,'agg'=4] {'enc'}, use_global_device_ids=true, to_apply=%region_20.21 | all-reduce | flops 192 | bytes 1536 | tf_op jit(solution)/shard_map/psum | solution.py:241
  720.9 83.9 %all-reduce.3.cloned.1.call-done = f32[2048,192]{0,1:T(8,128)} async-done(((f32[2048,192]{0,1:T(8,128)}), f32[2048,192]{0,1:T(8,128)}) %all-reduce.3.cloned.1.call-update) | async-done | bytes 1572880 | tf_op jit(solution)/shard_map/psum | solution.py:241
  (124 shorter events, 49.3 us)
Async XLA Ops:
  7.2 26.7 %copy-start = (bf16[2048,192]{0,1:T(8,128)(2,1)S(1)}, bf16[2048,192]{0,1:T(8,128)(2,1)}, u32[]{:S(2)}) copy-start(bf16[2048,192]{0,1:T(8,128)(2,1)} %param.16) | copy-start | bytes 2359300
  7.2 149.0 %all-gather.7.cloned.1.call-start = ((), (), s32[]{:S(2)}) async-start(), calls=%async_computation.10 | async-start | bytes 1585152 | tf_op jit(solution)/shard_map/all_gather | solution.py:140
  7.9 290.4 %all-gather.5.cloned.1.call-start = ((), (), s32[]{:S(2)}) async-start(), calls=%async_computation.9 | async-start | bytes 4755456 | tf_op jit(solution)/shard_map/all_gather | solution.py:139
  10.5 28.7 %copy-start.8 = (s32[144]{0:T(256)}, s32[144]{0:T(256)S(1)}, u32[]{:S(2)}) copy-start(s32[144]{0:T(256)S(1)} %multiply_add_fusion) | copy-start | bytes 1732
  11.5 35.5 %all-to-all-start.2 = ((bf16[128,2,1]{1,2,0:T(2,128)(2,1)}), bf16[128,2,1]{1,2,0:T(2,128)(2,1)}, u32[]{:S(2)}, u32[]{:S(2)}) async-start(bf16[128,2,1]{1,2,0:T(2,128)(2,1)} %reshape.536), calls=%async_computation.2 | async-start | bytes 131072 | tf_op jit(solution)/shard_map/all_to_all | solution.py:124
  47.0 8.5 %all-to-all-start.3 = ((bf16[128,2,1]{1,2,0:T(2,128)(2,1)}), bf16[128,2,1]{1,2,0:T(2,128)(2,1)S(1)}, u32[]{:S(2)}, u32[]{:S(2)}) async-start(bf16[128,2,1]{1,2,0:T(2,128)(2,1)} %all-to-all-done.2), calls=%async_computation.3 | async-start | bytes 131072 | tf_op jit(solution)/shard_map/all_to_all | solution.py:123
  55.5 27.3 %all-to-all-start = ((bf16[128,2,192]{2,1,0:T(2,128)(2,1)}), bf16[128,2,192]{2,1,0:T(2,128)(2,1)}, u32[]{:S(2)}, u32[]{:S(2)}) async-start(bf16[128,2,192]{2,1,0:T(2,128)(2,1)} %reshape.504), calls=%async_computation | async-start | bytes 262144 | tf_op jit(solution)/shard_map/all_to_all | solution.py:117
  82.8 8.1 all-to-all-start.1
  86.1 296.8 %reduce-scatter.9.cloned.1.call-start = ((), (), s32[]{:S(2)}) async-start(), calls=%async_computation.12 | async-start | bytes 983040
  91.6 213.3 %copy-start.4 = (f32[64]{0:T(128)}, f32[64]{0:T(128)S(1)}, u32[]{:S(2)}) copy-start(f32[64]{0:T(128)S(1)} %div.95) | copy-start | bytes 772
  92.2 212.7 %copy-start.6 = (f32[64]{0:T(128)}, f32[64]{0:T(128)S(1)}, u32[]{:S(2)}) copy-start(f32[64]{0:T(128)S(1)} %rsqrt.12) | copy-start | bytes 772
  158.5 146.4 %copy-start.2 = (f32[768]{0:T(1024)S(1)}, f32[768]{0:T(1024)}, u32[]{:S(2)}) copy-start(f32[768]{0:T(1024)} %param.18) | copy-start | bytes 9220
  345.5 5.0 copy-start.13
  351.0 2.3 copy-start.10
  351.0 2.3 copy-start.14
  353.3 62.2 %reduce-scatter.7.cloned.1.call-start = ((), (), s32[]{:S(2)}) async-start(), calls=%async_computation.11 | async-start | bytes 983040
  355.5 61.1 %copy-start.3 = (f32[768]{0:T(1024)S(1)}, f32[768]{0:T(1024)}, u32[]{:S(2)}) copy-start(f32[768]{0:T(1024)} %param.18) | copy-start | bytes 9220
  355.6 61.1 %copy-start.5 = (f32[64]{0:T(128)S(1)}, f32[64]{0:T(128)}, u32[]{:S(2)}) copy-start(f32[64]{0:T(128)} %copy-done.4) | copy-start | bytes 772
  355.6 61.1 %copy-start.7 = (f32[64]{0:T(128)S(1)}, f32[64]{0:T(128)}, u32[]{:S(2)}) copy-start(f32[64]{0:T(128)} %copy-done.6) | copy-start | bytes 772
  416.6 3.4 copy-start.12
  420.0 28.9 %copy-start.1 = (f32[144,4,192]{2,0,1:T(8,128)S(1)}, f32[144,4,192]{2,0,1:T(8,128)}, u32[]{:S(2)}) copy-start(f32[144,4,192]{2,0,1:T(8,128)} %get-tuple-element.20) | copy-start | bytes 1327108
  420.0 46.2 %copy-start.9 = (s32[144]{0:T(256)S(1)}, s32[144]{0:T(256)}, u32[]{:S(2)}) copy-start(s32[144]{0:T(256)} %copy-done.8) | copy-start | bytes 1732
  429.6 36.4 %all-to-all-start.5 = ((bf16[128,2,192]{2,1,0:T(2,128)(2,1)}), bf16[128,2,192]{2,1,0:T(2,128)(2,1)S(1)}, u32[]{:S(2)}, u32[]{:S(2)}) async-start(bf16[128,2,192]{2,1,0:T(2,128)(2,1)} %copy.90), calls=%async_computation.5 | async-start | bytes 262144 | tf_op jit(solution)/shard_map/all_to_all | solution.py:216
  448.7 356.2 %all-reduce.3.cloned.1.call-start = ((), (), s32[]{:S(2)}) async-start(), calls=%async_computation.8 | async-start | bytes 3145728 | tf_op jit(solution)/shard_map/psum | solution.py:241
  (1 other events, 2.0 us)
Sparse Core Ops, SparseCore 0:
  11.1 145.0 all-gather.6
  159.2 139.0 all-gather.4
  353.4 29.4 reduce-scatter.8
  385.6 29.8 reduce-scatter.6
  472.3 332.4 all-reduce.2
where the time goes:
time: 817 us; the launch traced here: 814 us
  waiting for transfers between devices  383 us (47%)
  blocking collectives  292 us (36%)
  starting transfers between devices  58.3 us (7%)
  matrix products  31.1 us (4%)
  local copies, waits for them, and re-layouts  24.1 us (3%)
  between operations  15 us (2%)
  other arithmetic  11.4 us (1%)
    psum x1, blocking collectives, on_device(): enc_grad, bias_grad = lax.psum((weight_part, bias_part), 'enc')  249 us
    all_gather x1, waiting for transfers between devices, on_device(): lax.all_gather(qkv_weight, 'enc', axis=0, tiled=True)  140 us
    psum x1, waiting for transfers between devices, on_device(): enc_grad, bias_grad = lax.psum((weight_part, bias_part), 'enc')  83.9 us
    all_gather x1, waiting for transfers between devices, on_device(): lax.all_gather(out_weight, 'enc', axis=0, tiled=True)  63.9 us
    unnamed x7, waiting for transfers between devices  58.9 us
    all_to_all x1, starting transfers between devices, on_device(): lax.all_to_all(send_tags, 'enc', split_axis=0, concat_axis=0, tiled=True)  21 us
    all_to_all x1, starting transfers between devices, on_device(): lax.all_to_all(lax.all_to_all(grad_rows.reshape(local_slots // send_slots...  19 us
    unnamed x42, local copies, waits for them, and re-layouts  18.3 us
  transfers between devices with their start and end apart: 10, of which 10 were waited for; matrix products, arithmetic and copies ran while one was open for 3% of the time, Pallas kernels for 0%

commit v1 on v0

v1 whole, which is shorter than its diff:
```python
import jax
import jax.numpy as jnp
from jax import lax
from jax.experimental import pallas as pl
from jax.experimental.pallas import tpu as pltpu
from jax.sharding import Mesh, PartitionSpec as P

POS = 4
HEADS = 12
CLASSES = 32
HD = 64
SLOTS = 2
BLOCK = 256
ENC = ("y", "z", "c")
NEAR = ("y", "c")
eps = 1e-05

bf16 = jnp.bfloat16
f32 = jnp.float32
EXACT = lax.Precision.HIGHEST


def across(lhs, rhs, dims, precision=None):
    return lax.dot_general(
        lhs, rhs, ((dims[:1], dims[1:]), ((), ())), precision=precision, preferred_element_type=f32
    )


def normed_parts(rows_ref, cols):
    parts = [rows_ref[part, :, :cols].astype(f32) for part in range(rows_ref.shape[0])]
    width = cols * len(parts)
    mean = sum(jnp.sum(part, axis=1, keepdims=True) for part in parts) / width
    centred = [part - mean for part in parts]
    variance = sum(jnp.sum(part * part, axis=1, keepdims=True) for part in centred) / width
    inv_std = lax.rsqrt(variance + eps)
    return parts, [part * inv_std for part in centred], inv_std


def forward_kernel(place_ref, rows_ref, weight_ref, gain_ref, cls_ref, logits_ref, att_ref, qkv_ref):
    groups, slots, _ = rows_ref.shape
    cols = gain_ref.shape[2]
    parts, normed, _ = normed_parts(rows_ref, cols)
    qkv = jnp.zeros((slots, 3 * cols), f32)
    for part in range(groups):
        normed_in = (normed[part] * gain_ref[part]).astype(bf16)
        block = weight_ref[part * cols : (part + 1) * cols, : 3 * cols]
        qkv = qkv + across(normed_in, block, (1, 0))
    column = lax.broadcasted_iota(jnp.int32, (slots, 3 * cols), 1)
    qkv = jnp.where(column < cols, qkv * HD ** (-0.5), qkv).astype(bf16)
    qkv_ref[...] = qkv
    tags = rows_ref[0, :, cols : cols + 1].astype(f32)
    count = jnp.sum(tags, axis=0, keepdims=True) * 0.0 + jnp.sum(
        (tags > 0).astype(f32), axis=0, keepdims=True
    )
    down = lax.broadcasted_iota(jnp.int32, (slots, slots), 0)
    along = lax.broadcasted_iota(jnp.int32, (slots, slots), 1)
    tag_row = jnp.sum(jnp.where(down == along, tags, 0.0), axis=0, keepdims=True)
    query_pos = tags.astype(jnp.int32) - 1
    key_pos = tag_row.astype(jnp.int32) - 1
    wc_pair = weight_ref[pl.ds(pl.multiple_of(place_ref[0] * cols, 16), cols), 3 * cols :].astype(f32)
    wc = wc_pair[:, :CLASSES] + wc_pair[:, CLASSES : 2 * CLASSES]
    total = jnp.zeros((1, CLASSES), f32)
    for head in range(cols // HD):
        group = head % 3
        low = (1 << group) - 1
        query_key = ((query_pos >> (6 + group)) << group) + (query_pos & low)
        key_key = ((key_pos >> (6 + group)) << group) + (key_pos & low)
        query_key = jnp.where(query_pos < 0, -1, query_key)
        key_key = jnp.where(key_pos < 0, -2, key_key)
        visible = query_key == key_key
        first = head * HD
        scores = across(
            qkv[:, first : first + HD], qkv[:, cols + first : cols + first + HD], (1, 1)
        )
        masked = jnp.where(visible, scores, -1e30)
        row_max = jnp.max(masked, axis=1, keepdims=True)
        weights = jnp.where(visible, jnp.exp(masked - row_max), 0.0)
        row_total = jnp.sum(weights, axis=1, keepdims=True)
        att = weights / jnp.where(row_total > 0, row_total, 1.0)
        att_ref[head] = att
        att_total = jnp.sum(att.astype(bf16).astype(f32), axis=0, keepdims=True)
        values = qkv[:, 2 * cols + first : 2 * cols + first + HD].astype(f32)
        mixed_total = across(att_total, values, (1, 0), EXACT)
        total = total + across(mixed_total, wc[first : first + HD], (1, 0), EXACT)
    for part in range(groups):
        row_sum = jnp.sum(parts[part], axis=0, keepdims=True) * (1.0 / groups)
        total = total + across(row_sum, cls_ref[part], (1, 1), EXACT)
    logits_ref[...] = total / count


def backward_kernel(
    place_ref,
    logits_ref,
    owner_ref,
    label_ref,
    rows_ref,
    weight_ref,
    gain_ref,
    cls_ref,
    att_ref,
    qkv_ref,
    grad_ref,
):
    groups, slots, _ = rows_ref.shape
    cols = gain_ref.shape[2]
    _, normed, inv_std = normed_parts(rows_ref, cols)
    tags = rows_ref[0, :, cols : cols + 1].astype(f32)
    live = (tags > 0).astype(f32)
    count = jnp.sum(live, axis=0, keepdims=True)
    logits = logits_ref[...]
    scaled = jnp.exp(logits - jnp.max(logits, axis=1, keepdims=True))
    class_probs = scaled / jnp.sum(scaled, axis=1, keepdims=True)
    mine = owner_ref[...] == place_ref[1]
    my_label = jnp.sum(jnp.where(mine, label_ref[...], 0).astype(f32), axis=1, keepdims=True)
    class_ids = lax.broadcasted_iota(jnp.int32, (1, CLASSES), 1).astype(f32)
    grad_logits = (class_probs - (class_ids == my_label).astype(f32)) / count
    wc_pair = weight_ref[pl.ds(pl.multiple_of(place_ref[0] * cols, 16), cols), 3 * cols :].astype(f32)
    wc = wc_pair[:, :CLASSES] + wc_pair[:, CLASSES : 2 * CLASSES]
    grad_mixed = across(grad_logits, wc, (1, 1), EXACT).astype(bf16)
    qkv = qkv_ref[...]
    grad_q, grad_k, grad_v = [], [], []
    for head in range(cols // HD):
        first = head * HD
        att = att_ref[head]
        queries = qkv[:, first : first + HD]
        keys = qkv[:, cols + first : cols + first + HD]
        values = qkv[:, 2 * cols + first : 2 * cols + first + HD]
        head_grad = grad_mixed[:, first : first + HD]
        grad_att = across(head_grad, values, (1, 1))
        expected = jnp.sum(att * grad_att, axis=1, keepdims=True)
        grad_scores = (att * (grad_att - expected)).astype(bf16)
        grad_q.append(across(grad_scores, keys, (1, 0)) * HD ** (-0.5))
        grad_k.append(across(grad_scores, queries, (0, 0)))
        spread = jnp.broadcast_to(head_grad, (slots, HD))
        grad_v.append(across(att.astype(bf16), spread, (0, 0)))
    grad_qkv = jnp.concatenate(grad_q + grad_k + grad_v, axis=1).astype(bf16)
    scaled_parts = []
    for part in range(groups):
        block = weight_ref[part * cols : (part + 1) * cols, : 3 * cols]
        scaled_parts.append(across(grad_qkv, block, (1, 1)) * gain_ref[part])
    width = cols * groups
    mean = sum(jnp.sum(e, axis=1, keepdims=True) for e in scaled_parts) / width
    slope = (
        sum(jnp.sum(e * n, axis=1, keepdims=True) for e, n in zip(scaled_parts, normed)) / width
    )
    for part in range(groups):
        pooled = across(grad_logits, cls_ref[part], (1, 0), EXACT) * (1.0 / groups)
        grad = inv_std * (scaled_parts[part] - mean - normed[part] * slope)
        grad_ref[part] = (live * pooled + grad).astype(bf16)


def on_device(
    features,
    tile_slide,
    tile_pos,
    slide_owner,
    slide_label,
    enc_weight,
    enc_bias,
    norm_gain,
    qkv_weight,
    out_weight,
    cls_weight,
):
    enc_count = lax.axis_size(ENC)
    far_count = lax.axis_size("z")
    near_count = lax.axis_size(NEAR)
    groups = lax.axis_size("x")
    tile_count, _, channels = features.shape
    cols = enc_weight.shape[1]
    emb = cols * groups
    slide_count = slide_owner.shape[0]
    slot_total = enc_count * SLOTS
    group_at = lax.axis_index("x")
    owner_at = lax.axis_index(ENC)

    with jax.named_scope("weights"):
        wc_rows = jnp.dot(out_weight.astype(f32), cls_weight, precision=EXACT)
        wc_high = wc_rows.astype(bf16)
        wc_low = (wc_rows - wc_high.astype(f32)).astype(bf16)
        picked = [
            lax.dynamic_slice_in_dim(qkv_weight, part * emb + group_at * cols, cols, 1)
            for part in range(3)
        ]
        weight_rows = jnp.concatenate(picked + [wc_high, wc_low], axis=1)
        far_rows = lax.all_gather(weight_rows, "z", axis=0, tiled=False)
        near_rows = lax.all_gather(far_rows, NEAR, axis=0, tiled=False)
        held = near_rows.shape[2:]
        weights = (
            near_rows.reshape((lax.axis_size("y"), lax.axis_size("c"), far_count) + held)
            .transpose(0, 2, 1, 3, 4)
            .reshape(emb, held[1])
        )

    with jax.named_scope("encode"):
        flattened = features.reshape(tile_count * POS, channels)
        preact = (
            jnp.dot(flattened, enc_weight, preferred_element_type=f32).reshape(
                tile_count, POS, cols
            )
            + enc_bias
        )
        tile_rows = jnp.mean(jnp.maximum(preact, 0.0), axis=1).astype(bf16)

    with jax.named_scope("dispatch"):
        slide_ids = tile_slide[:, 0]
        slide_range = jnp.arange(slide_count, dtype=jnp.int32)
        owners = jnp.sum(
            jnp.where(slide_ids[:, None] == slide_range[None, :], slide_owner[None, :], 0), axis=1
        )
        tile_range = jnp.arange(tile_count, dtype=jnp.int32)
        earlier = tile_range[None, :] < tile_range[:, None]
        slot_rank = jnp.sum(
            ((slide_ids[:, None] == slide_ids[None, :]) & earlier).astype(jnp.int32), axis=1
        )
        target = owners * SLOTS + slot_rank
        placing = (jnp.arange(slot_total, dtype=jnp.int32)[:, None] == target[None, :]).astype(bf16)
        tagged = jnp.concatenate(
            [
                tile_rows,
                (tile_pos + 1).astype(bf16)[:, None],
                jnp.zeros((tile_count, BLOCK - cols - 1), bf16),
            ],
            axis=1,
        )
        send_rows = (
            jnp.dot(placing, tagged, preferred_element_type=f32)
            .astype(bf16)
            .reshape(enc_count, SLOTS, BLOCK)
        )
        slot_rows = lax.all_to_all(send_rows, ENC, split_axis=0, concat_axis=0, tiled=True)
        rows = lax.all_gather(slot_rows.reshape(slot_total, BLOCK), "x", axis=0, tiled=False)

    with jax.named_scope("attend"):
        place = jnp.stack([group_at, owner_at]).astype(jnp.int32)
        gain = norm_gain.reshape(groups, 1, cols)
        cls_parts = cls_weight.T.reshape(CLASSES, groups, cols).transpose(1, 0, 2)
        in_smem = pl.BlockSpec(memory_space=pltpu.SMEM)
        in_vmem = pl.BlockSpec(memory_space=pltpu.VMEM)
        part_logits, att, qkv = pl.pallas_call(
            forward_kernel,
            out_shape=(
                jax.ShapeDtypeStruct((1, CLASSES), f32),
                jax.ShapeDtypeStruct((cols // HD, slot_total, slot_total), f32),
                jax.ShapeDtypeStruct((slot_total, 3 * cols), bf16),
            ),
            in_specs=[in_smem] + [in_vmem] * 4,
            out_specs=(in_vmem,) * 3,
            compiler_params=pltpu.CompilerParams(vmem_limit_bytes=32 << 20),
            name="forward",
        )(place, rows, weights, gain, cls_parts)
        logits = lax.psum(part_logits, "x")
        grad_parts = pl.pallas_call(
            backward_kernel,
            out_shape=jax.ShapeDtypeStruct((groups, slot_total, cols), bf16),
            in_specs=[in_smem] + [in_vmem] * 9,
            out_specs=in_vmem,
            compiler_params=pltpu.CompilerParams(vmem_limit_bytes=32 << 20),
            name="backward",
        )(
            place,
            logits,
            slide_owner[None, :],
            slide_label[None, :],
            rows,
            weights,
            gain,
            cls_parts,
            att,
            qkv,
        )

    with jax.named_scope("give_back"):
        from_groups = lax.all_to_all(grad_parts, "x", split_axis=0, concat_axis=0, tiled=True)
        grad_rows = jnp.sum(from_groups.astype(f32), axis=0).astype(bf16)
        back_rows = lax.all_to_all(
            grad_rows.reshape(enc_count, SLOTS, cols), ENC, split_axis=0, concat_axis=0, tiled=True
        ).reshape(slot_total, cols)

    with jax.named_scope("encoder_grad"):
        tile_grads = across(placing, back_rows, (0, 0))
        grad_preact = jnp.where(preact > 0, tile_grads[:, None, :] / POS, 0.0).astype(bf16)
        grad_preact = grad_preact.reshape(tile_count * POS, cols)
        grad_part = across(grad_preact, flattened, (0, 0)).astype(bf16)
        bias_part = jnp.sum(grad_preact.astype(f32), axis=0).astype(bf16)

    with jax.named_scope("reduce"):
        near_rows = cols // near_count
        lanes = channels // far_count
        bias_lanes = jnp.broadcast_to(
            bias_part.reshape(near_count, near_rows, 1), (near_count, near_rows, lanes)
        )
        near_send = jnp.concatenate(
            [grad_part.reshape(near_count, near_rows, channels), bias_lanes], axis=2
        )
        near_sum = jnp.sum(
            lax.all_to_all(near_send, NEAR, split_axis=0, concat_axis=0, tiled=True).astype(f32),
            axis=0,
        )
        far_send = (
            near_sum[:, :channels].reshape(near_rows, far_count, lanes).transpose(1, 0, 2)
        ).astype(bf16)
        bias_row = jnp.pad(near_sum[:, channels], (0, lanes - near_rows)).astype(bf16)
        far_send = jnp.concatenate(
            [far_send, jnp.broadcast_to(bias_row[None, None, :], (far_count, 8, lanes))], axis=1
        )
        far_sum = jnp.sum(
            lax.all_to_all(far_send, "z", split_axis=0, concat_axis=0, tiled=True).astype(f32),
            axis=0,
        ).astype(bf16)
        far_all = lax.all_gather(far_sum, "z", axis=0, tiled=False)
        all_parts = lax.all_gather(far_all, NEAR, axis=0, tiled=False).astype(f32)
        enc_grad = (
            all_parts[:, :, :near_rows].transpose(0, 2, 1, 3).reshape(cols, channels).T
        )
        bias_grad = all_parts[:, 0, near_rows, :near_rows].reshape(cols)
    return (logits, enc_grad, bias_grad)


def solution(mesh):
    enc_count, groups = mesh.devices.shape
    split = Mesh(mesh.devices.reshape(4, enc_count // 8, 2, groups), ("y", "z", "c", "x"))
    return jax.shard_map(
        on_device,
        mesh=split,
        in_specs=(
            P(ENC, None, None),
            P(ENC, None),
            P(ENC),
            P(),
            P(),
            P(None, "x"),
            P("x"),
            P(),
            P(ENC, None),
            P(ENC, None),
            P(),
        ),
        out_specs=(P(ENC, None), P(None, "x"), P("x")),
        check_vma=False,
    )
```

time: 817 us -> 264 us (0.32)
  waiting for transfers between devices: 383 us -> 48.1 us
  blocking collectives: 292 us -> 130 us
  matrix products: 31.1 us -> 10.3 us
  starting transfers between devices: 58.3 us -> 40.4 us
  local copies, waits for them, and re-layouts: 24.1 us -> 9.49 us
    psum x2 -> x1, blocking collectives: 257 us -> 8.02 us  [on_device(): logits = lax.psum(part_logits, 'x')]
    all_gather x2 -> x1, waiting for transfers between devices: 204 us -> 30.8 us  [on_device(): all_parts = lax.all_gather(far_all, NEAR, axis=0, tiled=False).astype(f32)]
    psum x1 -> x0, waiting for transfers between devices: 83.9 us -> none  [on_device(): enc_grad, bias_grad = lax.psum((weight_part, bias_part), 'enc')]
    all_gather x2 -> x4, blocking collectives: 20.4 us -> 81.1 us  [the longest x1 24.7 us: on_device(): far_rows = lax.all_gather(weight_rows, 'z', axis=0, tiled=False)]
    unnamed x7 -> x1, waiting for transfers between devices: 58.9 us -> 0.02 us
    all_to_all x1 -> x3, blocking collectives: 7.03 us -> 40.8 us  [the longest x1 17.6 us: on_device(): lax.all_to_all(near_send, NEAR, split_axis=0, concat_axis=0, tiled=True)]
    all_to_all x5 -> x2, waiting for transfers between devices: 36 us -> 17.2 us  [the longest x1 17.2 us: on_device(): lax.all_to_all(grad_rows.reshape(enc_count, SLOTS, cols), ENC, split_axis...]
    all_to_all x5 -> x2, starting transfers between devices: 57.8 us -> 40.4 us  [the longest x1 20.6 us: on_device(): lax.all_to_all(send_rows, ENC, split_axis=0, concat_axis=0, tiled=True)]
  transfers between devices with their start and end apart: 10 -> 3, of which waited for: 10 -> 2; matrix products, arithmetic and copies ran while one was open for 3% -> 1% of each run, Pallas kernels for 0% -> 0%
where the time goes in v1:
time: 264 us
  blocking collectives  130 us (49%)
  waiting for transfers between devices  48.1 us (18%)
  starting transfers between devices  40.4 us (15%)
  between operations  14.4 us (5%)
  matrix products  10.3 us (4%)
  local copies, waits for them, and re-layouts  9.49 us (4%)
  Pallas kernels  6.27 us (2%)
  other arithmetic  4.69 us (2%)
    all_gather x1, waiting for transfers between devices, on_device(): all_parts = lax.all_gather(far_all, NEAR, axis=0, tiled=False).astype(f32)  30.8 us
    all_gather x1, blocking collectives, on_device(): far_rows = lax.all_gather(weight_rows, 'z', axis=0, tiled=False)  24.7 us
    all_gather x1, blocking collectives, on_device(): far_all = lax.all_gather(far_sum, 'z', axis=0, tiled=False)  24.7 us
    all_gather x1, blocking collectives, on_device(): near_rows = lax.all_gather(far_rows, NEAR, axis=0, tiled=False)  20.6 us
    all_to_all x1, starting transfers between devices, on_device(): lax.all_to_all(send_rows, ENC, split_axis=0, concat_axis=0, tiled=True)  20.6 us
    all_to_all x1, starting transfers between devices, on_device(): lax.all_to_all(grad_rows.reshape(enc_count, SLOTS, cols), ENC, split_axis...  19.8 us
    all_to_all x1, blocking collectives, on_device(): lax.all_to_all(near_send, NEAR, split_axis=0, concat_axis=0, tiled=True)  17.6 us
    all_to_all x1, waiting for transfers between devices, on_device(): lax.all_to_all(grad_rows.reshape(enc_count, SLOTS, cols), ENC, split_axis...  17.2 us
  transfers between devices with their start and end apart: 3, of which 2 were waited for; matrix products, arithmetic and copies ran while one was open for 1% of the time, Pallas kernels for 0%

profile of v1, /device:TPU:1, one launch (start us, length us, event | category | flops | bytes accessed | tf_op | source)
XLA Modules:
  0.0 263.6 jit_solution(4722518313536185540)
XLA Ops:
  7.2 0.8 add_convert_fusion
  7.9 0.9 convert_reduce_fusion
  8.9 0.9 select_reduce_fusion
  9.9 5.2 %maximum_reduce_fusion = (f32[144,192]{1,0:T(8,128)S(1)}, f32[144,4,192]{2,0,1:T(8,128)}) fusion(f32[192]{0:T(256)} %param.17, bf16[2048,192]{0,1:T(8,128)(2,1)S(1)} %copy-done, bf16[144,4,2048]{2,1,0:T(4,128)(2,1)} %param.11), kind=kOutput, calls=%fused_computation.16 | convolution fusion | flops 453288960 | bytes 3699456 | tf_op jit(solution)/shard_map/encode/dot_general | solution.py:198
  16.2 20.6 %all-to-all-start = ((bf16[128,2,256]{2,1,0:T(2,128)(2,1)}), bf16[128,2,256]{2,1,0:T(2,128)(2,1)S(1)}, u32[]{:S(2)}, u32[]{:S(2)}) async-start(bf16[128,2,256]{2,1,0:T(2,128)(2,1)} %reshape.57), calls=%async_computation | async-start | bytes 262144 | tf_op jit(solution)/shard_map/dispatch/all_to_all | solution.py:231
  37.2 0.8 constant_dynamic-slice_fusion
  38.1 24.7 %all-gather.4 = bf16[16,6,640]{2,1,0:T(8,128)(2,1)S(1)} all-gather(bf16[1,6,640]{2,1,0:T(8,128)(2,1)S(1)} %bitcast.59), channel_id=2, replica_groups=mesh['y'=4,'z'=16,'c'=2,'x'=4] {'z'}, dimensions={0}, use_global_device_ids=true | all-gather | bytes 130560 | tf_op jit(solution)/shard_map/weights/all_gather | solution.py:186
  62.9 20.6 %all-gather.1 = bf16[128,6,640]{2,0,1:T(8,128)(2,1)S(1)} all-gather(bf16[16,6,640]{2,0,1:T(8,128)(2,1)S(1)} %copy.64), channel_id=3, replica_groups=mesh['y'=4,'z'=16,'c'=2,'x'=4] {'y','c'}, dimensions={0}, use_global_device_ids=true | all-gather | bytes 1105920 | tf_op jit(solution)/shard_map/weights/all_gather | solution.py:187
  84.6 11.0 %all_gather.27.rows_ref = bf16[4,256,256]{2,1,0:T(8,128)(2,1)S(1)} all-gather(bf16[1,256,256]{2,1,0:T(8,128)(2,1)S(1)} %reshape.58), channel_id=1, replica_groups=mesh['y'=4,'z'=16,'c'=2,'x'=4] {'x'}, dimensions={0}, use_global_device_ids=true | all-gather | bytes 655360 | tf_op jit(solution)/shard_map/dispatch/all_gather | solution.py:232
  95.6 3.0 %forward.1 = (f32[1,32]{1,0:T(1,128)S(1)}, f32[3,256,256]{2,1,0:T(8,128)S(1)}, bf16[256,576]{1,0:T(8,128)(2,1)S(1)}) custom-call(s32[2]{0:T(128)S(1)} %pad_add_fusion.place_ref, bf16[4,256,256]{2,1,0:T(8,128)(2,1)S(1)} %all_gather.27.rows_ref, bf16[768,640]{1,0:T(8,128)(2,1)S(1)} %reshape.60.weight_ref, f32[4,1,192]{2,1,0:T(1,128)S(1)} %reshape.61.gain_ref, ...), custom_call_target="tpu_custom_call" | custom-call | tf_op jit(solution)/shard_map/attend/forward/pallas_call | solution.py:240
  98.6 0.9 copy-done.1
  99.5 8.0 %psum.7.logits_ref = f32[1,32]{1,0:T(1,128)S(1)} all-reduce(f32[1,32]{1,0:T(1,128)S(1)} %get-tuple-element.6), channel_id=1, replica_groups=mesh['y'=4,'z'=16,'c'=2,'x'=4] {'x'}, use_global_device_ids=true, to_apply=%region_3.4 | all-reduce | flops 32 | bytes 256 | tf_op jit(solution)/shard_map/attend/psum | solution.py:252
  107.6 1.1 copy-done.2
  108.7 3.3 %backward.1 = bf16[4,256,192]{2,1,0:T(8,128)(2,1)S(1)} custom-call(s32[2]{0:T(128)S(1)} %pad_add_fusion.place_ref, f32[1,32]{1,0:T(1,128)S(1)} %psum.7.logits_ref, s32[1,128]{1,0:T(1,128)S(1)} %bitcast.50, s32[1,128]{1,0:T(1,128)S(1)} %bitcast.51, bf16[4,256,256]{2,1,0:T(8,128)(2,1)S(1)} %all_gather.27.rows_ref, bf16[768,640]{1,0:T(8,128)(2,1)S(1)} %reshape.60.weight_ref, ...), custom_call_target="tpu_custom_call" | custom-call | tf_op jit(solution)/shard_map/attend/backward/pallas_call | solution.py:253
  112.2 8.6 %all_to_all.25 = bf16[4,256,192]{1,2,0:T(8,128)(2,1)S(1)} all-to-all(bf16[4,256,192]{1,2,0:T(8,128)(2,1)S(1)} %copy.67), channel_id=1, replica_groups=mesh['y'=4,'z'=16,'c'=2,'x'=4] {'x'}, dimensions={0} | all-to-all | bytes 786432 | tf_op jit(solution)/shard_map/give_back/all_to_all | solution.py:274
  121.7 19.8 %all-to-all-start.2 = ((bf16[128,2,192]{2,1,0:T(2,128)(2,1)}), bf16[128,2,192]{2,1,0:T(2,128)(2,1)S(1)}, u32[]{:S(2)}, u32[]{:S(2)}) async-start(bf16[128,2,192]{2,1,0:T(2,128)(2,1)} %reshape.63), calls=%async_computation.2 | async-start | bytes 262144 | tf_op jit(solution)/shard_map/give_back/all_to_all | solution.py:276
  141.7 17.2 %all-to-all-done.2 = bf16[128,2,192]{2,1,0:T(2,128)(2,1)S(1)} async-done(((bf16[128,2,192]{2,1,0:T(2,128)(2,1)}), bf16[128,2,192]{2,1,0:T(2,128)(2,1)S(1)}, u32[]{:S(2)}, u32[]{:S(2)}) %all-to-all-start.2) | async-done | bytes 98336 | tf_op jit(solution)/shard_map/give_back/all_to_all | solution.py:276
  159.5 4.6 %fusion = bf16[192,2048]{1,0:T(8,128)(2,1)S(1)} fusion(bf16[144,4,2048]{2,1,0:T(4,128)(2,1)} %param.11, bf16[144,192]{1,0:T(8,128)(2,1)S(1)} %convolution_multiply_fusion, u8[144,192]{1,0:T(8,128)(4,1)S(1)} %fusion.12), kind=kOutput, calls=%fused_computation.1 | convolution fusion | flops 453931008 | bytes 3228672 | tf_op jit(solution)/shard_map/encoder_grad/dot_general | solution.py:24
  164.3 17.6 %all_to_all.26 = bf16[8,24,2176]{2,1,0:T(8,128)(2,1)S(1)} all-to-all(bf16[8,24,2176]{2,1,0:T(8,128)(2,1)S(1)} %pad_maximum_fusion), channel_id=1, replica_groups=mesh['y'=4,'z'=16,'c'=2,'x'=4] {'y','c'}, dimensions={0} | all-to-all | bytes 1671168 | tf_op jit(solution)/shard_map/reduce/all_to_all | solution.py:297
  182.2 14.6 %all_to_all.27 = bf16[16,32,128]{2,1,0:T(8,128)(2,1)S(1)} all-to-all(bf16[16,32,128]{2,1,0:T(8,128)(2,1)S(1)} %pad_maximum_fusion.1), channel_id=1, replica_groups=mesh['y'=4,'z'=16,'c'=2,'x'=4] {'z'}, dimensions={0} | all-to-all | bytes 262144 | tf_op jit(solution)/shard_map/reduce/all_to_all | solution.py:308
  196.8 24.7 %all-gather.2 = bf16[512,128]{1,0:T(8,128)(2,1)} all-gather(bf16[32,128]{1,0:T(8,128)(2,1)S(1)} %reduce_sum.78), channel_id=4, replica_groups=mesh['y'=4,'z'=16,'c'=2,'x'=4] {'z'}, dimensions={0}, use_global_device_ids=true | all-gather | bytes 139264 | tf_op jit(solution)/shard_map/reduce/all_gather | solution.py:311
  221.6 30.8 %all-gather.7.cloned.1.call-done = bf16[128,32,128]{2,1,0:T(8,128)(2,1)} async-done(((bf16[16,32,128]{2,1,0:T(8,128)(2,1)}), bf16[128,32,128]{2,1,0:T(8,128)(2,1)}) %all-gather.7.cloned.1.call-update) | async-done | bytes 1048592 | tf_op jit(solution)/shard_map/reduce/all_gather | solution.py:312
  252.4 1.5 bitcast_convert_fusion
  255.0 1.7 copy.89
  (60 shorter events, 6.2 us)
Async XLA Ops:
  7.2 2.7 %copy-start = (bf16[2048,192]{0,1:T(8,128)(2,1)S(1)}, bf16[2048,192]{0,1:T(8,128)(2,1)}, u32[]{:S(2)}) copy-start(bf16[2048,192]{0,1:T(8,128)(2,1)} %param.16) | copy-start | bytes 2359300
  9.9 26.9 %copy-start.9 = (f32[768]{0:T(1024)S(1)}, f32[768]{0:T(1024)}, u32[]{:S(2)}) copy-start(f32[768]{0:T(1024)} %param.18) | copy-start | bytes 9220
  9.9 27.0 %copy-start.7 = (f32[768,32]{0,1:T(8,128)S(1)}, f32[768,32]{0,1:T(8,128)}, u32[]{:S(2)}) copy-start(f32[768,32]{0,1:T(8,128)} %param.21) | copy-start | bytes 294916
  9.9 27.0 %copy-start.8 = (bf16[6,768]{1,0:T(8,128)(2,1)S(1)}, bf16[6,768]{1,0:T(8,128)(2,1)}, u32[]{:S(2)}) copy-start(bf16[6,768]{1,0:T(8,128)(2,1)} %param.20) | copy-start | bytes 27652
  16.2 68.4 %all-to-all-start = ((bf16[128,2,256]{2,1,0:T(2,128)(2,1)}), bf16[128,2,256]{2,1,0:T(2,128)(2,1)S(1)}, u32[]{:S(2)}, u32[]{:S(2)}) async-start(bf16[128,2,256]{2,1,0:T(2,128)(2,1)} %reshape.57), calls=%async_computation | async-start | bytes 262144 | tf_op jit(solution)/shard_map/dispatch/all_to_all | solution.py:231
  84.0 23.5 %copy-start.3 = (s32[128]{0:T(128)S(1)}, s32[128]{0:T(128)}, u32[]{:S(2)}) copy-start(s32[128]{0:T(128)} %param.14) | copy-start | bytes 1540
  84.1 23.5 %copy-start.4 = (s32[128]{0:T(128)S(1)}, s32[128]{0:T(128)}, u32[]{:S(2)}) copy-start(s32[128]{0:T(128)} %param.15) | copy-start | bytes 1540
  98.6 0.9 copy-start.1
  107.5 4.7 %copy-start.5 = (f32[1,32]{1,0:T(1,128)}, f32[1,32]{1,0:T(1,128)S(1)}, u32[]{:S(2)}) copy-start(f32[1,32]{1,0:T(1,128)S(1)} %psum.7.logits_ref) | copy-start | bytes 388
  107.6 1.1 copy-start.2
  112.0 29.6 %copy-start.6 = (f32[144,4,192]{2,0,1:T(8,128)S(1)}, f32[144,4,192]{2,0,1:T(8,128)}, u32[]{:S(2)}) copy-start(f32[144,4,192]{2,0,1:T(8,128)} %get-tuple-element.15) | copy-start | bytes 1327108
  121.7 37.2 %all-to-all-start.2 = ((bf16[128,2,192]{2,1,0:T(2,128)(2,1)}), bf16[128,2,192]{2,1,0:T(2,128)(2,1)S(1)}, u32[]{:S(2)}, u32[]{:S(2)}) async-start(bf16[128,2,192]{2,1,0:T(2,128)(2,1)} %reshape.63), calls=%async_computation.2 | async-start | bytes 262144 | tf_op jit(solution)/shard_map/give_back/all_to_all | solution.py:276
  141.6 110.8 %all-gather.7.cloned.1.call-start = ((), (), s32[]{:S(2)}) async-start(), calls=%async_computation.5 | async-start | bytes 1179648 | tf_op jit(solution)/shard_map/reduce/all_gather | solution.py:312
Sparse Core Ops, SparseCore 0:
  221.7 30.6 all-gather.6

commit v2 on v1

--- a/solution.py
+++ b/solution.py
@@ -24,6 +24,11 @@
     return lax.dot_general(
         lhs, rhs, ((dims[:1], dims[1:]), ((), ())), precision=precision, preferred_element_type=f32
     )
+
+
+def gather_far(block, far_count):
+    copies = jnp.broadcast_to(block[None], (far_count,) + block.shape)
+    return lax.all_to_all(copies, "z", split_axis=0, concat_axis=0, tiled=True)
 
 
 def normed_parts(rows_ref, cols):
@@ -90,7 +95,7 @@
 
 def backward_kernel(
     place_ref,
-    logits_ref,
+    part_logits_ref,
     owner_ref,
     label_ref,
     rows_ref,
@@ -99,6 +104,7 @@
     cls_ref,
     att_ref,
     qkv_ref,
+    logits_ref,
     grad_ref,
 ):
     groups, slots, _ = rows_ref.shape
@@ -107,7 +113,8 @@
     tags = rows_ref[0, :, cols : cols + 1].astype(f32)
     live = (tags > 0).astype(f32)
     count = jnp.sum(live, axis=0, keepdims=True)
-    logits = logits_ref[...]
+    logits = sum(part_logits_ref[part] for part in range(groups))
+    logits_ref[...] = logits
     scaled = jnp.exp(logits - jnp.max(logits, axis=1, keepdims=True))
     class_probs = scaled / jnp.sum(scaled, axis=1, keepdims=True)
     mine = owner_ref[...] == place_ref[1]
@@ -162,7 +169,6 @@
     out_weight,
     cls_weight,
 ):
-    enc_count = lax.axis_size(ENC)
     far_count = lax.axis_size("z")
     near_count = lax.axis_size(NEAR)
     groups = lax.axis_size("x")
@@ -170,7 +176,7 @@
     cols = enc_weight.shape[1]
     emb = cols * groups
     slide_count = slide_owner.shape[0]
-    slot_total = enc_count * SLOTS
+    slot_total = far_count * near_count * SLOTS
     group_at = lax.axis_index("x")
     owner_at = lax.axis_index(ENC)
 
@@ -183,14 +189,10 @@
             for part in range(3)
         ]
         weight_rows = jnp.concatenate(picked + [wc_high, wc_low], axis=1)
-        far_rows = lax.all_gather(weight_rows, "z", axis=0, tiled=False)
-        near_rows = lax.all_gather(far_rows, NEAR, axis=0, tiled=False)
-        held = near_rows.shape[2:]
-        weights = (
-            near_rows.reshape((lax.axis_size("y"), lax.axis_size("c"), far_count) + held)
-            .transpose(0, 2, 1, 3, 4)
-            .reshape(emb, held[1])
-        )
+        far_rows = gather_far(weight_rows, far_count)
+        line_rows = lax.all_gather(far_rows, "y", axis=0)
+        held = lax.all_gather(line_rows, "c", axis=0)
+        weights = held.transpose(1, 2, 0, 3, 4).reshape(emb, held.shape[4])
 
     with jax.named_scope("encode"):
         flattened = features.reshape(tile_count * POS, channels)
@@ -213,23 +215,35 @@
         slot_rank = jnp.sum(
             ((slide_ids[:, None] == slide_ids[None, :]) & earlier).astype(jnp.int32), axis=1
         )
-        target = owners * SLOTS + slot_rank
+        near_owner = owners // (2 * far_count) * 2 + owners % 2
+        far_owner = owners // 2 % far_count
+        target = (far_owner * near_count + near_owner) * SLOTS + slot_rank
         placing = (jnp.arange(slot_total, dtype=jnp.int32)[:, None] == target[None, :]).astype(bf16)
+        unread = BLOCK - cols - 1
         tagged = jnp.concatenate(
             [
                 tile_rows,
                 (tile_pos + 1).astype(bf16)[:, None],
-                jnp.zeros((tile_count, BLOCK - cols - 1), bf16),
+                jnp.broadcast_to(far_rows[:1, 0, :unread], (tile_count, unread)),
             ],
             axis=1,
         )
         send_rows = (
             jnp.dot(placing, tagged, preferred_element_type=f32)
             .astype(bf16)
-            .reshape(enc_count, SLOTS, BLOCK)
-        )
-        slot_rows = lax.all_to_all(send_rows, ENC, split_axis=0, concat_axis=0, tiled=True)
-        rows = lax.all_gather(slot_rows.reshape(slot_total, BLOCK), "x", axis=0, tiled=False)
+            .reshape(far_count, near_count * SLOTS, BLOCK)
+        )
+        far_in = lax.all_to_all(send_rows, "z", split_axis=0, concat_axis=0, tiled=True)
+        lane = lax.broadcasted_iota(jnp.int32, far_in.shape, 2)
+        far_in = jnp.where(lane > cols, line_rows[0, :1, :1, :BLOCK], far_in)
+        by_near = far_in.reshape(far_count, near_count, SLOTS, BLOCK).transpose(1, 0, 2, 3)
+        send_near = jnp.broadcast_to(
+            by_near.reshape(1, near_count, far_count * SLOTS, BLOCK),
+            (groups, near_count, far_count * SLOTS, BLOCK),
+        ).reshape(groups * near_count, far_count * SLOTS, BLOCK)
+        rows = lax.all_to_all(
+            send_near, ("x",) + NEAR, split_axis=0, concat_axis=0, tiled=True
+        ).reshape(groups, slot_total, BLOCK)
 
     with jax.named_scope("attend"):
         place = jnp.stack([group_at, owner_at]).astype(jnp.int32)
@@ -249,17 +263,20 @@
             compiler_params=pltpu.CompilerParams(vmem_limit_bytes=32 << 20),
             name="forward",
         )(place, rows, weights, gain, cls_parts)
-        logits = lax.psum(part_logits, "x")
-        grad_parts = pl.pallas_call(
+        all_logits = lax.all_gather(part_logits, "x", axis=0)
+        logits, grad_parts = pl.pallas_call(
             backward_kernel,
-            out_shape=jax.ShapeDtypeStruct((groups, slot_total, cols), bf16),
+            out_shape=(
+                jax.ShapeDtypeStruct((1, CLASSES), f32),
+                jax.ShapeDtypeStruct((groups, slot_total, cols), bf16),
+            ),
             in_specs=[in_smem] + [in_vmem] * 9,
-            out_specs=in_vmem,
+            out_specs=(in_vmem,) * 2,
             compiler_params=pltpu.CompilerParams(vmem_limit_bytes=32 << 20),
             name="backward",
         )(
             place,
-            logits,
+            all_logits,
             slide_owner[None, :],
             slide_label[None, :],
             rows,
@@ -271,10 +288,20 @@
         )
 
     with jax.named_scope("give_back"):
-        from_groups = lax.all_to_all(grad_parts, "x", split_axis=0, concat_axis=0, tiled=True)
-        grad_rows = jnp.sum(from_groups.astype(f32), axis=0).astype(bf16)
+        from_near = lax.all_to_all(
+            grad_parts.reshape(groups * near_count, far_count * SLOTS, cols),
+            ("x",) + NEAR,
+            split_axis=0,
+            concat_axis=0,
+            tiled=True,
+        ).reshape(groups, near_count, far_count, SLOTS, cols)
+        grad_rows = jnp.sum(from_near.astype(f32), axis=0).astype(bf16)
         back_rows = lax.all_to_all(
-            grad_rows.reshape(enc_count, SLOTS, cols), ENC, split_axis=0, concat_axis=0, tiled=True
+            grad_rows.transpose(1, 0, 2, 3).reshape(far_count, near_count * SLOTS, cols),
+            "z",
+            split_axis=0,
+            concat_axis=0,
+            tiled=True,
         ).reshape(slot_total, cols)
 
     with jax.named_scope("encoder_grad"):
@@ -285,16 +312,25 @@
         bias_part = jnp.sum(grad_preact.astype(f32), axis=0).astype(bf16)
 
     with jax.named_scope("reduce"):
+        core_at = lax.axis_index("c")
         near_rows = cols // near_count
+        core_rows = cols // 2
         lanes = channels // far_count
-        bias_lanes = jnp.broadcast_to(
-            bias_part.reshape(near_count, near_rows, 1), (near_count, near_rows, lanes)
-        )
-        near_send = jnp.concatenate(
-            [grad_part.reshape(near_count, near_rows, channels), bias_lanes], axis=2
-        )
+        both = jnp.concatenate(
+            [grad_part, jnp.broadcast_to(bias_part[:, None], (cols, lanes))], axis=1
+        )
+        kept = lax.dynamic_slice_in_dim(both, core_at * core_rows, core_rows, 0)
+        sent = lax.dynamic_slice_in_dim(both, (1 - core_at) * core_rows, core_rows, 0)
+        other = lax.ppermute(sent, "c", [(0, 1), (1, 0)])
+        core_sum = (kept.astype(f32) + other.astype(f32)).astype(bf16)
         near_sum = jnp.sum(
-            lax.all_to_all(near_send, NEAR, split_axis=0, concat_axis=0, tiled=True).astype(f32),
+            lax.all_to_all(
+                core_sum.reshape(core_rows // near_rows, near_rows, channels + lanes),
+                "y",
+                split_axis=0,
+                concat_axis=0,
+                tiled=True,
+            ).astype(f32),
             axis=0,
         )
         far_send = (
@@ -302,18 +338,18 @@
         ).astype(bf16)
         bias_row = jnp.pad(near_sum[:, channels], (0, lanes - near_rows)).astype(bf16)
         far_send = jnp.concatenate(
-            [far_send, jnp.broadcast_to(bias_row[None, None, :], (far_count, 8, lanes))], axis=1
+            [far_send, jnp.broadcast_to(bias_row[None, None, :], (far_count, 1, lanes))], axis=1
         )
         far_sum = jnp.sum(
             lax.all_to_all(far_send, "z", split_axis=0, concat_axis=0, tiled=True).astype(f32),
             axis=0,
         ).astype(bf16)
-        far_all = lax.all_gather(far_sum, "z", axis=0, tiled=False)
-        all_parts = lax.all_gather(far_all, NEAR, axis=0, tiled=False).astype(f32)
+        far_all = gather_far(far_sum, far_count)
+        all_parts = lax.all_gather(lax.all_gather(far_all, "y", axis=0), "c", axis=0).astype(f32)
         enc_grad = (
-            all_parts[:, :, :near_rows].transpose(0, 2, 1, 3).reshape(cols, channels).T
-        )
-        bias_grad = all_parts[:, 0, near_rows, :near_rows].reshape(cols)
+            all_parts[:, :, :, :near_rows].transpose(0, 1, 3, 2, 4).reshape(cols, channels).T
+        )
+        bias_grad = all_parts[:, :, 0, near_rows, :near_rows].reshape(cols)
     return (logits, enc_grad, bias_grad)
 
 

time: 264 us -> 207 us (0.78)
  blocking collectives: 130 us -> 101 us
  waiting for transfers between devices: 48.1 us -> 25 us
  between operations: 14.4 us -> 1.02 us
  starting transfers between devices: 40.4 us -> 47.5 us
    all_gather x4 -> x5, blocking collectives: 81.1 us -> 38.8 us  [the longest x1 11.7 us: on_device(): line_rows = lax.all_gather(far_rows, 'y', axis=0)]
    all_gather x1 -> x0, waiting for transfers between devices: 30.8 us -> none  [on_device(): all_parts = lax.all_gather(far_all, NEAR, axis=0, tiled=False).astype(f32)]
    all_to_all x2 -> x3, blocking collectives: 26.2 us -> 45.1 us  [the longest x1 17.3 us: gather_far(): return lax.all_to_all(copies, 'z', split_axis=0, concat_axis=0, tiled=True)]
    psum x1 -> x0, blocking collectives: 8.02 us -> none  [on_device(): logits = lax.psum(part_logits, 'x')]
    all_to_all x2 -> x4, waiting for transfers between devices: 17.2 us -> 23.7 us  [the longest x1 12.7 us: on_device(): lax.all_to_all(grad_rows.transpose(1, 0, 2, 3).reshape(far_count, near_co...]
    all_to_all x2 -> x4, starting transfers between devices: 40.4 us -> 44.3 us  [the longest x1 15.7 us: gather_far(): return lax.all_to_all(copies, 'z', split_axis=0, concat_axis=0, tiled=True)]
    ppermute x0 -> x1, starting transfers between devices: none -> 3.13 us  [on_device(): other = lax.ppermute(sent, 'c', [(0, 1), (1, 0)])]
  transfers between devices with their start and end apart: 3 -> 5, of which waited for: 2 -> 5; matrix products, arithmetic and copies ran while one was open for 1% -> 5% of each run, Pallas kernels for 0% -> 0%
where the time goes in v2:
time: 207 us; the launch traced here: 206 us
  blocking collectives  101 us (49%)
  starting transfers between devices  47.5 us (23%)
  waiting for transfers between devices  25 us (12%)
  matrix products  11.1 us (5%)
  local copies, waits for them, and re-layouts  10.9 us (5%)
  Pallas kernels  6.28 us (3%)
  other arithmetic  3.47 us (2%)
    all_to_all x1, blocking collectives, gather_far(): return lax.all_to_all(copies, 'z', split_axis=0, concat_axis=0, tiled=True)  17.3 us
    all_to_all x1, blocking collectives, on_device(): lax.all_to_all(grad_parts.reshape(groups * near_count, far_count * SLOTS,...  17 us
    all_to_all x1, blocking collectives, on_device(): lax.all_to_all(far_send, 'z', split_axis=0, concat_axis=0, tiled=True)  16.6 us
    all_to_all x1, starting transfers between devices, gather_far(): return lax.all_to_all(copies, 'z', split_axis=0, concat_axis=0, tiled=True)  15.7 us
    all_to_all x1, waiting for transfers between devices, on_device(): lax.all_to_all(grad_rows.transpose(1, 0, 2, 3).reshape(far_count, near_co...  12.7 us
    all_gather x1, blocking collectives, on_device(): line_rows = lax.all_gather(far_rows, 'y', axis=0)  11.7 us
    all_to_all x1, blocking collectives, on_device(): lax.all_to_all(core_sum.reshape(core_rows // near_rows, near_rows, channe...  10.9 us
    all_to_all x1, starting transfers between devices, on_device(): lax.all_to_all(send_near, ('x',) + NEAR, split_axis=0, concat_axis=0, til...  10.7 us
  transfers between devices with their start and end apart: 5, of which 5 were waited for; matrix products, arithmetic and copies ran while one was open for 5% of the time, Pallas kernels for 0%

profile of v2, /device:TPU:1, one launch (start us, length us, event | category | flops | bytes accessed | tf_op | source)
XLA Modules:
  0.0 205.9 jit_solution(4784572328286441814)
XLA Ops:
  3.4 15.7 %all-to-all-start = ((bf16[16,6,640]{2,1,0:T(8,128)(2,1)}), bf16[16,6,640]{2,1,0:T(8,128)(2,1)S(1)}, u32[]{:S(2)}, u32[]{:S(2)}) async-start(bf16[16,6,640]{2,1,0:T(8,128)(2,1)} %broadcast_in_dim.54), calls=%async_computation | async-start | bytes 327680 | tf_op jit(solution)/shard_map/weights/all_to_all | solution.py:31
  20.8 4.3 %maximum_reduce_fusion = (f32[144,192]{1,0:T(8,128)S(1)}, f32[144,4,192]{2,0,1:T(8,128)S(1)}) fusion(f32[192]{0:T(256)} %param.17, bf16[2048,192]{0,1:T(8,128)(2,1)S(1)} %copy-done, bf16[144,4,2048]{2,1,0:T(4,128)(2,1)} %param.11), kind=kOutput, calls=%fused_computation.19 | convolution fusion | flops 453288960 | bytes 3699456 | tf_op jit(solution)/shard_map/encode/dot_general | solution.py:200
  25.5 5.8 %all-to-all-done = bf16[16,6,640]{2,1,0:T(8,128)(2,1)S(1)} async-done(((bf16[16,6,640]{2,1,0:T(8,128)(2,1)}), bf16[16,6,640]{2,1,0:T(8,128)(2,1)S(1)}, u32[]{:S(2)}, u32[]{:S(2)}) %all-to-all-start) | async-done | bytes 122912 | tf_op jit(solution)/shard_map/weights/all_to_all | solution.py:31
  32.3 7.7 %all-to-all-start.1 = ((bf16[16,16,256]{2,1,0:T(8,128)(2,1)}), bf16[16,16,256]{2,1,0:T(8,128)(2,1)S(1)}, u32[]{:S(2)}, u32[]{:S(2)}) async-start(bf16[16,16,256]{2,1,0:T(8,128)(2,1)} %bitcast.6), calls=%async_computation.1 | async-start | bytes 262144 | tf_op jit(solution)/shard_map/dispatch/all_to_all | solution.py:236
  40.1 11.7 %all-gather = bf16[64,6,640]{2,0,1:T(8,128)(2,1)S(1)} all-gather(bf16[16,6,640]{2,0,1:T(8,128)(2,1)S(1)} %copy.68), channel_id=2, replica_groups=mesh['y'=4,'z'=16,'c'=2,'x'=4] {'y'}, dimensions={0}, use_global_device_ids=true | all-gather | bytes 614400 | tf_op jit(solution)/shard_map/weights/all_gather | solution.py:193
  53.1 10.7 %all-to-all-start.2 = ((bf16[32,32,256]{2,1,0:T(8,128)(2,1)}), bf16[32,32,256]{2,1,0:T(8,128)(2,1)S(1)}, u32[]{:S(2)}, u32[]{:S(2)}) async-start(bf16[32,32,256]{2,1,0:T(8,128)(2,1)} %bitcast.10), calls=%async_computation.2 | async-start | bytes 1048576 | tf_op jit(solution)/shard_map/dispatch/all_to_all | solution.py:244
  64.2 2.5 %all-gather.1 = bf16[8,16,6,640]{3,1,0,2:T(8,128)(2,1)S(1)} all-gather(bf16[4,16,6,640]{3,1,0,2:T(8,128)(2,1)S(1)} %bitcast.70), channel_id=3, replica_groups=mesh['y'=4,'z'=16,'c'=2,'x'=4] {'c'}, dimensions={0}, use_global_device_ids=true | all-gather | bytes 1474560 | tf_op jit(solution)/shard_map/weights/all_gather | solution.py:194
  66.7 1.6 copy.75
  68.3 2.2 %reshape.128.weight_ref = bf16[768,640]{1,0:T(8,128)(2,1)S(1)} reshape(bf16[4,16,2,6,640]{4,3,2,1,0:T(8,128)(2,1)} %copy.75) | data formatting | bytes 1966080 | tf_op jit(solution)/shard_map/weights/reshape | solution.py:195
  70.5 4.9 %all-to-all-done.2 = bf16[32,32,256]{2,1,0:T(8,128)(2,1)S(1)} async-done(((bf16[32,32,256]{2,1,0:T(8,128)(2,1)}), bf16[32,32,256]{2,1,0:T(8,128)(2,1)S(1)}, u32[]{:S(2)}, u32[]{:S(2)}) %all-to-all-start.2) | async-done | bytes 524320 | tf_op jit(solution)/shard_map/dispatch/all_to_all | solution.py:244
  75.4 3.0 %forward.1 = (f32[1,32]{1,0:T(1,128)S(1)}, f32[3,256,256]{2,1,0:T(8,128)S(1)}, bf16[256,576]{1,0:T(8,128)(2,1)S(1)}) custom-call(s32[2]{0:T(128)S(1)} %pad_add_fusion.place_ref, bf16[4,256,256]{2,1,0:T(8,128)(2,1)S(1)} %bitcast.58, bf16[768,640]{1,0:T(8,128)(2,1)S(1)} %reshape.128.weight_ref, f32[4,1,192]{2,1,0:T(1,128)S(1)} %reshape.129.gain_ref, ...), custom_call_target="tpu_custom_call" | custom-call | tf_op jit(solution)/shard_map/attend/forward/pallas_call | solution.py:254
  78.4 5.8 %all-gather.5.part_logits_ref = f32[4,1,32]{2,1,0:T(1,128)S(1)} all-gather(f32[1,1,32]{2,1,0:T(1,128)S(1)} %bitcast.65), channel_id=4, replica_groups=mesh['y'=4,'z'=16,'c'=2,'x'=4] {'x'}, dimensions={0}, use_global_device_ids=true | all-gather | bytes 640 | tf_op jit(solution)/shard_map/attend/all_gather | solution.py:266
  84.3 3.3 %backward.1 = (f32[1,32]{1,0:T(1,128)}, bf16[4,256,192]{2,1,0:T(8,128)(2,1)S(1)}) custom-call(s32[2]{0:T(128)S(1)} %pad_add_fusion.place_ref, f32[4,1,32]{2,1,0:T(1,128)S(1)} %all-gather.5.part_logits_ref, s32[1,128]{1,0:T(1,128)S(1)} %bitcast.63, s32[1,128]{1,0:T(1,128)S(1)} %bitcast.64, bf16[4,256,256]{2,1,0:T(8,128)(2,1)S(1)} %bitcast.59, ...), custom_call_target="tpu_custom_call" | custom-call | tf_op jit(solution)/shard_map/attend/backward/pallas_call | solution.py:267
  87.6 17.0 %all_to_all.40 = bf16[32,32,192]{2,1,0:T(8,128)(2,1)S(1)} all-to-all(bf16[32,32,192]{2,1,0:T(8,128)(2,1)S(1)} %bitcast.62), channel_id=1, replica_groups=mesh['y'=4,'z'=16,'c'=2,'x'=4] {'x','y','c'}, dimensions={0} | all-to-all | bytes 786432 | tf_op jit(solution)/shard_map/give_back/all_to_all | solution.py:291
  106.4 10.2 %all-to-all-start.4 = ((bf16[16,16,192]{2,1,0:T(8,128)(2,1)}), bf16[16,16,192]{2,1,0:T(8,128)(2,1)S(1)}, u32[]{:S(2)}, u32[]{:S(2)}) async-start(bf16[16,16,192]{2,1,0:T(8,128)(2,1)} %copy.78), calls=%async_computation.4 | async-start | bytes 262144 | tf_op jit(solution)/shard_map/give_back/all_to_all | solution.py:299
  116.7 12.7 %all-to-all-done.4 = bf16[16,16,192]{2,1,0:T(8,128)(2,1)S(1)} async-done(((bf16[16,16,192]{2,1,0:T(8,128)(2,1)}), bf16[16,16,192]{2,1,0:T(8,128)(2,1)S(1)}, u32[]{:S(2)}, u32[]{:S(2)}) %all-to-all-start.4) | async-done | bytes 98336 | tf_op jit(solution)/shard_map/give_back/all_to_all | solution.py:299
  129.7 4.6 %fusion = bf16[192,2048]{1,0:T(8,128)(2,1)S(1)} fusion(bf16[144,4,2048]{2,1,0:T(4,128)(2,1)} %param.11, bf16[144,192]{1,0:T(8,128)(2,1)S(1)} %convolution_multiply_fusion, u8[144,192]{1,0:T(8,128)(4,1)S(1)} %fusion.14), kind=kOutput, calls=%fused_computation.1 | convolution fusion | flops 453931008 | bytes 3228672 | tf_op jit(solution)/shard_map/encoder_grad/dot_general | solution.py:24
  134.4 3.1 %collective-permute-start = (bf16[96,2176]{1,0:T(8,128)(2,1)S(1)}, bf16[96,2176]{1,0:T(8,128)(2,1)S(1)}, u32[]{:S(2)}, u32[]{:S(2)}) collective-permute-start(bf16[96,2176]{1,0:T(8,128)(2,1)S(1)} %fusion.8), channel_id=1, source_target_pairs={{0,4},{4,0},{1,5},{5,1},{2,6},{6,2},{3,7},{7,3},{8,12},{12,8},{9,1... | collective-permute-start | bytes 1253384 | tf_op jit(solution)/shard_map/reduce/ppermute | solution.py:324
  139.0 10.9 %all_to_all.41 = bf16[4,24,2176]{2,1,0:T(8,128)(2,1)S(1)} all-to-all(bf16[4,24,2176]{2,1,0:T(8,128)(2,1)S(1)} %bitcast.71), channel_id=1, replica_groups=mesh['y'=4,'z'=16,'c'=2,'x'=4] {'y'}, dimensions={0} | all-to-all | bytes 835584 | tf_op jit(solution)/shard_map/reduce/all_to_all | solution.py:327
  150.2 16.6 %all_to_all.42 = bf16[16,25,128]{2,1,0:T(8,128)(2,1)S(1)} all-to-all(bf16[16,25,128]{2,1,0:T(8,128)(2,1)S(1)} %copy.80), channel_id=1, replica_groups=mesh['y'=4,'z'=16,'c'=2,'x'=4] {'z'}, dimensions={0} | all-to-all | bytes 204800 | tf_op jit(solution)/shard_map/reduce/all_to_all | solution.py:344
  166.8 17.3 %all_to_all.43 = bf16[16,25,128]{2,1,0:T(8,128)(2,1)S(1)} all-to-all(bf16[16,25,128]{2,1,0:T(8,128)(2,1)S(1)} %broadcast_in_dim.102), channel_id=1, replica_groups=mesh['y'=4,'z'=16,'c'=2,'x'=4] {'z'}, dimensions={0} | all-to-all | bytes 204800 | tf_op jit(solution)/shard_map/reduce/all_to_all | solution.py:31
  184.1 9.8 %all-gather.3 = bf16[64,25,128]{2,0,1:T(8,128)(2,1)S(1)} all-gather(bf16[16,25,128]{2,0,1:T(8,128)(2,1)S(1)} %copy.83), channel_id=5, replica_groups=mesh['y'=4,'z'=16,'c'=2,'x'=4] {'y'}, dimensions={0}, use_global_device_ids=true | all-gather | bytes 512000 | tf_op jit(solution)/shard_map/reduce/all_gather | solution.py:348
  193.9 9.0 %all-gather.4 = bf16[8,16,25,128]{3,1,0,2:T(8,128)(2,1)S(1)} all-gather(bf16[4,16,25,128]{3,1,0,2:T(8,128)(2,1)S(1)} %bitcast.72), channel_id=6, replica_groups=mesh['y'=4,'z'=16,'c'=2,'x'=4] {'c'}, dimensions={0}, use_global_device_ids=true | all-gather | bytes 1228800 | tf_op jit(solution)/shard_map/reduce/all_gather | solution.py:348
  204.1 1.8 copy.100
  (64 shorter events, 12.7 us)
Async XLA Ops:
  0.6 20.1 %copy-start = (bf16[2048,192]{0,1:T(8,128)(2,1)S(1)}, bf16[2048,192]{0,1:T(8,128)(2,1)}, u32[]{:S(2)}) copy-start(bf16[2048,192]{0,1:T(8,128)(2,1)} %param.16) | copy-start | bytes 2359300
  3.4 28.0 %all-to-all-start = ((bf16[16,6,640]{2,1,0:T(8,128)(2,1)}), bf16[16,6,640]{2,1,0:T(8,128)(2,1)S(1)}, u32[]{:S(2)}, u32[]{:S(2)}) async-start(bf16[16,6,640]{2,1,0:T(8,128)(2,1)} %broadcast_in_dim.54), calls=%async_computation | async-start | bytes 327680 | tf_op jit(solution)/shard_map/weights/all_to_all | solution.py:31
  20.8 4.4 %copy-start.1 = (s32[128]{0:T(128)S(1)}, s32[128]{0:T(128)}, u32[]{:S(2)}) copy-start(s32[128]{0:T(128)} %param.14) | copy-start | bytes 1540
  20.8 4.4 %copy-start.4 = (s32[144,1]{0,1:T(1,128)S(1)}, s32[144,1]{0,1:T(1,128)}, u32[]{:S(2)}) copy-start(s32[144,1]{0,1:T(1,128)} %param.12) | copy-start | bytes 1732
  25.2 38.7 %copy-start.5 = (f32[768]{0:T(1024)S(1)}, f32[768]{0:T(1024)}, u32[]{:S(2)}) copy-start(f32[768]{0:T(1024)} %param.18) | copy-start | bytes 9220
  25.2 38.7 %copy-start.3 = (f32[768,32]{0,1:T(8,128)S(1)}, f32[768,32]{0,1:T(8,128)}, u32[]{:S(2)}) copy-start(f32[768,32]{0,1:T(8,128)} %param.21) | copy-start | bytes 294916
  32.3 19.7 %all-to-all-start.1 = ((bf16[16,16,256]{2,1,0:T(8,128)(2,1)}), bf16[16,16,256]{2,1,0:T(8,128)(2,1)S(1)}, u32[]{:S(2)}, u32[]{:S(2)}) async-start(bf16[16,16,256]{2,1,0:T(8,128)(2,1)} %bitcast.6), calls=%async_computation.1 | async-start | bytes 262144 | tf_op jit(solution)/shard_map/dispatch/all_to_all | solution.py:236
  53.1 22.4 %all-to-all-start.2 = ((bf16[32,32,256]{2,1,0:T(8,128)(2,1)}), bf16[32,32,256]{2,1,0:T(8,128)(2,1)S(1)}, u32[]{:S(2)}, u32[]{:S(2)}) async-start(bf16[32,32,256]{2,1,0:T(8,128)(2,1)} %bitcast.10), calls=%async_computation.2 | async-start | bytes 1048576 | tf_op jit(solution)/shard_map/dispatch/all_to_all | solution.py:244
  68.3 15.9 %copy-start.2 = (s32[128]{0:T(128)S(1)}, s32[128]{0:T(128)}, u32[]{:S(2)}) copy-start(s32[128]{0:T(128)} %param.15) | copy-start | bytes 1540
  106.4 22.9 %all-to-all-start.4 = ((bf16[16,16,192]{2,1,0:T(8,128)(2,1)}), bf16[16,16,192]{2,1,0:T(8,128)(2,1)S(1)}, u32[]{:S(2)}, u32[]{:S(2)}) async-start(bf16[16,16,192]{2,1,0:T(8,128)(2,1)} %copy.78), calls=%async_computation.4 | async-start | bytes 262144 | tf_op jit(solution)/shard_map/give_back/all_to_all | solution.py:299
  134.4 4.5 %collective-permute-start = (bf16[96,2176]{1,0:T(8,128)(2,1)S(1)}, bf16[96,2176]{1,0:T(8,128)(2,1)S(1)}, u32[]{:S(2)}, u32[]{:S(2)}) collective-permute-start(bf16[96,2176]{1,0:T(8,128)(2,1)S(1)} %fusion.8), channel_id=1, source_target_pairs={{0,4},{4,0},{1,5},{5,1},{2,6},{6,2},{3,7},{7,3},{8,12},{12,8},{9,1... | collective-permute-start | bytes 1253384 | tf_op jit(solution)/shard_map/reduce/ppermute | solution.py:324

commit v3 on v1

v3 whole, which is shorter than its diff:
```python
import functools

import jax
import jax.numpy as jnp
from jax import lax
from jax.experimental import pallas as pl
from jax.experimental.pallas import tpu as pltpu
from jax.sharding import Mesh, PartitionSpec as P

POS = 4
HEADS = 12
CLASSES = 32
HD = 64
SLOTS = 2
BLOCK = 256
LANES = 128
FAR = ("zh", "zl")
ENC = ("y", "zh", "zl", "c")
NEAR = ("y", "c")
PLANE = ("y", "zl")
eps = 1e-05

bf16 = jnp.bfloat16
f32 = jnp.float32
EXACT = lax.Precision.HIGHEST


def across(lhs, rhs, dims, precision=None):
    return lax.dot_general(
        lhs, rhs, ((dims[:1], dims[1:]), ((), ())), precision=precision, preferred_element_type=f32
    )


def swap(blocks, axes):
    return lax.all_to_all(blocks, axes, split_axis=0, concat_axis=0, tiled=True)


def gather_copies(block, axes):
    return swap(jnp.broadcast_to(block[None], (lax.axis_size(axes),) + block.shape), axes)


def sum_blocks(blocks, axes):
    return jnp.sum(swap(blocks, axes).astype(f32), axis=0).astype(bf16)


def normed_parts(rows_ref, cols):
    parts = [rows_ref[part, :, :cols].astype(f32) for part in range(rows_ref.shape[0])]
    width = cols * len(parts)
    mean = sum(jnp.sum(part, axis=1, keepdims=True) for part in parts) / width
    centred = [part - mean for part in parts]
    variance = sum(jnp.sum(part * part, axis=1, keepdims=True) for part in centred) / width
    inv_std = lax.rsqrt(variance + eps)
    return parts, [part * inv_std for part in centred], inv_std


def forward_kernel(
    own_rows, place_ref, rows_ref, weight_ref, gain_ref, cls_ref, logits_ref, att_ref, qkv_ref
):
    groups, slots, _ = rows_ref.shape
    cols = gain_ref.shape[2]
    parts, normed, _ = normed_parts(rows_ref, cols)
    size = weight_ref.shape[2] // (-(-(3 * cols + 2 * CLASSES) // LANES))
    order = held_order(own_rows, cols)
    qkv = 0.0
    for part in range(groups):
        normed_in = (normed[part] * gain_ref[part]).astype(bf16)
        normed_in = across(normed_in, order, (1, 0)).astype(bf16)
        block = jnp.concatenate(weight_block(weight_ref, part, size), axis=1)
        qkv = qkv + across(normed_in, block, (1, 0))
    qkv = qkv[:, : 3 * cols]
    column = lax.broadcasted_iota(jnp.int32, (slots, 3 * cols), 1)
    qkv = jnp.where(column < cols, qkv * HD ** (-0.5), qkv).astype(bf16)
    qkv_ref[...] = qkv
    tags = rows_ref[0, :, cols : cols + 1].astype(f32)
    count = jnp.sum(tags, axis=0, keepdims=True) * 0.0 + jnp.sum(
        (tags > 0).astype(f32), axis=0, keepdims=True
    )
    down = lax.broadcasted_iota(jnp.int32, (slots, slots), 0)
    along = lax.broadcasted_iota(jnp.int32, (slots, slots), 1)
    tag_row = jnp.sum(jnp.where(down == along, tags, 0.0), axis=0, keepdims=True)
    query_pos = tags.astype(jnp.int32) - 1
    key_pos = tag_row.astype(jnp.int32) - 1
    wc = class_block(weight_ref, order, place_ref[0], size, cols)
    total = jnp.zeros((1, CLASSES), f32)
    for head in range(cols // HD):
        group = head % 3
        low = (1 << group) - 1
        query_key = ((query_pos >> (6 + group)) << group) + (query_pos & low)
        key_key = ((key_pos >> (6 + group)) << group) + (key_pos & low)
        query_key = jnp.where(query_pos < 0, -1, query_key)
        key_key = jnp.where(key_pos < 0, -2, key_key)
        visible = query_key == key_key
        first = head * HD
        scores = across(
            qkv[:, first : first + HD], qkv[:, cols + first : cols + first + HD], (1, 1)
        )
        masked = jnp.where(visible, scores, -1e30)
        row_max = jnp.max(masked, axis=1, keepdims=True)
        weights = jnp.where(visible, jnp.exp(masked - row_max), 0.0)
        row_total = jnp.sum(weights, axis=1, keepdims=True)
        att = weights / jnp.where(row_total > 0, row_total, 1.0)
        att_ref[head] = att
        att_total = jnp.sum(att.astype(bf16).astype(f32), axis=0, keepdims=True)
        values = qkv[:, 2 * cols + first : 2 * cols + first + HD].astype(f32)
        mixed_total = across(att_total, values, (1, 0), EXACT)
        total = total + across(mixed_total, wc[first : first + HD], (1, 0), EXACT)
    for part in range(groups):
        row_sum = jnp.sum(parts[part], axis=0, keepdims=True) * (1.0 / groups)
        total = total + across(row_sum, cls_ref[part], (1, 1), EXACT)
    logits_ref[...] = total / count


def backward_kernel(
    own_rows,
    place_ref,
    part_logits_ref,
    owner_ref,
    label_ref,
    rows_ref,
    weight_ref,
    gain_ref,
    cls_ref,
    att_ref,
    qkv_ref,
    logits_ref,
    grad_ref,
):
    groups, slots, _ = rows_ref.shape
    cols = gain_ref.shape[2]
    _, normed, inv_std = normed_parts(rows_ref, cols)
    tags = rows_ref[0, :, cols : cols + 1].astype(f32)
    live = (tags > 0).astype(f32)
    count = jnp.sum(live, axis=0, keepdims=True)
    logits = sum(part_logits_ref[part] for part in range(groups))
    logits_ref[...] = logits
    scaled = jnp.exp(logits - jnp.max(logits, axis=1, keepdims=True))
    class_probs = scaled / jnp.sum(scaled, axis=1, keepdims=True)
    mine = owner_ref[...] == place_ref[1]
    my_label = jnp.sum(jnp.where(mine, label_ref[...], 0).astype(f32), axis=1, keepdims=True)
    class_ids = lax.broadcasted_iota(jnp.int32, (1, CLASSES), 1).astype(f32)
    grad_logits = (class_probs - (class_ids == my_label).astype(f32)) / count
    size = weight_ref.shape[2] // (-(-(3 * cols + 2 * CLASSES) // LANES))
    order = held_order(own_rows, cols)
    wc = class_block(weight_ref, order, place_ref[0], size, cols)
    grad_mixed = across(grad_logits, wc, (1, 1), EXACT).astype(bf16)
    qkv = qkv_ref[...]
    grad_q, grad_k, grad_v = [], [], []
    for head in range(cols // HD):
        first = head * HD
        att = att_ref[head]
        queries = qkv[:, first : first + HD]
        keys = qkv[:, cols + first : cols + first + HD]
        values = qkv[:, 2 * cols + first : 2 * cols + first + HD]
        head_grad = grad_mixed[:, first : first + HD]
        grad_att = across(head_grad, values, (1, 1))
        expected = jnp.sum(att * grad_att, axis=1, keepdims=True)
        grad_scores = (att * (grad_att - expected)).astype(bf16)
        grad_q.append(across(grad_scores, keys, (1, 0)) * HD ** (-0.5))
        grad_k.append(across(grad_scores, queries, (0, 0)))
        spread = jnp.broadcast_to(head_grad, (slots, HD))
        grad_v.append(across(att.astype(bf16), spread, (0, 0)))
    unused = jnp.zeros((slots, 2 * CLASSES), f32)
    grad_qkv = jnp.concatenate(grad_q + grad_k + grad_v + [unused], axis=1).astype(bf16)
    scaled_parts = []
    for part in range(groups):
        block = jnp.concatenate(weight_block(weight_ref, part, size), axis=1)
        grad_normed = across(grad_qkv, block, (1, 1))
        high = grad_normed.astype(bf16)
        low = (grad_normed - high.astype(f32)).astype(bf16)
        grad_normed = across(high, order, (1, 1)) + across(low, order, (1, 1))
        scaled_parts.append(grad_normed * gain_ref[part])
    width = cols * groups
    mean = sum(jnp.sum(e, axis=1, keepdims=True) for e in scaled_parts) / width
    slope = (
        sum(jnp.sum(e * n, axis=1, keepdims=True) for e, n in zip(scaled_parts, normed)) / width
    )
    for part in range(groups):
        pooled = across(grad_logits, cls_ref[part], (1, 0), EXACT) * (1.0 / groups)
        grad = inv_std * (scaled_parts[part] - mean - normed[part] * slope)
        grad_ref[part] = (live * pooled + grad).astype(bf16)


def as_column(row):
    size = row.shape[1]
    down = lax.broadcasted_iota(jnp.int32, (size, size), 0)
    along = lax.broadcasted_iota(jnp.int32, (size, size), 1)
    return jnp.sum(jnp.where(down == along, row, 0.0), axis=1, keepdims=True)


def held_rows(rows):
    return (rows + 8) // 8 * 8


def fold_rows(rows, count):
    blocks = rows.reshape(count, 2 * 8, rows.shape[1])
    rest = jnp.concatenate([blocks[:, :8, LANES:], blocks[:, 8:, LANES:]], axis=2)
    return jnp.concatenate([blocks[:, :, :LANES], rest], axis=1)


def unfold_rows(blocks):
    rest = blocks[:, 16:24]
    half = LANES // 2
    rest = jnp.concatenate([rest[:, :, :half], rest[:, :, half:]], axis=1)
    size = blocks.shape[0] * 16
    return blocks[:, :16].reshape(size, LANES), rest.reshape(size, half)


def slot_order(far_bits, slots):
    at = lax.broadcasted_iota(jnp.int32, (slots, slots), 0)
    source = lax.broadcasted_iota(jnp.int32, (slots, slots), 1)
    near = at >> (far_bits + 1)
    far = (at >> 1) & ((1 << far_bits) - 1)
    return (source == far * 16 + near * 2 + (at & 1)).astype(f32).astype(bf16)


def send_kernel(place_ref, *refs):
    sources, refs = refs[:9], refs[9:]
    send_ref, mask_ref, placing_ref = refs[:3]
    targets, sems = refs[3:12], refs[12]
    copies = [
        pltpu.make_async_copy(source, target, sems.at[number])
        for number, (source, target) in enumerate(zip(sources, targets))
    ]
    for copy in copies:
        copy.start()
    slide_ref, pos_ref, owner_ref, qkv_ref, out_ref, cls_ref = targets[:6]
    bias_ref, weight_ref, features_ref = targets[6:]
    for copy in copies[:6]:
        copy.wait()
    tiles, positions, channels = features_ref.shape
    far_count = send_ref.shape[0]
    cols = weight_ref.shape[0]
    slides = owner_ref.shape[1]

    slide_row = slide_ref[...]
    owner_column = as_column(owner_ref[...].astype(f32))
    slide_ids = lax.broadcasted_iota(jnp.int32, (slides, tiles), 0)
    owners = jnp.sum(
        jnp.where(slide_ids == slide_row, owner_column, 0.0), axis=0, keepdims=True
    ).astype(jnp.int32)
    slide_values = slide_row.astype(f32)
    down = lax.broadcasted_iota(jnp.int32, (tiles, tiles), 0)
    along = lax.broadcasted_iota(jnp.int32, (tiles, tiles), 1)
    earlier = (as_column(slide_values) == slide_values) & (down < along)
    slot_rank = jnp.sum(earlier.astype(f32), axis=0, keepdims=True).astype(jnp.int32)
    owner_pair = owners >> 1
    line = sum((owner_pair >= far_count * number).astype(jnp.int32) for number in range(1, 4))
    near_owner = line * 2 + (owners & 1)
    far_owner = owner_pair - line * far_count
    target = (far_owner * 8 + near_owner) * SLOTS + slot_rank
    slots = lax.broadcasted_iota(jnp.int32, placing_ref.shape, 0)
    placing = slots == target
    tags = jnp.sum(
        jnp.where(placing, (pos_ref[...] + 1).astype(f32), 0.0), axis=1, keepdims=True
    )
    placing = placing.astype(f32).astype(bf16)
    placing_ref[...] = placing
    slot_ids = lax.broadcasted_iota(jnp.int32, (far_count * 16, LANES), 0)
    lane_ids = lax.broadcasted_iota(jnp.int32, (far_count * 16, LANES), 1)
    tag_rows = jnp.where(lane_ids == (slot_ids & 15), tags, 0.0)
    tag_rows = jnp.sum(tag_rows.reshape(far_count, 16, LANES), axis=1)

    own_rows, emb = out_ref.shape
    wc = across(out_ref[...].astype(f32), cls_ref[...], (1, 1), EXACT)
    wc_high = wc.astype(bf16).astype(f32)
    picked = []
    for part in range(3):
        block = qkv_ref[:, part * emb : part * emb + cols]
        for group in range(1, emb // cols):
            first = part * emb + group * cols
            block = jnp.where(place_ref[0] == group, qkv_ref[:, first : first + cols], block)
        picked.append(block.astype(f32))
    rows = jnp.concatenate(picked + [wc_high, wc - wc_high], axis=1)
    padded = held_rows(own_rows)
    rows = jnp.concatenate([rows, jnp.zeros((padded - own_rows, rows.shape[1]), f32)], axis=0)
    held = [rows[:, at : at + LANES] for at in range(0, rows.shape[1], LANES)]
    is_tag = lax.broadcasted_iota(jnp.int32, (padded, LANES), 0) == own_rows

    for copy in copies[6:]:
        copy.wait()
    flattened = features_ref[...].reshape(tiles * positions, channels)
    preact = across(flattened, weight_ref[...], (1, 1)) + bias_ref[...]
    mask_ref[...] = jnp.where(preact > 0, 1.0 / positions, 0.0).astype(bf16)
    summed = jnp.sum(jnp.maximum(preact, 0.0).reshape(tiles, positions, cols), axis=1)
    tile_rows = (summed * (1.0 / positions)).astype(bf16)
    blocks = fold_rows(across(placing, tile_rows, (1, 0)), far_count)
    for far in range(far_count):
        first = jnp.where(is_tag, tag_rows[far : far + 1], held[0])
        send_ref[far] = jnp.concatenate([blocks[far], first] + held[1:], axis=0).astype(bf16)


def turn_kernel(own_rows, received_ref, rows_ref, held_ref):
    far_count = received_ref.shape[0]
    slots = far_count * 16
    far_bits = far_count.bit_length() - 1
    received = received_ref[...].astype(f32)
    order = slot_order(far_bits, slots)
    wide, narrow = unfold_rows(received)
    wide = across(order, wide.astype(bf16), (1, 0))
    narrow = across(order, narrow.astype(bf16), (1, 0))
    slot = lax.broadcasted_iota(jnp.int32, (slots, far_count), 0)
    far = lax.broadcasted_iota(jnp.int32, (slots, far_count), 1)
    from_far = (((slot >> 1) & (far_count - 1)) == far).astype(f32).astype(bf16)
    tag_rows = received[:, 24 + own_rows].astype(bf16)
    slot = lax.broadcasted_iota(jnp.int32, (slots, LANES), 0)
    lane = lax.broadcasted_iota(jnp.int32, (slots, LANES), 1)
    mine = lane == (slot >> (far_bits + 1)) * 2 + (slot & 1)
    tags = jnp.sum(
        jnp.where(mine, across(from_far, tag_rows, (1, 0)), 0.0), axis=1, keepdims=True
    )
    tags = jnp.broadcast_to(tags, (slots, LANES // 2))
    rows = jnp.concatenate([wide, narrow, tags], axis=1).astype(bf16)
    rows = rows.reshape(rows_ref.shape[1:])
    for group in range(rows_ref.shape[0]):
        rows_ref[group] = rows
    padded = held_rows(own_rows)
    size = far_count * own_rows
    row = lax.broadcasted_iota(jnp.int32, (size, 1), 0).astype(f32)
    column = lax.broadcasted_iota(jnp.int32, (size, far_count * padded), 1)
    far = jnp.floor((row + 0.5) * (1.0 / own_rows))
    kept = (column == (row + far * (padded - own_rows)).astype(jnp.int32)).astype(f32).astype(bf16)
    for block in range(held_ref.shape[0] // size):
        first = 24 + block * padded
        held = received[:, first : first + padded].reshape(far_count * padded, LANES)
        held = across(kept, held.astype(bf16), (1, 0))
        held_ref[block * size : (block + 1) * size] = held.astype(bf16)


def fold_kernel(parts_ref, back_ref):
    groups, near_count, rows, cols = parts_ref.shape
    slots = near_count * rows
    total = sum(parts_ref[group].astype(f32) for group in range(groups)).reshape(slots, cols)
    far_count = back_ref.shape[0]
    order = slot_order(far_count.bit_length() - 1, slots)
    ordered = across(order, total.astype(bf16), (0, 0))
    back_ref[...] = fold_rows(ordered, far_count).astype(bf16)


def held_order(own_rows, cols):
    row = lax.broadcasted_iota(jnp.int32, (cols, cols), 0)
    place = lax.broadcasted_iota(jnp.int32, (1, cols), 1).astype(f32)
    block = jnp.floor((place + 0.5) * (1.0 / own_rows))
    far_count = cols // (2 * own_rows)
    core = (block >= far_count).astype(f32)
    source = place + (block - core * far_count + core - core * far_count) * own_rows
    return (row == source.astype(jnp.int32)).astype(f32).astype(bf16)


def weight_block(weight_ref, part, size):
    columns = []
    for block in range(weight_ref.shape[2] // size):
        pair = [weight_ref[core, part, block * size : (block + 1) * size] for core in range(2)]
        columns.append(jnp.concatenate(pair, axis=0))
    return columns


def class_block(weight_ref, order, part, size, cols):
    last = weight_ref.shape[2] // size - 1
    pair = [weight_ref[core, part, last * size :] for core in range(2)]
    both = across(order, jnp.concatenate(pair, axis=0), (1, 0))
    first = 3 * cols - last * LANES
    return both[:, first : first + CLASSES] + both[:, first + CLASSES : first + 2 * CLASSES]


def weight_grad_kernel(
    place_ref, placing_ref, back_ref, mask_ref, features_ref, kept_ref, sent_ref
):
    tiles, positions, channels = features_ref.shape
    cols = mask_ref.shape[1]
    half = cols // 2
    back = jnp.concatenate(unfold_rows(back_ref[...].astype(f32)), axis=1).astype(bf16)
    tile_grads = across(placing_ref[...], back, (0, 0))
    spread = jnp.broadcast_to(tile_grads[:, None, :], (tiles, positions, cols))
    grad_preact = spread.reshape(tiles * positions, cols) * mask_ref[...].astype(f32)
    bias = jnp.sum(grad_preact, axis=0, keepdims=True)
    flattened = features_ref[...].reshape(tiles * positions, channels)
    grad = across(grad_preact.astype(bf16), flattened, (0, 0))
    lanes = channels // kept_ref.shape[0]
    first_core = place_ref[2] == 0
    for out_ref, is_first in ((kept_ref, first_core), (sent_ref, jnp.logical_not(first_core))):
        bias_half = jnp.where(is_first, bias[:, :half], bias[:, half:])
        bias_rows = jnp.broadcast_to(
            jnp.concatenate([bias_half, jnp.zeros((1, lanes - half), f32)], axis=1), (8, lanes)
        )
        for place in range(kept_ref.shape[0]):
            block = grad[:, place * lanes : (place + 1) * lanes]
            picked = jnp.where(is_first, block[:half], block[half:])
            out_ref[place] = jnp.concatenate([picked, bias_rows], axis=0).astype(bf16)


def unpack_kernel(parts_ref, grad_ref, bias_ref):
    cores, plane, _, lanes = parts_ref.shape
    half = grad_ref.shape[0] // cores
    biases = []
    for core in range(cores):
        for place in range(plane):
            block = parts_ref[core, place].astype(f32)
            grad_ref[core * half : (core + 1) * half, place * lanes : (place + 1) * lanes] = block[
                :half
            ]
            if place == 0:
                biases.append(block[half : half + 1, :half])
    bias_ref[...] = jnp.concatenate(biases, axis=1)


def run(kernel, name, out_shape, args, specs, scratch=()):
    vmem = pl.BlockSpec(memory_space=pltpu.VMEM)
    smem = pl.BlockSpec(memory_space=pltpu.SMEM)
    kinds = {"v": vmem, "s": smem, "a": pl.BlockSpec(memory_space=pl.ANY)}
    return pl.pallas_call(
        kernel,
        out_shape=out_shape,
        in_specs=[kinds[spec] for spec in specs],
        out_specs=(vmem,) * len(out_shape),
        scratch_shapes=list(scratch),
        compiler_params=pltpu.CompilerParams(vmem_limit_bytes=(56 if scratch else 40) << 20),
        name=name,
    )(*args)


def on_device(
    features,
    tile_slide,
    tile_pos,
    slide_owner,
    slide_label,
    enc_weight,
    enc_bias,
    norm_gain,
    qkv_weight,
    out_weight,
    cls_weight,
):
    far_count = lax.axis_size(FAR)
    near_count = lax.axis_size(NEAR)
    groups = lax.axis_size("x")
    tile_count, _, channels = features.shape
    cols = enc_weight.shape[1]
    emb = cols * groups
    slot_total = far_count * near_count * SLOTS
    group_at = lax.axis_index("x")
    owner_at = lax.axis_index(ENC)

    shape = jax.ShapeDtypeStruct
    place = jnp.stack([group_at, owner_at, lax.axis_index("c")]).astype(jnp.int32)
    width = 3 * cols + 2 * CLASSES

    with jax.named_scope("encode"):
        own_rows = qkv_weight.shape[0]
        width_blocks = width // LANES
        padded = held_rows(own_rows)
        sources = (
            tile_slide.reshape(1, tile_count),
            tile_pos[None, :],
            slide_owner[None, :],
            qkv_weight,
            out_weight,
            cls_weight.T,
            enc_bias[None, :],
            enc_weight.T,
            features,
        )
        send, mask, placing = run(
            send_kernel,
            "send",
            (
                shape((far_count, 24 + width_blocks * padded, LANES), bf16),
                shape((tile_count * POS, cols), bf16),
                shape((slot_total, tile_count), bf16),
            ),
            (place,) + sources,
            "s" + "a" * len(sources),
            [pltpu.VMEM(source.shape, source.dtype) for source in sources]
            + [pltpu.SemaphoreType.DMA((len(sources),))],
        )

    with jax.named_scope("dispatch"):
        send_near, far_held = run(
            functools.partial(turn_kernel, own_rows),
            "turn",
            (
                shape((groups, near_count, far_count * SLOTS, BLOCK), bf16),
                shape((width_blocks * far_count * own_rows, LANES), bf16),
            ),
            (swap(send, FAR),),
            "v",
        )
        rows = swap(
            send_near.reshape(groups * near_count, far_count * SLOTS, BLOCK), ("x",) + NEAR
        ).reshape(groups, slot_total, BLOCK)

    with jax.named_scope("weights"):
        weights = lax.all_gather(lax.all_gather(far_held, "y", axis=0), "c", axis=0)

    with jax.named_scope("attend"):
        gain = norm_gain.reshape(groups, 1, cols)
        cls_parts = cls_weight.T.reshape(CLASSES, groups, cols).transpose(1, 0, 2)
        part_logits, att, qkv = run(
            functools.partial(forward_kernel, own_rows),
            "forward",
            (
                shape((1, CLASSES), f32),
                shape((cols // HD, slot_total, slot_total), f32),
                shape((slot_total, 3 * cols), bf16),
            ),
            (place, rows, weights, gain, cls_parts),
            "svvvv",
        )
        all_logits = lax.all_gather(part_logits, "x", axis=0)
        logits, grad_parts = run(
            functools.partial(backward_kernel, own_rows),
            "backward",
            (shape((1, CLASSES), f32), shape((groups, slot_total, cols), bf16)),
            (
                place,
                all_logits,
                slide_owner[None, :],
                slide_label[None, :],
                rows,
                weights,
                gain,
                cls_parts,
                att,
                qkv,
            ),
            "svvvvvvvvv",
        )

    with jax.named_scope("give_back"):
        from_near = swap(
            grad_parts.reshape(groups * near_count, far_count * SLOTS, cols), ("x",) + NEAR
        ).reshape(groups, near_count, far_count * SLOTS, cols)
        (folded,) = run(
            fold_kernel, "fold", (shape((far_count, 24, LANES), bf16),), (from_near,), "v"
        )
        back_rows = swap(folded, FAR)

    with jax.named_scope("encoder_grad"):
        plane_count = lax.axis_size(PLANE)
        block = (cols // 2 + 8, channels // plane_count)
        kept, sent = run(
            weight_grad_kernel,
            "weight_grad",
            (shape((plane_count,) + block, bf16),) * 2,
            (place, placing, back_rows, mask, features),
            "svvvv",
        )

    with jax.named_scope("reduce"):
        other = lax.ppermute(sent, "c", [(0, 1), (1, 0)])
        core_sum = (kept.astype(f32) + other.astype(f32)).astype(bf16)
        plane_sum = sum_blocks(core_sum, PLANE)
        total = jnp.sum(gather_copies(plane_sum, "zh").astype(f32), axis=0).astype(bf16)
        all_parts = lax.all_gather(gather_copies(total, PLANE), "c", axis=0)
        enc_grad, bias_grad = run(
            unpack_kernel,
            "unpack",
            (shape((cols, channels), f32), shape((1, cols), f32)),
            (all_parts,),
            "v",
        )
    return (logits, enc_grad.T, bias_grad[0])


def solution(mesh):
    enc_count, groups = mesh.devices.shape
    far_count = enc_count // 8
    far_lanes = 4 if far_count >= 16 else far_count // 2
    shape = (4, far_count // far_lanes, far_lanes, 2, groups)
    split = Mesh(mesh.devices.reshape(shape), ENC + ("x",))
    return jax.shard_map(
        on_device,
        mesh=split,
        in_specs=(
            P(ENC, None, None),
            P(ENC, None),
            P(ENC),
            P(),
            P(),
            P(None, "x"),
            P("x"),
            P(),
            P(ENC, None),
            P(ENC, None),
            P(),
        ),
        out_specs=(P(ENC, None), P(None, "x"), P("x")),
        check_vma=False,
    )
```

time: 264 us -> 185 us (0.70)
  waiting for transfers between devices: 48.1 us -> 1.38 us
  starting transfers between devices: 40.4 us -> 16.4 us
  blocking collectives: 130 us -> 147 us
  between operations: 14.4 us -> 0.77 us
  Pallas kernels: 6.27 us -> 17.9 us
  matrix products: 10.3 us -> 0 us
  local copies, waits for them, and re-layouts: 9.49 us -> 0.34 us
  other arithmetic: 4.69 us -> 0.87 us
    all_to_all x3 -> x6, blocking collectives: 40.8 us -> 112 us  [swap(): return lax.all_to_all(blocks, axes, split_axis=0, concat_axis=0, tiled=True)]
    all_gather x4, blocking collectives: 81.1 us -> 34.6 us  [the longest x2 18.7 us: on_device(): weights = lax.all_gather(lax.all_gather(far_held, 'y', axis=0), 'c', axis=0)]
    all_gather x1 -> x0, waiting for transfers between devices: 30.8 us -> none  [on_device(): all_parts = lax.all_gather(far_all, NEAR, axis=0, tiled=False).astype(f32)]
    all_to_all x2 -> x1, starting transfers between devices: 40.4 us -> 13.3 us  [swap(): return lax.all_to_all(blocks, axes, split_axis=0, concat_axis=0, tiled=True)]
    all_to_all x2 -> x1, waiting for transfers between devices: 17.2 us -> 0.01 us  [swap(): return lax.all_to_all(blocks, axes, split_axis=0, concat_axis=0, tiled=True)]
    pallas_call x2 -> x7, Pallas kernels: 6.27 us -> 17.9 us  [run(): pl.pallas_call(kernel, out_shape=out_shape, in_specs=[kinds[spec] for spe...]
    dot_general x5 -> x0, matrix products: 10.3 us -> none  [the longest x1 5.19 us: on_device(): jnp.dot(flattened, enc_weight, preferred_element_type=f32)]
    psum x1 -> x0, blocking collectives: 8.02 us -> none  [on_device(): logits = lax.psum(part_logits, 'x')]
  transfers between devices with their start and end apart: 3 -> 2, of which waited for: 2 -> 1; matrix products, arithmetic and copies ran while one was open for 1% -> 0% of each run, Pallas kernels for 0% -> 0%
where the time goes in v3:
time: 185 us; the launch traced here: 184 us
  blocking collectives  147 us (79%)
  Pallas kernels  17.9 us (10%)
  starting transfers between devices  16.4 us (9%)
    all_to_all x6, blocking collectives, swap(): return lax.all_to_all(blocks, axes, split_axis=0, concat_axis=0, tiled=True)  112 us
    all_gather x2, blocking collectives, on_device(): weights = lax.all_gather(lax.all_gather(far_held, 'y', axis=0), 'c', axis=0)  18.7 us
    pallas_call x7, Pallas kernels, run(): pl.pallas_call(kernel, out_shape=out_shape, in_specs=[kinds[spec] for spe...  17.9 us
    all_to_all x1, starting transfers between devices, swap(): return lax.all_to_all(blocks, axes, split_axis=0, concat_axis=0, tiled=True)  13.3 us
    all_gather x1, blocking collectives, on_device(): all_logits = lax.all_gather(part_logits, 'x', axis=0)  9.07 us
    all_gather x1, blocking collectives, on_device(): all_parts = lax.all_gather(gather_copies(total, PLANE), 'c', axis=0)  6.78 us
  transfers between devices with their start and end apart: 2, of which 1 were waited for; matrix products, arithmetic and copies ran while one was open for 0% of the time, Pallas kernels for 0%

profile of v3, /device:TPU:1, one launch (start us, length us, event | category | flops | bytes accessed | tf_op | source)
XLA Modules:
  0.0 184.4 jit_solution(10285291250624666717)
XLA Ops:
  0.6 0.7 pad_add_fusion.place_ref
  1.3 5.2 %send.1 = (bf16[16,64,128]{2,1,0:T(8,128)(2,1)}, bf16[576,192]{1,0:T(8,128)(2,1)}, bf16[256,144]{1,0:T(8,128)(2,1)}) custom-call(s32[3]{0:T(128)} %pad_add_fusion.place_ref, s32[1,144]{1,0:T(1,128)} %bitcast.40, s32[1,144]{1,0:T(1,128)} %bitcast.41, s32[1,128]{1,0:T(1,128)} %bitcast.32, bf16[6,2304]{1,0:T(8,128)(2,1)} %refs_3_.1, bf16[6,768]{1,0:T(8,128)(2,1)} %refs_4_.1, ...), custom_call_target="tpu_custom_call" | custom-call | tf_op jit(solution)/shard_map/encode/send/pallas_call | solution.py:410
  6.5 28.9 %all_to_all.35.received_ref = bf16[16,64,128]{2,1,0:T(8,128)(2,1)S(1)} all-to-all(bf16[16,64,128]{2,1,0:T(8,128)(2,1)} %get-tuple-element.17), channel_id=1, replica_groups=mesh['y'=4,'zh'=4,'zl'=4,'c'=2,'x'=4] {'zh','zl'}, dimensions={0} | all-to-all | bytes 524288 | tf_op jit(solution)/shard_map/dispatch/all_to_all | solution.py:35
  35.4 1.1 turn.1
  36.6 13.3 %all-to-all-start.1 = ((bf16[32,32,256]{2,1,0:T(8,128)(2,1)}), bf16[32,32,256]{2,1,0:T(8,128)(2,1)S(1)}, u32[]{:S(2)}, u32[]{:S(2)}) async-start(bf16[32,32,256]{2,1,0:T(8,128)(2,1)} %bitcast.9), calls=%async_computation.1 | async-start | bytes 1048576 | tf_op jit(solution)/shard_map/dispatch/all_to_all | solution.py:35
  49.9 0.1 reshape.33
  50.0 0.1 reshape.32.gain_ref
  50.1 14.1 %all-gather = bf16[1920,128]{1,0:T(8,128)(2,1)S(1)} all-gather(bf16[480,128]{1,0:T(8,128)(2,1)S(1)} %get-tuple-element.19), channel_id=2, replica_groups=mesh['y'=4,'zh'=4,'zl'=4,'c'=2,'x'=4] {'y'}, dimensions={0}, use_global_device_ids=true | all-gather | bytes 614400 | tf_op jit(solution)/shard_map/weights/all_gather | solution.py:493
  64.2 4.7 %all-gather.1 = bf16[8,480,128]{2,1,0:T(8,128)(2,1)S(1)} all-gather(bf16[4,480,128]{2,1,0:T(8,128)(2,1)S(1)} %bitcast.36), channel_id=3, replica_groups=mesh['y'=4,'zh'=4,'zl'=4,'c'=2,'x'=4] {'c'}, dimensions={0}, use_global_device_ids=true | all-gather | bytes 1474560 | tf_op jit(solution)/shard_map/weights/all_gather | solution.py:493
  68.9 3.6 %forward.1 = (f32[1,32]{1,0:T(1,128)S(1)}, f32[3,256,256]{2,1,0:T(8,128)S(1)}, bf16[256,576]{1,0:T(8,128)(2,1)S(1)}) custom-call(s32[3]{0:T(128)S(1)} %copy-done.3, bf16[4,256,256]{2,1,0:T(8,128)(2,1)S(1)} %bitcast.25, bf16[2,4,480,128]{3,2,1,0:T(8,128)(2,1)S(1)} %bitcast.23, f32[4,1,192]{2,1,0:T(1,128)S(1)} %reshape.32.gain_ref, f32[4,32,192]{2,1,0:T(8,128)S(1)} %bitcast.29), custom_call_target="tpu_custom_call" | custom-call | tf_op jit(solution)/shard_map/attend/forward/pallas_call | solution.py:410
  72.5 9.1 %all-gather.4.part_logits_ref = f32[4,1,32]{2,1,0:T(1,128)S(1)} all-gather(f32[1,1,32]{2,1,0:T(1,128)S(1)} %bitcast.35), channel_id=4, replica_groups=mesh['y'=4,'zh'=4,'zl'=4,'c'=2,'x'=4] {'x'}, dimensions={0}, use_global_device_ids=true | all-gather | bytes 640 | tf_op jit(solution)/shard_map/attend/all_gather | solution.py:509
  81.6 4.5 %backward.1 = (f32[1,32]{1,0:T(1,128)}, bf16[4,256,192]{2,1,0:T(8,128)(2,1)S(1)}) custom-call(s32[3]{0:T(128)S(1)} %copy-done.3, f32[4,1,32]{2,1,0:T(1,128)S(1)} %all-gather.4.part_logits_ref, s32[1,128]{1,0:T(1,128)S(1)} %bitcast.33, s32[1,128]{1,0:T(1,128)S(1)} %bitcast.34, bf16[4,256,256]{2,1,0:T(8,128)(2,1)S(1)} %bitcast.26, ...), custom_call_target="tpu_custom_call" | custom-call | tf_op jit(solution)/shard_map/attend/backward/pallas_call | solution.py:410
  86.1 17.0 %all_to_all.36 = bf16[32,32,192]{2,1,0:T(8,128)(2,1)S(1)} all-to-all(bf16[32,32,192]{2,1,0:T(8,128)(2,1)S(1)} %bitcast.31), channel_id=1, replica_groups=mesh['y'=4,'zh'=4,'zl'=4,'c'=2,'x'=4] {'x','y','c'}, dimensions={0} | all-to-all | bytes 786432 | tf_op jit(solution)/shard_map/give_back/all_to_all | solution.py:35
  103.1 0.3 fold.1
  103.5 17.7 %all_to_all.37.back_ref = bf16[16,24,128]{2,1,0:T(8,128)(2,1)S(1)} all-to-all(bf16[16,24,128]{2,1,0:T(8,128)(2,1)S(1)} %fold.1), channel_id=1, replica_groups=mesh['y'=4,'zh'=4,'zl'=4,'c'=2,'x'=4] {'zh','zl'}, dimensions={0} | all-to-all | bytes 196608 | tf_op jit(solution)/shard_map/give_back/all_to_all | solution.py:35
  121.2 1.7 weight_grad.1
  122.9 3.1 %collective-permute-start = (bf16[16,104,128]{2,1,0:T(8,128)(2,1)S(1)}, bf16[16,104,128]{2,1,0:T(8,128)(2,1)S(1)}, u32[]{:S(2)}, u32[]{:S(2)}) collective-permute-start(bf16[16,104,128]{2,1,0:T(8,128)(2,1)S(1)} %get-tuple-element.28), channel_id=1, source_target_pairs={{0,4},{4,0},{1,5},{5,1},{2,6},{6,2},{3,7},{7,3},{8,12},{12,8},{9,1... | collective-permute-start | bytes 1277960 | tf_op jit(solution)/shard_map/reduce/ppermute | solution.py:550
  126.0 1.4 collective-permute-done
  127.4 0.1 add_convert_fusion
  127.5 18.1 %all_to_all.38 = bf16[16,104,128]{2,1,0:T(8,128)(2,1)S(1)} all-to-all(bf16[16,104,128]{2,1,0:T(8,128)(2,1)S(1)} %add_convert_fusion), channel_id=1, replica_groups=mesh['y'=4,'zh'=4,'zl'=4,'c'=2,'x'=4] {'y','zl'}, dimensions={0} | all-to-all | bytes 851968 | tf_op jit(solution)/shard_map/reduce/all_to_all | solution.py:35
  145.7 16.3 %all_to_all.39 = bf16[4,104,128]{2,1,0:T(8,128)(2,1)S(1)} all-to-all(bf16[4,104,128]{2,1,0:T(8,128)(2,1)S(1)} %broadcast_in_dim.29), channel_id=1, replica_groups=mesh['y'=4,'zh'=4,'zl'=4,'c'=2,'x'=4] {'zh'}, dimensions={0} | all-to-all | bytes 212992 | tf_op jit(solution)/shard_map/reduce/all_to_all | solution.py:35
  162.1 14.2 %all_to_all.40 = bf16[16,104,128]{2,1,0:T(8,128)(2,1)S(1)} all-to-all(bf16[16,104,128]{2,1,0:T(8,128)(2,1)S(1)} %broadcast_in_dim.30), channel_id=1, replica_groups=mesh['y'=4,'zh'=4,'zl'=4,'c'=2,'x'=4] {'y','zl'}, dimensions={0} | all-to-all | bytes 851968 | tf_op jit(solution)/shard_map/reduce/all_to_all | solution.py:35
  176.4 6.8 %all-gather.3 = bf16[32,104,128]{2,1,0:T(8,128)(2,1)S(1)} all-gather(bf16[16,104,128]{2,1,0:T(8,128)(2,1)S(1)} %all_to_all.40), channel_id=5, replica_groups=mesh['y'=4,'zh'=4,'zl'=4,'c'=2,'x'=4] {'c'}, dimensions={0}, use_global_device_ids=true | all-gather | bytes 1277952 | tf_op jit(solution)/shard_map/reduce/all_gather | solution.py:554
  183.1 1.3 unpack.1
  (22 shorter events, 0.2 us)
Async XLA Ops:
  1.3 48.5 %copy-start.6 = (f32[768,32]{0,1:T(8,128)S(1)}, f32[768,32]{0,1:T(8,128)}, u32[]{:S(2)}) copy-start(f32[768,32]{0,1:T(8,128)} %param.21) | copy-start | bytes 294916
  1.3 48.7 %copy-start.7 = (f32[768]{0:T(1024)S(1)}, f32[768]{0:T(1024)}, u32[]{:S(2)}) copy-start(f32[768]{0:T(1024)} %param.18) | copy-start | bytes 9220
  6.5 62.3 %copy-start.3 = (s32[3]{0:T(128)S(1)}, s32[3]{0:T(128)}, u32[]{:S(2)}) copy-start(s32[3]{0:T(128)} %pad_add_fusion.place_ref) | copy-start | bytes 40
  36.6 32.3 %all-to-all-start.1 = ((bf16[32,32,256]{2,1,0:T(8,128)(2,1)}), bf16[32,32,256]{2,1,0:T(8,128)(2,1)S(1)}, u32[]{:S(2)}, u32[]{:S(2)}) async-start(bf16[32,32,256]{2,1,0:T(8,128)(2,1)} %bitcast.9), calls=%async_computation.1 | async-start | bytes 1048576 | tf_op jit(solution)/shard_map/dispatch/all_to_all | solution.py:35
  49.8 31.7 %copy-start.4 = (s32[128]{0:T(128)S(1)}, s32[128]{0:T(128)}, u32[]{:S(2)}) copy-start(s32[128]{0:T(128)} %param.14) | copy-start | bytes 1540
  49.9 31.7 %copy-start.5 = (s32[128]{0:T(128)S(1)}, s32[128]{0:T(128)}, u32[]{:S(2)}) copy-start(s32[128]{0:T(128)} %param.15) | copy-start | bytes 1540
  72.5 48.7 %copy-start = (bf16[144,4,2048]{2,1,0:T(4,128)(2,1)S(1)}, bf16[144,4,2048]{2,1,0:T(4,128)(2,1)}, u32[]{:S(2)}) copy-start(bf16[144,4,2048]{2,1,0:T(4,128)(2,1)} %features_ref.1) | copy-start | bytes 7077892
  72.5 48.7 %copy-start.1 = (bf16[576,192]{1,0:T(8,128)(2,1)S(1)}, bf16[576,192]{1,0:T(8,128)(2,1)}, u32[]{:S(2)}) copy-start(bf16[576,192]{1,0:T(8,128)(2,1)} %get-tuple-element.26.mask_ref) | copy-start | bytes 663556
  72.5 48.7 %copy-start.2 = (bf16[256,144]{1,0:T(8,128)(2,1)S(1)}, bf16[256,144]{1,0:T(8,128)(2,1)}, u32[]{:S(2)}) copy-start(bf16[256,144]{1,0:T(8,128)(2,1)} %get-tuple-element.24.placing_ref) | copy-start | bytes 221188
  122.9 4.5 %collective-permute-start = (bf16[16,104,128]{2,1,0:T(8,128)(2,1)S(1)}, bf16[16,104,128]{2,1,0:T(8,128)(2,1)S(1)}, u32[]{:S(2)}, u32[]{:S(2)}) collective-permute-start(bf16[16,104,128]{2,1,0:T(8,128)(2,1)S(1)} %get-tuple-element.28), channel_id=1, source_target_pairs={{0,4},{4,0},{1,5},{5,1},{2,6},{6,2},{3,7},{7,3},{8,12},{12,8},{9,1... | collective-permute-start | bytes 1277960 | tf_op jit(solution)/shard_map/reduce/ppermute | solution.py:550

commit v4 on v3

--- a/solution.py
+++ b/solution.py
@@ -43,8 +43,11 @@
     return jnp.sum(swap(blocks, axes).astype(f32), axis=0).astype(bf16)
 
 
-def normed_parts(rows_ref, cols):
-    parts = [rows_ref[part, :, :cols].astype(f32) for part in range(rows_ref.shape[0])]
+def normed_parts(place_ref, rows_ref, cols):
+    parts = [
+        rows_ref[part_of(place_ref, step), :, :cols].astype(f32)
+        for step in range(rows_ref.shape[0])
+    ]
     width = cols * len(parts)
     mean = sum(jnp.sum(part, axis=1, keepdims=True) for part in parts) / width
     centred = [part - mean for part in parts]
@@ -54,18 +57,27 @@
 
 
 def forward_kernel(
-    own_rows, place_ref, rows_ref, weight_ref, gain_ref, cls_ref, logits_ref, att_ref, qkv_ref
+    own_rows,
+    place_ref,
+    rows_ref,
+    weight_ref,
+    gain_ref,
+    cls_ref,
+    logits_ref,
+    att_ref,
+    qkv_ref,
+    weights_ref,
 ):
     groups, slots, _ = rows_ref.shape
     cols = gain_ref.shape[2]
-    parts, normed, _ = normed_parts(rows_ref, cols)
+    parts, normed, _ = normed_parts(place_ref, rows_ref, cols)
     size = weight_ref.shape[2] // (-(-(3 * cols + 2 * CLASSES) // LANES))
     order = held_order(own_rows, cols)
     qkv = 0.0
-    for part in range(groups):
-        normed_in = (normed[part] * gain_ref[part]).astype(bf16)
-        normed_in = across(normed_in, order, (1, 0)).astype(bf16)
-        block = jnp.concatenate(weight_block(weight_ref, part, size), axis=1)
+    for step in range(groups):
+        normed_in = (normed[step] * gain_ref[part_of(place_ref, step)]).astype(bf16)
+        block = across(order, weight_block(weight_ref, step, size), (1, 0)).astype(bf16)
+        weights_ref[step] = block
         qkv = qkv + across(normed_in, block, (1, 0))
     qkv = qkv[:, : 3 * cols]
     column = lax.broadcasted_iota(jnp.int32, (slots, 3 * cols), 1)
@@ -80,8 +92,8 @@
     tag_row = jnp.sum(jnp.where(down == along, tags, 0.0), axis=0, keepdims=True)
     query_pos = tags.astype(jnp.int32) - 1
     key_pos = tag_row.astype(jnp.int32) - 1
-    wc = class_block(weight_ref, order, place_ref[0], size, cols)
-    total = jnp.zeros((1, CLASSES), f32)
+    wc = class_block(weights_ref, place_ref, cols)
+    mixed = []
     for head in range(cols // HD):
         group = head % 3
         low = (1 << group) - 1
@@ -101,23 +113,23 @@
         att = weights / jnp.where(row_total > 0, row_total, 1.0)
         att_ref[head] = att
         att_total = jnp.sum(att.astype(bf16).astype(f32), axis=0, keepdims=True)
-        values = qkv[:, 2 * cols + first : 2 * cols + first + HD].astype(f32)
-        mixed_total = across(att_total, values, (1, 0), EXACT)
-        total = total + across(mixed_total, wc[first : first + HD], (1, 0), EXACT)
-    for part in range(groups):
-        row_sum = jnp.sum(parts[part], axis=0, keepdims=True) * (1.0 / groups)
-        total = total + across(row_sum, cls_ref[part], (1, 1), EXACT)
+        values = qkv[:, 2 * cols + first : 2 * cols + first + HD]
+        mixed.append(across(in_terms(att_total), values, (1, 0)))
+    mixed_total = jnp.sum(jnp.concatenate(mixed, axis=1), axis=0, keepdims=True)
+    total = across(mixed_total, wc, (1, 0), EXACT)
+    for step in range(groups):
+        row_sum = jnp.sum(parts[step], axis=0, keepdims=True) * (1.0 / groups)
+        total = total + across(row_sum, cls_ref[part_of(place_ref, step)], (1, 1), EXACT)
     logits_ref[...] = total / count
 
 
 def backward_kernel(
-    own_rows,
     place_ref,
     part_logits_ref,
     owner_ref,
     label_ref,
     rows_ref,
-    weight_ref,
+    weights_ref,
     gain_ref,
     cls_ref,
     att_ref,
@@ -127,7 +139,7 @@
 ):
     groups, slots, _ = rows_ref.shape
     cols = gain_ref.shape[2]
-    _, normed, inv_std = normed_parts(rows_ref, cols)
+    _, normed, inv_std = normed_parts(place_ref, rows_ref, cols)
     tags = rows_ref[0, :, cols : cols + 1].astype(f32)
     live = (tags > 0).astype(f32)
     count = jnp.sum(live, axis=0, keepdims=True)
@@ -139,9 +151,7 @@
     my_label = jnp.sum(jnp.where(mine, label_ref[...], 0).astype(f32), axis=1, keepdims=True)
     class_ids = lax.broadcasted_iota(jnp.int32, (1, CLASSES), 1).astype(f32)
     grad_logits = (class_probs - (class_ids == my_label).astype(f32)) / count
-    size = weight_ref.shape[2] // (-(-(3 * cols + 2 * CLASSES) // LANES))
-    order = held_order(own_rows, cols)
-    wc = class_block(weight_ref, order, place_ref[0], size, cols)
+    wc = class_block(weights_ref, place_ref, cols)
     grad_mixed = across(grad_logits, wc, (1, 1), EXACT).astype(bf16)
     qkv = qkv_ref[...]
     grad_q, grad_k, grad_v = [], [], []
@@ -162,22 +172,19 @@
     unused = jnp.zeros((slots, 2 * CLASSES), f32)
     grad_qkv = jnp.concatenate(grad_q + grad_k + grad_v + [unused], axis=1).astype(bf16)
     scaled_parts = []
-    for part in range(groups):
-        block = jnp.concatenate(weight_block(weight_ref, part, size), axis=1)
-        grad_normed = across(grad_qkv, block, (1, 1))
-        high = grad_normed.astype(bf16)
-        low = (grad_normed - high.astype(f32)).astype(bf16)
-        grad_normed = across(high, order, (1, 1)) + across(low, order, (1, 1))
-        scaled_parts.append(grad_normed * gain_ref[part])
+    for step in range(groups):
+        grad_normed = across(grad_qkv, weights_ref[step], (1, 1))
+        scaled_parts.append(grad_normed * gain_ref[part_of(place_ref, step)])
     width = cols * groups
     mean = sum(jnp.sum(e, axis=1, keepdims=True) for e in scaled_parts) / width
     slope = (
         sum(jnp.sum(e * n, axis=1, keepdims=True) for e, n in zip(scaled_parts, normed)) / width
     )
-    for part in range(groups):
+    for step in range(groups):
+        part = part_of(place_ref, step)
         pooled = across(grad_logits, cls_ref[part], (1, 0), EXACT) * (1.0 / groups)
-        grad = inv_std * (scaled_parts[part] - mean - normed[part] * slope)
-        grad_ref[part] = (live * pooled + grad).astype(bf16)
+        grad = inv_std * (scaled_parts[step] - mean - normed[step] * slope)
+        grad_ref[part] = fold_rows(live * pooled + grad, grad_ref.shape[1]).astype(bf16)
 
 
 def as_column(row):
@@ -187,22 +194,32 @@
     return jnp.sum(jnp.where(down == along, row, 0.0), axis=1, keepdims=True)
 
 
-def held_rows(rows):
-    return (rows + 8) // 8 * 8
+def in_terms(row):
+    high = row.astype(bf16)
+    rest = row - high.astype(f32)
+    middle = rest.astype(bf16)
+    low = (rest - middle.astype(f32)).astype(bf16)
+    terms = [term.astype(f32) for term in (high, middle, low)]
+    return jnp.concatenate(terms + [jnp.zeros((5, row.shape[1]), f32)], axis=0).astype(bf16)
+
+
+def held_rows(blocks, rows):
+    return (blocks * rows + 8) // 8 * 8
 
 
 def fold_rows(rows, count):
-    blocks = rows.reshape(count, 2 * 8, rows.shape[1])
-    rest = jnp.concatenate([blocks[:, :8, LANES:], blocks[:, 8:, LANES:]], axis=2)
+    blocks = rows.reshape(count, rows.shape[0] // count, rows.shape[1])
+    half = blocks.shape[1] // 2
+    rest = jnp.concatenate([blocks[:, :half, LANES:], blocks[:, half:, LANES:]], axis=2)
     return jnp.concatenate([blocks[:, :, :LANES], rest], axis=1)
 
 
-def unfold_rows(blocks):
-    rest = blocks[:, 16:24]
+def unfold_rows(blocks, size):
+    rest = blocks[:, size : size + size // 2]
     half = LANES // 2
     rest = jnp.concatenate([rest[:, :, :half], rest[:, :, half:]], axis=1)
-    size = blocks.shape[0] * 16
-    return blocks[:, :16].reshape(size, LANES), rest.reshape(size, half)
+    total = blocks.shape[0] * size
+    return blocks[:, :size].reshape(total, LANES), rest.reshape(total, half)
 
 
 def slot_order(far_bits, slots):
@@ -225,7 +242,7 @@
         copy.start()
     slide_ref, pos_ref, owner_ref, qkv_ref, out_ref, cls_ref = targets[:6]
     bias_ref, weight_ref, features_ref = targets[6:]
-    for copy in copies[:6]:
+    for copy in copies:
         copy.wait()
     tiles, positions, channels = features_ref.shape
     far_count = send_ref.shape[0]
@@ -271,13 +288,11 @@
             block = jnp.where(place_ref[0] == group, qkv_ref[:, first : first + cols], block)
         picked.append(block.astype(f32))
     rows = jnp.concatenate(picked + [wc_high, wc - wc_high], axis=1)
-    padded = held_rows(own_rows)
-    rows = jnp.concatenate([rows, jnp.zeros((padded - own_rows, rows.shape[1]), f32)], axis=0)
     held = [rows[:, at : at + LANES] for at in range(0, rows.shape[1], LANES)]
-    is_tag = lax.broadcasted_iota(jnp.int32, (padded, LANES), 0) == own_rows
-
-    for copy in copies[6:]:
-        copy.wait()
+    tag_at = len(held) * own_rows
+    padded = held_rows(len(held), own_rows)
+    held = jnp.concatenate(held + [jnp.zeros((padded - tag_at, LANES), f32)], axis=0)
+    is_tag = lax.broadcasted_iota(jnp.int32, (padded, LANES), 0) == tag_at
     flattened = features_ref[...].reshape(tiles * positions, channels)
     preact = across(flattened, weight_ref[...], (1, 1)) + bias_ref[...]
     mask_ref[...] = jnp.where(preact > 0, 1.0 / positions, 0.0).astype(bf16)
@@ -285,8 +300,8 @@
     tile_rows = (summed * (1.0 / positions)).astype(bf16)
     blocks = fold_rows(across(placing, tile_rows, (1, 0)), far_count)
     for far in range(far_count):
-        first = jnp.where(is_tag, tag_rows[far : far + 1], held[0])
-        send_ref[far] = jnp.concatenate([blocks[far], first] + held[1:], axis=0).astype(bf16)
+        rest = jnp.where(is_tag, tag_rows[far : far + 1], held)
+        send_ref[far] = jnp.concatenate([blocks[far], rest], axis=0).astype(bf16)
 
 
 def turn_kernel(own_rows, received_ref, rows_ref, held_ref):
@@ -295,13 +310,15 @@
     far_bits = far_count.bit_length() - 1
     received = received_ref[...].astype(f32)
     order = slot_order(far_bits, slots)
-    wide, narrow = unfold_rows(received)
+    wide, narrow = unfold_rows(received, 16)
     wide = across(order, wide.astype(bf16), (1, 0))
     narrow = across(order, narrow.astype(bf16), (1, 0))
     slot = lax.broadcasted_iota(jnp.int32, (slots, far_count), 0)
     far = lax.broadcasted_iota(jnp.int32, (slots, far_count), 1)
     from_far = (((slot >> 1) & (far_count - 1)) == far).astype(f32).astype(bf16)
-    tag_rows = received[:, 24 + own_rows].astype(bf16)
+    size = far_count * own_rows
+    block_count = held_ref.shape[0] // size
+    tag_rows = received[:, 24 + block_count * own_rows].astype(bf16)
     slot = lax.broadcasted_iota(jnp.int32, (slots, LANES), 0)
     lane = lax.broadcasted_iota(jnp.int32, (slots, LANES), 1)
     mine = lane == (slot >> (far_bits + 1)) * 2 + (slot & 1)
@@ -313,27 +330,25 @@
     rows = rows.reshape(rows_ref.shape[1:])
     for group in range(rows_ref.shape[0]):
         rows_ref[group] = rows
-    padded = held_rows(own_rows)
-    size = far_count * own_rows
+    padded = received.shape[1] - 24
+    held = received[:, 24:].reshape(far_count * padded, LANES).astype(bf16)
     row = lax.broadcasted_iota(jnp.int32, (size, 1), 0).astype(f32)
     column = lax.broadcasted_iota(jnp.int32, (size, far_count * padded), 1)
     far = jnp.floor((row + 0.5) * (1.0 / own_rows))
-    kept = (column == (row + far * (padded - own_rows)).astype(jnp.int32)).astype(f32).astype(bf16)
-    for block in range(held_ref.shape[0] // size):
-        first = 24 + block * padded
-        held = received[:, first : first + padded].reshape(far_count * padded, LANES)
-        held = across(kept, held.astype(bf16), (1, 0))
-        held_ref[block * size : (block + 1) * size] = held.astype(bf16)
+    source = (row + far * (padded - own_rows)).astype(jnp.int32)
+    for block in range(block_count):
+        kept = (column == source + block * own_rows).astype(f32).astype(bf16)
+        held_ref[block * size : (block + 1) * size] = across(kept, held, (1, 0)).astype(bf16)
 
 
 def fold_kernel(parts_ref, back_ref):
-    groups, near_count, rows, cols = parts_ref.shape
-    slots = near_count * rows
-    total = sum(parts_ref[group].astype(f32) for group in range(groups)).reshape(slots, cols)
+    groups = parts_ref.shape[0]
     far_count = back_ref.shape[0]
-    order = slot_order(far_count.bit_length() - 1, slots)
-    ordered = across(order, total.astype(bf16), (0, 0))
-    back_ref[...] = fold_rows(ordered, far_count).astype(bf16)
+    total = sum(parts_ref[group].astype(f32) for group in range(groups))
+    wide, narrow = unfold_rows(total, far_count * SLOTS)
+    total = jnp.concatenate([wide, narrow], axis=1).astype(bf16)
+    order = slot_order(far_count.bit_length() - 1, total.shape[0])
+    back_ref[...] = fold_rows(across(order, total, (0, 0)), far_count).astype(bf16)
 
 
 def held_order(own_rows, cols):
@@ -346,20 +361,22 @@
     return (row == source.astype(jnp.int32)).astype(f32).astype(bf16)
 
 
-def weight_block(weight_ref, part, size):
+def weight_block(weight_ref, step, size):
     columns = []
     for block in range(weight_ref.shape[2] // size):
-        pair = [weight_ref[core, part, block * size : (block + 1) * size] for core in range(2)]
+        pair = [weight_ref[core, step, block * size : (block + 1) * size] for core in range(2)]
         columns.append(jnp.concatenate(pair, axis=0))
-    return columns
-
-
-def class_block(weight_ref, order, part, size, cols):
-    last = weight_ref.shape[2] // size - 1
-    pair = [weight_ref[core, part, last * size :] for core in range(2)]
-    both = across(order, jnp.concatenate(pair, axis=0), (1, 0))
-    first = 3 * cols - last * LANES
-    return both[:, first : first + CLASSES] + both[:, first + CLASSES : first + 2 * CLASSES]
+    return jnp.concatenate(columns, axis=1)
+
+
+def part_of(place_ref, step):
+    return place_ref[3] ^ step
+
+
+def class_block(weights_ref, place_ref, cols):
+    mine = weights_ref[place_ref[3] ^ place_ref[0]]
+    both = mine[:, 3 * cols :].astype(f32)
+    return both[:, :CLASSES] + both[:, CLASSES : 2 * CLASSES]
 
 
 def weight_grad_kernel(
@@ -368,7 +385,7 @@
     tiles, positions, channels = features_ref.shape
     cols = mask_ref.shape[1]
     half = cols // 2
-    back = jnp.concatenate(unfold_rows(back_ref[...].astype(f32)), axis=1).astype(bf16)
+    back = jnp.concatenate(unfold_rows(back_ref[...].astype(f32), 16), axis=1).astype(bf16)
     tile_grads = across(placing_ref[...], back, (0, 0))
     spread = jnp.broadcast_to(tile_grads[:, None, :], (tiles, positions, cols))
     grad_preact = spread.reshape(tiles * positions, cols) * mask_ref[...].astype(f32)
@@ -442,13 +459,14 @@
     owner_at = lax.axis_index(ENC)
 
     shape = jax.ShapeDtypeStruct
-    place = jnp.stack([group_at, owner_at, lax.axis_index("c")]).astype(jnp.int32)
+    place = jnp.stack([group_at, owner_at, lax.axis_index("c"), lax.axis_index("y")]).astype(
+        jnp.int32
+    )
     width = 3 * cols + 2 * CLASSES
 
     with jax.named_scope("encode"):
         own_rows = qkv_weight.shape[0]
         width_blocks = width // LANES
-        padded = held_rows(own_rows)
         sources = (
             tile_slide.reshape(1, tile_count),
             tile_pos[None, :],
@@ -464,7 +482,7 @@
             send_kernel,
             "send",
             (
-                shape((far_count, 24 + width_blocks * padded, LANES), bf16),
+                shape((far_count, 24 + held_rows(width_blocks, own_rows), LANES), bf16),
                 shape((tile_count * POS, cols), bf16),
                 shape((slot_total, tile_count), bf16),
             ),
@@ -490,34 +508,41 @@
         ).reshape(groups, slot_total, BLOCK)
 
     with jax.named_scope("weights"):
-        weights = lax.all_gather(lax.all_gather(far_held, "y", axis=0), "c", axis=0)
+        steps = [
+            lax.ppermute(far_held, "y", [(at, at ^ step) for at in range(4)]) for step in range(1, 4)
+        ]
+        weights = lax.all_gather(jnp.stack([far_held] + steps), "c", axis=0)
 
     with jax.named_scope("attend"):
         gain = norm_gain.reshape(groups, 1, cols)
         cls_parts = cls_weight.T.reshape(CLASSES, groups, cols).transpose(1, 0, 2)
-        part_logits, att, qkv = run(
+        part_logits, att, qkv, ordered = run(
             functools.partial(forward_kernel, own_rows),
             "forward",
             (
                 shape((1, CLASSES), f32),
                 shape((cols // HD, slot_total, slot_total), f32),
                 shape((slot_total, 3 * cols), bf16),
+                shape((groups, cols, width), bf16),
             ),
             (place, rows, weights, gain, cls_parts),
             "svvvv",
         )
         all_logits = lax.all_gather(part_logits, "x", axis=0)
         logits, grad_parts = run(
-            functools.partial(backward_kernel, own_rows),
+            backward_kernel,
             "backward",
-            (shape((1, CLASSES), f32), shape((groups, slot_total, cols), bf16)),
+            (
+                shape((1, CLASSES), f32),
+                shape((groups, near_count, far_count * SLOTS * 3 // 2, LANES), bf16),
+            ),
             (
                 place,
                 all_logits,
                 slide_owner[None, :],
                 slide_label[None, :],
                 rows,
-                weights,
+                ordered,
                 gain,
                 cls_parts,
                 att,
@@ -528,8 +553,8 @@
 
     with jax.named_scope("give_back"):
         from_near = swap(
-            grad_parts.reshape(groups * near_count, far_count * SLOTS, cols), ("x",) + NEAR
-        ).reshape(groups, near_count, far_count * SLOTS, cols)
+            grad_parts.reshape((groups * near_count,) + grad_parts.shape[2:]), ("x",) + NEAR
+        ).reshape(grad_parts.shape)
         (folded,) = run(
             fold_kernel, "fold", (shape((far_count, 24, LANES), bf16),), (from_near,), "v"
         )

time: 185 us -> 179 us (0.968)
  blocking collectives: 147 us -> 127 us
  starting transfers between devices: 16.4 us -> 25.2 us
  waiting for transfers between devices: 1.38 us -> 6.93 us
    all_gather x2 -> x1, blocking collectives: 18.7 us -> 2.84 us  [on_device(): weights = lax.all_gather(jnp.stack([far_held] + steps), 'c', axis=0)]
    ppermute x0 -> x3, starting transfers between devices: none -> 8.98 us  [on_device(): lax.ppermute(far_held, 'y', [(at, at ^ step) for at in range(4)])]
    ppermute x0 -> x3, waiting for transfers between devices: none -> 5.55 us  [on_device(): lax.ppermute(far_held, 'y', [(at, at ^ step) for at in range(4)])]
    all_to_all x6, blocking collectives: 112 us -> 110 us  [swap(): return lax.all_to_all(blocks, axes, split_axis=0, concat_axis=0, tiled=True)]
  transfers between devices with their start and end apart: 2 -> 5, of which waited for: 1 -> 2; matrix products, arithmetic and copies ran while one was open for 0% -> 0% of each run, Pallas kernels for 0% -> 0%
where the time goes in v4:
time: 179 us; the launch traced here: 178 us
  blocking collectives  127 us (71%)
  starting transfers between devices  25.2 us (14%)
  Pallas kernels  16.7 us (9%)
  waiting for transfers between devices  6.93 us (4%)
    all_to_all x6, blocking collectives, swap(): return lax.all_to_all(blocks, axes, split_axis=0, concat_axis=0, tiled=True)  110 us
    pallas_call x7, Pallas kernels, run(): pl.pallas_call(kernel, out_shape=out_shape, in_specs=[kinds[spec] for spe...  16.7 us
    all_to_all x1, starting transfers between devices, swap(): return lax.all_to_all(blocks, axes, split_axis=0, concat_axis=0, tiled=True)  12.7 us
    ppermute x3, starting transfers between devices, on_device(): lax.ppermute(far_held, 'y', [(at, at ^ step) for at in range(4)])  8.98 us
    all_gather x1, blocking collectives, on_device(): all_logits = lax.all_gather(part_logits, 'x', axis=0)  7.57 us
    all_gather x1, blocking collectives, on_device(): all_parts = lax.all_gather(gather_copies(total, PLANE), 'c', axis=0)  6.78 us
    ppermute x3, waiting for transfers between devices, on_device(): lax.ppermute(far_held, 'y', [(at, at ^ step) for at in range(4)])  5.55 us
    ppermute x1, starting transfers between devices, on_device(): other = lax.ppermute(sent, 'c', [(0, 1), (1, 0)])  3.6 us
  transfers between devices with their start and end apart: 5, of which 2 were waited for; matrix products, arithmetic and copies ran while one was open for 0% of the time, Pallas kernels for 0%

profile of v4, /device:TPU:1, one launch (start us, length us, event | category | flops | bytes accessed | tf_op | source)
XLA Modules:
  0.0 178.3 jit_solution(10362339278081821160)
XLA Ops:
  0.6 0.6 pad_add_fusion.place_ref
  1.3 5.3 %send.1 = (bf16[16,56,128]{2,1,0:T(8,128)(2,1)}, bf16[576,192]{1,0:T(8,128)(2,1)}, bf16[256,144]{1,0:T(8,128)(2,1)}) custom-call(s32[4]{0:T(128)} %pad_add_fusion.place_ref, s32[1,144]{1,0:T(1,128)} %bitcast.46, s32[1,144]{1,0:T(1,128)} %bitcast.47, s32[1,128]{1,0:T(1,128)} %bitcast.36, bf16[6,2304]{1,0:T(8,128)(2,1)} %refs_3_.1, bf16[6,768]{1,0:T(8,128)(2,1)} %refs_4_.1, ...), custom_call_target="tpu_custom_call" | custom-call | tf_op jit(solution)/shard_map/encode/send/pallas_call | solution.py:427
  6.6 28.5 %all_to_all.35.received_ref = bf16[16,56,128]{2,1,0:T(8,128)(2,1)S(1)} all-to-all(bf16[16,56,128]{2,1,0:T(8,128)(2,1)} %get-tuple-element.18), channel_id=1, replica_groups=mesh['y'=4,'zh'=4,'zl'=4,'c'=2,'x'=4] {'zh','zl'}, dimensions={0} | all-to-all | bytes 458752 | tf_op jit(solution)/shard_map/dispatch/all_to_all | solution.py:35
  35.1 1.2 turn.1
  36.2 12.7 %all-to-all-start.1 = ((bf16[32,32,256]{2,1,0:T(8,128)(2,1)}), bf16[32,32,256]{2,1,0:T(8,128)(2,1)S(1)}, u32[]{:S(2)}, u32[]{:S(2)}) async-start(bf16[32,32,256]{2,1,0:T(8,128)(2,1)} %bitcast.10), calls=%async_computation.1 | async-start | bytes 1048576 | tf_op jit(solution)/shard_map/dispatch/all_to_all | solution.py:35
  48.9 4.5 %collective-permute-start.2 = (bf16[480,128]{1,0:T(8,128)(2,1)S(1)}, bf16[480,128]{1,0:T(8,128)(2,1)S(1)}, u32[]{:S(2)}, u32[]{:S(2)}) collective-permute-start(bf16[480,128]{1,0:T(8,128)(2,1)S(1)} %get-tuple-element.20), channel_id=1, source_target_pairs={{0,384},{128,256},{256,128},{384,0},{1,385},{129,257},{257,129},{3... | collective-permute-start | bytes 368648 | tf_op jit(solution)/shard_map/weights/ppermute | solution.py:512
  53.4 2.5 %collective-permute-start.1 = (bf16[480,128]{1,0:T(8,128)(2,1)S(1)}, bf16[480,128]{1,0:T(8,128)(2,1)S(1)}, u32[]{:S(2)}, u32[]{:S(2)}) collective-permute-start(bf16[480,128]{1,0:T(8,128)(2,1)S(1)} %get-tuple-element.20), channel_id=1, source_target_pairs={{0,256},{128,384},{256,0},{384,128},{1,257},{129,385},{257,1},{385... | collective-permute-start | bytes 368648 | tf_op jit(solution)/shard_map/weights/ppermute | solution.py:512
  55.9 2.0 %collective-permute-start = (bf16[480,128]{1,0:T(8,128)(2,1)S(1)}, bf16[480,128]{1,0:T(8,128)(2,1)S(1)}, u32[]{:S(2)}, u32[]{:S(2)}) collective-permute-start(bf16[480,128]{1,0:T(8,128)(2,1)S(1)} %get-tuple-element.20), channel_id=1, source_target_pairs={{0,128},{128,0},{256,384},{384,256},{1,129},{129,1},{257,385},{385... | collective-permute-start | bytes 368648 | tf_op jit(solution)/shard_map/weights/ppermute | solution.py:512
  58.2 5.5 %collective-permute-done.2 = bf16[480,128]{1,0:T(8,128)(2,1)S(1)} collective-permute-done((bf16[480,128]{1,0:T(8,128)(2,1)S(1)}, bf16[480,128]{1,0:T(8,128)(2,1)S(1)}, u32[]{:S(2)}, u32[]{:S(2)}) %collective-permute-start.2) | collective-permute-done | bytes 122912 | tf_op jit(solution)/shard_map/weights/ppermute | solution.py:512
  63.8 2.8 %all-gather = bf16[8,480,128]{2,1,0:T(8,128)(2,1)S(1)} all-gather(bf16[4,480,128]{2,1,0:T(8,128)(2,1)S(1)} %pad_maximum_fusion), channel_id=2, replica_groups=mesh['y'=4,'zh'=4,'zl'=4,'c'=2,'x'=4] {'c'}, dimensions={0}, use_global_device_ids=true | all-gather | bytes 1474560 | tf_op jit(solution)/shard_map/weights/all_gather | solution.py:514
  66.7 3.1 %forward.1 = (f32[1,32]{1,0:T(1,128)S(1)}, f32[3,256,256]{2,1,0:T(8,128)S(1)}, bf16[256,576]{1,0:T(8,128)(2,1)S(1)}, bf16[4,192,640]{2,1,0:T(8,128)(2,1)S(1)}) custom-call(s32[4]{0:T(128)S(1)} %copy-done.3, bf16[4,256,256]{2,1,0:T(8,128)(2,1)S(1)} %bitcast.27, bf16[2,4,480,128]{3,2,1,0:T(8,128)(2,1)S(1)} %bitcast.29, f32[4,1,192]{2,1,0:T(1,128)S(1)} %reshape.32.gain_ref, ...), custom_call_target="tpu_custom_call" | custom-call | tf_op jit(solution)/shard_map/attend/forward/pallas_call | solution.py:427
  69.8 7.6 %all-gather.3.part_logits_ref = f32[4,1,32]{2,1,0:T(1,128)S(1)} all-gather(f32[1,1,32]{2,1,0:T(1,128)S(1)} %bitcast.39), channel_id=3, replica_groups=mesh['y'=4,'zh'=4,'zl'=4,'c'=2,'x'=4] {'x'}, dimensions={0}, use_global_device_ids=true | all-gather | bytes 640 | tf_op jit(solution)/shard_map/attend/all_gather | solution.py:531
  77.4 3.8 %backward.1 = (f32[1,32]{1,0:T(1,128)}, bf16[4,8,48,128]{3,2,1,0:T(8,128)(2,1)S(1)}) custom-call(s32[4]{0:T(128)S(1)} %copy-done.3, f32[4,1,32]{2,1,0:T(1,128)S(1)} %all-gather.3.part_logits_ref, s32[1,128]{1,0:T(1,128)S(1)} %bitcast.37, s32[1,128]{1,0:T(1,128)S(1)} %bitcast.38, bf16[4,256,256]{2,1,0:T(8,128)(2,1)S(1)} %bitcast.28, ...), custom_call_target="tpu_custom_call" | custom-call | tf_op jit(solution)/shard_map/attend/backward/pallas_call | solution.py:427
  81.2 16.3 %all_to_all.36 = bf16[32,48,128]{2,1,0:T(8,128)(2,1)S(1)} all-to-all(bf16[32,48,128]{2,1,0:T(8,128)(2,1)S(1)} %bitcast.34), channel_id=1, replica_groups=mesh['y'=4,'zh'=4,'zl'=4,'c'=2,'x'=4] {'x','y','c'}, dimensions={0} | all-to-all | bytes 786432 | tf_op jit(solution)/shard_map/give_back/all_to_all | solution.py:35
  97.5 0.3 fold.1
  97.8 17.0 %all_to_all.37.back_ref = bf16[16,24,128]{2,1,0:T(8,128)(2,1)S(1)} all-to-all(bf16[16,24,128]{2,1,0:T(8,128)(2,1)S(1)} %fold.1), channel_id=1, replica_groups=mesh['y'=4,'zh'=4,'zl'=4,'c'=2,'x'=4] {'zh','zl'}, dimensions={0} | all-to-all | bytes 196608 | tf_op jit(solution)/shard_map/give_back/all_to_all | solution.py:35
  114.8 1.7 weight_grad.1
  116.5 3.6 %collective-permute-start.3 = (bf16[16,104,128]{2,1,0:T(8,128)(2,1)S(1)}, bf16[16,104,128]{2,1,0:T(8,128)(2,1)S(1)}, u32[]{:S(2)}, u32[]{:S(2)}) collective-permute-start(bf16[16,104,128]{2,1,0:T(8,128)(2,1)S(1)} %get-tuple-element.30), channel_id=1, source_target_pairs={{0,4},{4,0},{1,5},{5,1},{2,6},{6,2},{3,7},{7,3},{8,12},{12,8},{9,1... | collective-permute-start | bytes 1277960 | tf_op jit(solution)/shard_map/reduce/ppermute | solution.py:575
  120.2 1.4 collective-permute-done.3
  121.7 17.8 %all_to_all.38 = bf16[16,104,128]{2,1,0:T(8,128)(2,1)S(1)} all-to-all(bf16[16,104,128]{2,1,0:T(8,128)(2,1)S(1)} %add_convert_fusion), channel_id=1, replica_groups=mesh['y'=4,'zh'=4,'zl'=4,'c'=2,'x'=4] {'y','zl'}, dimensions={0} | all-to-all | bytes 851968 | tf_op jit(solution)/shard_map/reduce/all_to_all | solution.py:35
  139.6 16.3 %all_to_all.39 = bf16[4,104,128]{2,1,0:T(8,128)(2,1)S(1)} all-to-all(bf16[4,104,128]{2,1,0:T(8,128)(2,1)S(1)} %broadcast_in_dim.29), channel_id=1, replica_groups=mesh['y'=4,'zh'=4,'zl'=4,'c'=2,'x'=4] {'zh'}, dimensions={0} | all-to-all | bytes 212992 | tf_op jit(solution)/shard_map/reduce/all_to_all | solution.py:35
  156.0 14.2 %all_to_all.40 = bf16[16,104,128]{2,1,0:T(8,128)(2,1)S(1)} all-to-all(bf16[16,104,128]{2,1,0:T(8,128)(2,1)S(1)} %broadcast_in_dim.30), channel_id=1, replica_groups=mesh['y'=4,'zh'=4,'zl'=4,'c'=2,'x'=4] {'y','zl'}, dimensions={0} | all-to-all | bytes 851968 | tf_op jit(solution)/shard_map/reduce/all_to_all | solution.py:35
  170.2 6.8 %all-gather.2 = bf16[32,104,128]{2,1,0:T(8,128)(2,1)S(1)} all-gather(bf16[16,104,128]{2,1,0:T(8,128)(2,1)S(1)} %all_to_all.40), channel_id=4, replica_groups=mesh['y'=4,'zh'=4,'zl'=4,'c'=2,'x'=4] {'c'}, dimensions={0}, use_global_device_ids=true | all-gather | bytes 1277952 | tf_op jit(solution)/shard_map/reduce/all_gather | solution.py:579
  177.0 1.3 unpack.1
  (28 shorter events, 0.6 us)
Async XLA Ops:
  1.3 56.6 %copy-start.6 = (f32[768,32]{0,1:T(8,128)S(1)}, f32[768,32]{0,1:T(8,128)}, u32[]{:S(2)}) copy-start(f32[768,32]{0,1:T(8,128)} %param.21) | copy-start | bytes 294916
  1.3 56.8 %copy-start.7 = (f32[768]{0:T(1024)S(1)}, f32[768]{0:T(1024)}, u32[]{:S(2)}) copy-start(f32[768]{0:T(1024)} %param.18) | copy-start | bytes 9220
  6.6 60.1 %copy-start.3 = (s32[4]{0:T(128)S(1)}, s32[4]{0:T(128)}, u32[]{:S(2)}) copy-start(s32[4]{0:T(128)} %pad_add_fusion.place_ref) | copy-start | bytes 52
  36.2 30.4 %all-to-all-start.1 = ((bf16[32,32,256]{2,1,0:T(8,128)(2,1)}), bf16[32,32,256]{2,1,0:T(8,128)(2,1)S(1)}, u32[]{:S(2)}, u32[]{:S(2)}) async-start(bf16[32,32,256]{2,1,0:T(8,128)(2,1)} %bitcast.10), calls=%async_computation.1 | async-start | bytes 1048576 | tf_op jit(solution)/shard_map/dispatch/all_to_all | solution.py:35
  48.9 28.5 %copy-start.4 = (s32[128]{0:T(128)S(1)}, s32[128]{0:T(128)}, u32[]{:S(2)}) copy-start(s32[128]{0:T(128)} %param.14) | copy-start | bytes 1540
  48.9 28.5 %copy-start.5 = (s32[128]{0:T(128)S(1)}, s32[128]{0:T(128)}, u32[]{:S(2)}) copy-start(s32[128]{0:T(128)} %param.15) | copy-start | bytes 1540
  48.9 14.8 %collective-permute-start.2 = (bf16[480,128]{1,0:T(8,128)(2,1)S(1)}, bf16[480,128]{1,0:T(8,128)(2,1)S(1)}, u32[]{:S(2)}, u32[]{:S(2)}) collective-permute-start(bf16[480,128]{1,0:T(8,128)(2,1)S(1)} %get-tuple-element.20), channel_id=1, source_target_pairs={{0,384},{128,256},{256,128},{384,0},{1,385},{129,257},{257,129},{3... | collective-permute-start | bytes 368648 | tf_op jit(solution)/shard_map/weights/ppermute | solution.py:512
  53.4 10.3 %collective-permute-start.1 = (bf16[480,128]{1,0:T(8,128)(2,1)S(1)}, bf16[480,128]{1,0:T(8,128)(2,1)S(1)}, u32[]{:S(2)}, u32[]{:S(2)}) collective-permute-start(bf16[480,128]{1,0:T(8,128)(2,1)S(1)} %get-tuple-element.20), channel_id=1, source_target_pairs={{0,256},{128,384},{256,0},{384,128},{1,257},{129,385},{257,1},{385... | collective-permute-start | bytes 368648 | tf_op jit(solution)/shard_map/weights/ppermute | solution.py:512
  55.9 7.8 %collective-permute-start = (bf16[480,128]{1,0:T(8,128)(2,1)S(1)}, bf16[480,128]{1,0:T(8,128)(2,1)S(1)}, u32[]{:S(2)}, u32[]{:S(2)}) collective-permute-start(bf16[480,128]{1,0:T(8,128)(2,1)S(1)} %get-tuple-element.20), channel_id=1, source_target_pairs={{0,128},{128,0},{256,384},{384,256},{1,129},{129,1},{257,385},{385... | collective-permute-start | bytes 368648 | tf_op jit(solution)/shard_map/weights/ppermute | solution.py:512
  69.8 45.0 %copy-start = (bf16[144,4,2048]{2,1,0:T(4,128)(2,1)S(1)}, bf16[144,4,2048]{2,1,0:T(4,128)(2,1)}, u32[]{:S(2)}) copy-start(bf16[144,4,2048]{2,1,0:T(4,128)(2,1)} %features_ref.1) | copy-start | bytes 7077892
  69.8 45.0 %copy-start.1 = (bf16[576,192]{1,0:T(8,128)(2,1)S(1)}, bf16[576,192]{1,0:T(8,128)(2,1)}, u32[]{:S(2)}) copy-start(bf16[576,192]{1,0:T(8,128)(2,1)} %get-tuple-element.28.mask_ref) | copy-start | bytes 663556
  69.8 45.0 %copy-start.2 = (bf16[256,144]{1,0:T(8,128)(2,1)S(1)}, bf16[256,144]{1,0:T(8,128)(2,1)}, u32[]{:S(2)}) copy-start(bf16[256,144]{1,0:T(8,128)(2,1)} %get-tuple-element.26.placing_ref) | copy-start | bytes 221188
  116.5 5.0 %collective-permute-start.3 = (bf16[16,104,128]{2,1,0:T(8,128)(2,1)S(1)}, bf16[16,104,128]{2,1,0:T(8,128)(2,1)S(1)}, u32[]{:S(2)}, u32[]{:S(2)}) collective-permute-start(bf16[16,104,128]{2,1,0:T(8,128)(2,1)S(1)} %get-tuple-element.30), channel_id=1, source_target_pairs={{0,4},{4,0},{1,5},{5,1},{2,6},{6,2},{3,7},{7,3},{8,12},{12,8},{9,1... | collective-permute-start | bytes 1277960 | tf_op jit(solution)/shard_map/reduce/ppermute | solution.py:575

commit v5 on v4

--- a/solution.py
+++ b/solution.py
@@ -35,6 +35,25 @@
     return lax.all_to_all(blocks, axes, split_axis=0, concat_axis=0, tiled=True)
 
 
+def plane_groups():
+    lines, far_count, cores = 4, lax.axis_size(FAR), 2
+    length = lax.axis_size("zl")
+    groups = []
+    for core in range(cores):
+        for first in range(0, far_count, length):
+            stretch = [(first + core * length // 2 + at) % far_count for at in range(length)]
+            groups.append(
+                [(line * far_count + far) * cores + core for line in range(lines) for far in stretch]
+            )
+    return groups
+
+
+def swap_plane(blocks):
+    return lax.all_to_all(
+        blocks, ENC, split_axis=0, concat_axis=0, axis_index_groups=plane_groups(), tiled=True
+    )
+
+
 def gather_copies(block, axes):
     return swap(jnp.broadcast_to(block[None], (lax.axis_size(axes),) + block.shape), axes)
 
@@ -43,10 +62,10 @@
     return jnp.sum(swap(blocks, axes).astype(f32), axis=0).astype(bf16)
 
 
-def normed_parts(place_ref, rows_ref, cols):
+def normed_parts(rows_ref, cols):
     parts = [
-        rows_ref[part_of(place_ref, step), :, :cols].astype(f32)
-        for step in range(rows_ref.shape[0])
+        rows_ref[part, :, :cols].astype(f32)
+        for part in range(rows_ref.shape[0])
     ]
     width = cols * len(parts)
     mean = sum(jnp.sum(part, axis=1, keepdims=True) for part in parts) / width
@@ -70,14 +89,14 @@
 ):
     groups, slots, _ = rows_ref.shape
     cols = gain_ref.shape[2]
-    parts, normed, _ = normed_parts(place_ref, rows_ref, cols)
-    size = weight_ref.shape[2] // (-(-(3 * cols + 2 * CLASSES) // LANES))
+    parts, normed, _ = normed_parts(rows_ref, cols)
+    size = weight_ref.shape[1] // (-(-(3 * cols + 2 * CLASSES) // LANES))
     order = held_order(own_rows, cols)
     qkv = 0.0
-    for step in range(groups):
-        normed_in = (normed[step] * gain_ref[part_of(place_ref, step)]).astype(bf16)
-        block = across(order, weight_block(weight_ref, step, size), (1, 0)).astype(bf16)
-        weights_ref[step] = block
+    for part in range(groups):
+        normed_in = (normed[part] * gain_ref[part]).astype(bf16)
+        block = across(order, weight_block(weight_ref, part, size), (1, 0)).astype(bf16)
+        weights_ref[part] = block
         qkv = qkv + across(normed_in, block, (1, 0))
     qkv = qkv[:, : 3 * cols]
     column = lax.broadcasted_iota(jnp.int32, (slots, 3 * cols), 1)
@@ -116,10 +135,10 @@
         values = qkv[:, 2 * cols + first : 2 * cols + first + HD]
         mixed.append(across(in_terms(att_total), values, (1, 0)))
     mixed_total = jnp.sum(jnp.concatenate(mixed, axis=1), axis=0, keepdims=True)
-    total = across(mixed_total, wc, (1, 0), EXACT)
-    for step in range(groups):
-        row_sum = jnp.sum(parts[step], axis=0, keepdims=True) * (1.0 / groups)
-        total = total + across(row_sum, cls_ref[part_of(place_ref, step)], (1, 1), EXACT)
+    total = fine(mixed_total, wc, (1, 0))
+    for part in range(groups):
+        row_sum = jnp.sum(parts[part], axis=0, keepdims=True) * (1.0 / groups)
+        total = total + fine(row_sum, cls_ref[part], (1, 1))
     logits_ref[...] = total / count
 
 
@@ -139,7 +158,7 @@
 ):
     groups, slots, _ = rows_ref.shape
     cols = gain_ref.shape[2]
-    _, normed, inv_std = normed_parts(place_ref, rows_ref, cols)
+    _, normed, inv_std = normed_parts(rows_ref, cols)
     tags = rows_ref[0, :, cols : cols + 1].astype(f32)
     live = (tags > 0).astype(f32)
     count = jnp.sum(live, axis=0, keepdims=True)
@@ -152,7 +171,7 @@
     class_ids = lax.broadcasted_iota(jnp.int32, (1, CLASSES), 1).astype(f32)
     grad_logits = (class_probs - (class_ids == my_label).astype(f32)) / count
     wc = class_block(weights_ref, place_ref, cols)
-    grad_mixed = across(grad_logits, wc, (1, 1), EXACT).astype(bf16)
+    grad_mixed = fine(grad_logits, wc, (1, 1)).astype(bf16)
     qkv = qkv_ref[...]
     grad_q, grad_k, grad_v = [], [], []
     for head in range(cols // HD):
@@ -172,18 +191,17 @@
     unused = jnp.zeros((slots, 2 * CLASSES), f32)
     grad_qkv = jnp.concatenate(grad_q + grad_k + grad_v + [unused], axis=1).astype(bf16)
     scaled_parts = []
-    for step in range(groups):
-        grad_normed = across(grad_qkv, weights_ref[step], (1, 1))
-        scaled_parts.append(grad_normed * gain_ref[part_of(place_ref, step)])
+    for part in range(groups):
+        grad_normed = across(grad_qkv, weights_ref[part], (1, 1))
+        scaled_parts.append(grad_normed * gain_ref[part])
     width = cols * groups
     mean = sum(jnp.sum(e, axis=1, keepdims=True) for e in scaled_parts) / width
     slope = (
         sum(jnp.sum(e * n, axis=1, keepdims=True) for e, n in zip(scaled_parts, normed)) / width
     )
-    for step in range(groups):
-        part = part_of(place_ref, step)
-        pooled = across(grad_logits, cls_ref[part], (1, 0), EXACT) * (1.0 / groups)
-        grad = inv_std * (scaled_parts[step] - mean - normed[step] * slope)
+    for part in range(groups):
+        pooled = fine(grad_logits, cls_ref[part], (1, 0)) * (1.0 / groups)
+        grad = inv_std * (scaled_parts[part] - mean - normed[part] * slope)
         grad_ref[part] = fold_rows(live * pooled + grad, grad_ref.shape[1]).astype(bf16)
 
 
@@ -201,6 +219,14 @@
     low = (rest - middle.astype(f32)).astype(bf16)
     terms = [term.astype(f32) for term in (high, middle, low)]
     return jnp.concatenate(terms + [jnp.zeros((5, row.shape[1]), f32)], axis=0).astype(bf16)
+
+
+def fine(row, matrix, dims):
+    terms = in_terms(row)
+    high = matrix.astype(bf16)
+    low = (matrix - high.astype(f32)).astype(bf16)
+    summed = across(terms, high, dims) + across(terms, low, dims)
+    return jnp.sum(summed, axis=0, keepdims=True)
 
 
 def held_rows(blocks, rows):
@@ -361,48 +387,44 @@
     return (row == source.astype(jnp.int32)).astype(f32).astype(bf16)
 
 
-def weight_block(weight_ref, step, size):
+def weight_block(weight_ref, part, size):
     columns = []
-    for block in range(weight_ref.shape[2] // size):
-        pair = [weight_ref[core, step, block * size : (block + 1) * size] for core in range(2)]
+    for block in range(weight_ref.shape[1] // size):
+        pair = [
+            weight_ref[part * 2 + core, block * size : (block + 1) * size] for core in range(2)
+        ]
         columns.append(jnp.concatenate(pair, axis=0))
     return jnp.concatenate(columns, axis=1)
 
 
-def part_of(place_ref, step):
-    return place_ref[3] ^ step
-
-
 def class_block(weights_ref, place_ref, cols):
-    mine = weights_ref[place_ref[3] ^ place_ref[0]]
+    mine = weights_ref[place_ref[0]]
     both = mine[:, 3 * cols :].astype(f32)
     return both[:, :CLASSES] + both[:, CLASSES : 2 * CLASSES]
 
 
 def weight_grad_kernel(
-    place_ref, placing_ref, back_ref, mask_ref, features_ref, kept_ref, sent_ref
+    of_other, place_ref, placing_ref, back_ref, mask_ref, features_ref, half_ref
 ):
     tiles, positions, channels = features_ref.shape
-    cols = mask_ref.shape[1]
-    half = cols // 2
-    back = jnp.concatenate(unfold_rows(back_ref[...].astype(f32), 16), axis=1).astype(bf16)
+    half = mask_ref.shape[1] // 2
+    is_first = place_ref[2] == (1 if of_other else 0)
+    back = jnp.concatenate(unfold_rows(back_ref[...].astype(f32), 16), axis=1)
+    back = jnp.where(is_first, back[:, :half], back[:, half:]).astype(bf16)
+    mask = mask_ref[...].astype(f32)
+    mask = jnp.where(is_first, mask[:, :half], mask[:, half:])
     tile_grads = across(placing_ref[...], back, (0, 0))
-    spread = jnp.broadcast_to(tile_grads[:, None, :], (tiles, positions, cols))
-    grad_preact = spread.reshape(tiles * positions, cols) * mask_ref[...].astype(f32)
+    spread = jnp.broadcast_to(tile_grads[:, None, :], (tiles, positions, half))
+    grad_preact = spread.reshape(tiles * positions, half) * mask
     bias = jnp.sum(grad_preact, axis=0, keepdims=True)
     flattened = features_ref[...].reshape(tiles * positions, channels)
     grad = across(grad_preact.astype(bf16), flattened, (0, 0))
-    lanes = channels // kept_ref.shape[0]
-    first_core = place_ref[2] == 0
-    for out_ref, is_first in ((kept_ref, first_core), (sent_ref, jnp.logical_not(first_core))):
-        bias_half = jnp.where(is_first, bias[:, :half], bias[:, half:])
-        bias_rows = jnp.broadcast_to(
-            jnp.concatenate([bias_half, jnp.zeros((1, lanes - half), f32)], axis=1), (8, lanes)
-        )
-        for place in range(kept_ref.shape[0]):
-            block = grad[:, place * lanes : (place + 1) * lanes]
-            picked = jnp.where(is_first, block[:half], block[half:])
-            out_ref[place] = jnp.concatenate([picked, bias_rows], axis=0).astype(bf16)
+    lanes = channels // half_ref.shape[0]
+    bias_rows = jnp.concatenate([bias, jnp.zeros((1, lanes - half), f32)], axis=1)
+    bias_rows = jnp.broadcast_to(bias_rows, (8, lanes))
+    for place in range(half_ref.shape[0]):
+        block = grad[:, place * lanes : (place + 1) * lanes]
+        half_ref[place] = jnp.concatenate([block, bias_rows], axis=0).astype(bf16)
 
 
 def unpack_kernel(parts_ref, grad_ref, bias_ref):
@@ -459,9 +481,7 @@
     owner_at = lax.axis_index(ENC)
 
     shape = jax.ShapeDtypeStruct
-    place = jnp.stack([group_at, owner_at, lax.axis_index("c"), lax.axis_index("y")]).astype(
-        jnp.int32
-    )
+    place = jnp.stack([group_at, owner_at, lax.axis_index("c")]).astype(jnp.int32)
     width = 3 * cols + 2 * CLASSES
 
     with jax.named_scope("encode"):
@@ -486,7 +506,7 @@
                 shape((tile_count * POS, cols), bf16),
                 shape((slot_total, tile_count), bf16),
             ),
-            (place,) + sources,
+            (group_at.astype(jnp.int32)[None],) + sources,
             "s" + "a" * len(sources),
             [pltpu.VMEM(source.shape, source.dtype) for source in sources]
             + [pltpu.SemaphoreType.DMA((len(sources),))],
@@ -508,10 +528,7 @@
         ).reshape(groups, slot_total, BLOCK)
 
     with jax.named_scope("weights"):
-        steps = [
-            lax.ppermute(far_held, "y", [(at, at ^ step) for at in range(4)]) for step in range(1, 4)
-        ]
-        weights = lax.all_gather(jnp.stack([far_held] + steps), "c", axis=0)
+        weights = lax.all_gather(far_held, NEAR, axis=0)
 
     with jax.named_scope("attend"):
         gain = norm_gain.reshape(groups, 1, cols)
@@ -563,20 +580,29 @@
     with jax.named_scope("encoder_grad"):
         plane_count = lax.axis_size(PLANE)
         block = (cols // 2 + 8, channels // plane_count)
-        kept, sent = run(
-            weight_grad_kernel,
-            "weight_grad",
-            (shape((plane_count,) + block, bf16),) * 2,
-            (place, placing, back_rows, mask, features),
+        operands = (place, placing, back_rows, mask, features)
+        (sent,) = run(
+            functools.partial(weight_grad_kernel, True),
+            "other_half",
+            (shape((plane_count,) + block, bf16),),
+            operands,
             "svvvv",
         )
+        other = lax.ppermute(sent, "c", [(0, 1), (1, 0)])
+        (kept,) = run(
+            functools.partial(weight_grad_kernel, False),
+            "own_half",
+            (shape((plane_count,) + block, bf16),),
+            operands,
+            "svvvv",
+        )
 
     with jax.named_scope("reduce"):
-        other = lax.ppermute(sent, "c", [(0, 1), (1, 0)])
         core_sum = (kept.astype(f32) + other.astype(f32)).astype(bf16)
-        plane_sum = sum_blocks(core_sum, PLANE)
+        plane_sum = jnp.sum(swap_plane(core_sum).astype(f32), axis=0).astype(bf16)
         total = jnp.sum(gather_copies(plane_sum, "zh").astype(f32), axis=0).astype(bf16)
-        all_parts = lax.all_gather(gather_copies(total, PLANE), "c", axis=0)
+        copies = jnp.broadcast_to(total[None], (plane_count,) + total.shape)
+        all_parts = lax.all_gather(swap_plane(copies), "c", axis=0)
         enc_grad, bias_grad = run(
             unpack_kernel,
             "unpack",

time: 179 us -> 175 us (0.978)
  blocking collectives: 127 us -> 112 us
  starting transfers between devices: 25.2 us -> 32 us
  waiting for transfers between devices: 6.93 us -> 12.4 us
    all_to_all x6 -> x3, blocking collectives: 110 us -> 48.8 us  [swap(): return lax.all_to_all(blocks, axes, split_axis=0, concat_axis=0, tiled=True)]
    all_to_all x0 -> x2, blocking collectives: none -> 32.2 us  [swap_plane(): lax.all_to_all(blocks, ENC, split_axis=0, concat_axis=0, axis_index_group...]
    all_to_all x1 -> x2, starting transfers between devices: 12.7 us -> 28.4 us  [swap(): return lax.all_to_all(blocks, axes, split_axis=0, concat_axis=0, tiled=True)]
    all_to_all x1 -> x2, waiting for transfers between devices: 0.01 us -> 12.4 us  [swap(): return lax.all_to_all(blocks, axes, split_axis=0, concat_axis=0, tiled=True)]
    all_gather x2, blocking collectives: 9.62 us -> 20.8 us  [the longest x1 16.9 us: on_device(): weights = lax.all_gather(far_held, NEAR, axis=0)]
    ppermute x3 -> x0, starting transfers between devices: 8.98 us -> none  [on_device(): lax.ppermute(far_held, 'y', [(at, at ^ step) for at in range(4)])]
    ppermute x3 -> x0, waiting for transfers between devices: 5.55 us -> none  [on_device(): lax.ppermute(far_held, 'y', [(at, at ^ step) for at in range(4)])]
    all_gather x1, blocking collectives: 7.57 us -> 9.78 us  [on_device(): all_logits = lax.all_gather(part_logits, 'x', axis=0)]
  transfers between devices with their start and end apart: 5 -> 3, of which waited for: 2 -> 1; matrix products, arithmetic and copies ran while one was open for 0% -> 0% of each run, Pallas kernels for 0% -> 1%
where the time goes in v5:
time: 175 us; the launch traced here: 174 us
  blocking collectives  112 us (64%)
  starting transfers between devices  32 us (18%)
  Pallas kernels  16.6 us (9%)
  waiting for transfers between devices  12.4 us (7%)
    all_to_all x3, blocking collectives, swap(): return lax.all_to_all(blocks, axes, split_axis=0, concat_axis=0, tiled=True)  48.8 us
    all_to_all x2, blocking collectives, swap_plane(): lax.all_to_all(blocks, ENC, split_axis=0, concat_axis=0, axis_index_group...  32.2 us
    all_to_all x2, starting transfers between devices, swap(): return lax.all_to_all(blocks, axes, split_axis=0, concat_axis=0, tiled=True)  28.4 us
    all_gather x1, blocking collectives, on_device(): weights = lax.all_gather(far_held, NEAR, axis=0)  16.9 us
    pallas_call x8, Pallas kernels, run(): pl.pallas_call(kernel, out_shape=out_shape, in_specs=[kinds[spec] for spe...  16.6 us
    all_to_all x2, waiting for transfers between devices, swap(): return lax.all_to_all(blocks, axes, split_axis=0, concat_axis=0, tiled=True)  12.4 us
    all_gather x1, blocking collectives, on_device(): all_logits = lax.all_gather(part_logits, 'x', axis=0)  9.78 us
    all_gather x1, blocking collectives, on_device(): all_parts = lax.all_gather(swap_plane(copies), 'c', axis=0)  3.83 us
  transfers between devices with their start and end apart: 3, of which 1 were waited for; matrix products, arithmetic and copies ran while one was open for 0% of the time, Pallas kernels for 1%

profile of v5, /device:TPU:1, one launch (start us, length us, event | category | flops | bytes accessed | tf_op | source)
XLA Modules:
  0.0 174.0 jit_solution(13694356937782456690)
XLA Ops:
  0.7 4.5 %send.1 = (bf16[16,56,128]{2,1,0:T(8,128)(2,1)}, bf16[576,192]{1,0:T(8,128)(2,1)}, bf16[256,144]{1,0:T(8,128)(2,1)}) custom-call(s32[1]{0:T(128)} %bitcast.place_ref, s32[1,144]{1,0:T(1,128)} %bitcast.37, s32[1,144]{1,0:T(1,128)} %bitcast.38, s32[1,128]{1,0:T(1,128)} %bitcast.30, bf16[6,2304]{1,0:T(8,128)(2,1)} %refs_3_.1, bf16[6,768]{1,0:T(8,128)(2,1)} %refs_4_.1, ...), custom_call_target="tpu_custom_call" | custom-call | tf_op jit(solution)/shard_map/encode/send/pallas_call | solution.py:449
  5.1 15.8 %all-to-all-start = ((bf16[16,56,128]{2,1,0:T(8,128)(2,1)}), bf16[16,56,128]{2,1,0:T(8,128)(2,1)S(1)}, u32[]{:S(2)}, u32[]{:S(2)}) async-start(bf16[16,56,128]{2,1,0:T(8,128)(2,1)} %get-tuple-element.16), calls=%async_computation | async-start | bytes 458752 | tf_op jit(solution)/shard_map/dispatch/all_to_all | solution.py:35
  20.9 0.1 reshape.33
  21.1 0.1 reshape.32.gain_ref
  21.2 12.4 %all-to-all-done.received_ref = bf16[16,56,128]{2,1,0:T(8,128)(2,1)S(1)} async-done(((bf16[16,56,128]{2,1,0:T(8,128)(2,1)}), bf16[16,56,128]{2,1,0:T(8,128)(2,1)S(1)}, u32[]{:S(2)}, u32[]{:S(2)}) %all-to-all-start) | async-done | bytes 229408 | tf_op jit(solution)/shard_map/dispatch/all_to_all | solution.py:35
  33.7 1.2 turn.1
  34.8 12.7 %all-to-all-start.1 = ((bf16[32,32,256]{2,1,0:T(8,128)(2,1)}), bf16[32,32,256]{2,1,0:T(8,128)(2,1)S(1)}, u32[]{:S(2)}, u32[]{:S(2)}) async-start(bf16[32,32,256]{2,1,0:T(8,128)(2,1)} %bitcast.9), calls=%async_computation.1 | async-start | bytes 1048576 | tf_op jit(solution)/shard_map/dispatch/all_to_all | solution.py:35
  47.5 0.1 pad_add_fusion.place_ref
  47.6 16.9 %all-gather = bf16[3840,128]{1,0:T(8,128)(2,1)S(1)} all-gather(bf16[480,128]{1,0:T(8,128)(2,1)S(1)} %get-tuple-element.18), channel_id=2, replica_groups=mesh['y'=4,'zh'=4,'zl'=4,'c'=2,'x'=4] {'y','c'}, dimensions={0}, use_global_device_ids=true | all-gather | bytes 1105920 | tf_op jit(solution)/shard_map/weights/all_gather | solution.py:531
  64.5 3.0 %forward.1 = (f32[1,32]{1,0:T(1,128)S(1)}, f32[3,256,256]{2,1,0:T(8,128)S(1)}, bf16[256,576]{1,0:T(8,128)(2,1)S(1)}, bf16[4,192,640]{2,1,0:T(8,128)(2,1)S(1)}) custom-call(s32[3]{0:T(128)S(1)} %pad_add_fusion.place_ref, bf16[4,256,256]{2,1,0:T(8,128)(2,1)S(1)} %bitcast.22, bf16[8,480,128]{2,1,0:T(8,128)(2,1)S(1)} %bitcast.24, ...), custom_call_target="tpu_custom_call" | custom-call | tf_op jit(solution)/shard_map/attend/forward/pallas_call | solution.py:449
  67.5 9.8 %all-gather.3.part_logits_ref = f32[4,1,32]{2,1,0:T(1,128)S(1)} all-gather(f32[1,1,32]{2,1,0:T(1,128)S(1)} %bitcast.33), channel_id=3, replica_groups=mesh['y'=4,'zh'=4,'zl'=4,'c'=2,'x'=4] {'x'}, dimensions={0}, use_global_device_ids=true | all-gather | bytes 640 | tf_op jit(solution)/shard_map/attend/all_gather | solution.py:548
  77.3 3.2 %backward.1 = (f32[1,32]{1,0:T(1,128)}, bf16[4,8,48,128]{3,2,1,0:T(8,128)(2,1)S(1)}) custom-call(s32[3]{0:T(128)S(1)} %pad_add_fusion.place_ref, f32[4,1,32]{2,1,0:T(1,128)S(1)} %all-gather.3.part_logits_ref, s32[1,128]{1,0:T(1,128)S(1)} %bitcast.31, s32[1,128]{1,0:T(1,128)S(1)} %bitcast.32, bf16[4,256,256]{2,1,0:T(8,128)(2,1)S(1)} %bitcast.23, ...), custom_call_target="tpu_custom_call" | custom-call | tf_op jit(solution)/shard_map/attend/backward/pallas_call | solution.py:449
  80.5 15.5 %all_to_all.35 = bf16[32,48,128]{2,1,0:T(8,128)(2,1)S(1)} all-to-all(bf16[32,48,128]{2,1,0:T(8,128)(2,1)S(1)} %bitcast.29), channel_id=1, replica_groups=mesh['y'=4,'zh'=4,'zl'=4,'c'=2,'x'=4] {'x','y','c'}, dimensions={0} | all-to-all | bytes 786432 | tf_op jit(solution)/shard_map/give_back/all_to_all | solution.py:35
  96.0 0.3 fold.1
  96.3 17.0 %all_to_all.36.back_ref = bf16[16,24,128]{2,1,0:T(8,128)(2,1)S(1)} all-to-all(bf16[16,24,128]{2,1,0:T(8,128)(2,1)S(1)} %fold.1), channel_id=1, replica_groups=mesh['y'=4,'zh'=4,'zl'=4,'c'=2,'x'=4] {'zh','zl'}, dimensions={0} | all-to-all | bytes 196608 | tf_op jit(solution)/shard_map/give_back/all_to_all | solution.py:35
  113.3 1.6 other_half.1
  114.9 3.6 %collective-permute-start = (bf16[16,104,128]{2,1,0:T(8,128)(2,1)S(1)}, bf16[16,104,128]{2,1,0:T(8,128)(2,1)S(1)}, u32[]{:S(2)}, u32[]{:S(2)}) collective-permute-start(bf16[16,104,128]{2,1,0:T(8,128)(2,1)S(1)} %other_half.1), channel_id=1, source_target_pairs={{0,4},{4,0},{1,5},{5,1},{2,6},{6,2},{3,7},{7,3},{8,12},{12,8},{9,1... | collective-permute-start | bytes 1277960 | tf_op jit(solution)/shard_map/encoder_grad/ppermute | solution.py:591
  118.5 1.6 own_half.1
  120.1 0.1 add_convert_fusion
  120.2 15.0 %all_to_all.37 = bf16[16,104,128]{2,1,0:T(8,128)(2,1)S(1)} all-to-all(bf16[16,104,128]{2,1,0:T(8,128)(2,1)S(1)} %add_convert_fusion), channel_id=1, replica_groups={{0,8,16,24,128,136,144,152,256,264,272,280,384,392,400,408},{32,40,48,5..., dimensions={0} | all-to-all | bytes 851968 | tf_op jit(solution)/shard_map/reduce/all_to_all | solution.py:52
  135.3 16.4 %all_to_all.38 = bf16[4,104,128]{2,1,0:T(8,128)(2,1)S(1)} all-to-all(bf16[4,104,128]{2,1,0:T(8,128)(2,1)S(1)} %broadcast_in_dim.30), channel_id=1, replica_groups=mesh['y'=4,'zh'=4,'zl'=4,'c'=2,'x'=4] {'zh'}, dimensions={0} | all-to-all | bytes 212992 | tf_op jit(solution)/shard_map/reduce/all_to_all | solution.py:35
  151.8 17.1 %all_to_all.39 = bf16[16,104,128]{2,1,0:T(8,128)(2,1)S(1)} all-to-all(bf16[16,104,128]{2,1,0:T(8,128)(2,1)S(1)} %broadcast_in_dim.31), channel_id=1, replica_groups={{0,8,16,24,128,136,144,152,256,264,272,280,384,392,400,408},{32,40,48,5..., dimensions={0} | all-to-all | bytes 851968 | tf_op jit(solution)/shard_map/reduce/all_to_all | solution.py:52
  168.9 3.8 %all-gather.2 = bf16[32,104,128]{2,1,0:T(8,128)(2,1)S(1)} all-gather(bf16[16,104,128]{2,1,0:T(8,128)(2,1)S(1)} %all_to_all.39), channel_id=4, replica_groups=mesh['y'=4,'zh'=4,'zl'=4,'c'=2,'x'=4] {'c'}, dimensions={0}, use_global_device_ids=true | all-gather | bytes 1277952 | tf_op jit(solution)/shard_map/reduce/all_gather | solution.py:605
  172.8 1.3 unpack.1
  (21 shorter events, 0.2 us)
Async XLA Ops:
  0.6 20.3 %copy-start.5 = (f32[768,32]{0,1:T(8,128)S(1)}, f32[768,32]{0,1:T(8,128)}, u32[]{:S(2)}) copy-start(f32[768,32]{0,1:T(8,128)} %param.21) | copy-start | bytes 294916
  0.6 20.4 %copy-start.6 = (f32[768]{0:T(1024)S(1)}, f32[768]{0:T(1024)}, u32[]{:S(2)}) copy-start(f32[768]{0:T(1024)} %param.18) | copy-start | bytes 9220
  5.1 28.5 %all-to-all-start = ((bf16[16,56,128]{2,1,0:T(8,128)(2,1)}), bf16[16,56,128]{2,1,0:T(8,128)(2,1)S(1)}, u32[]{:S(2)}, u32[]{:S(2)}) async-start(bf16[16,56,128]{2,1,0:T(8,128)(2,1)} %get-tuple-element.16), calls=%async_computation | async-start | bytes 458752 | tf_op jit(solution)/shard_map/dispatch/all_to_all | solution.py:35
  20.9 56.4 %copy-start.3 = (s32[128]{0:T(128)S(1)}, s32[128]{0:T(128)}, u32[]{:S(2)}) copy-start(s32[128]{0:T(128)} %param.14) | copy-start | bytes 1540
  20.9 56.4 %copy-start.4 = (s32[128]{0:T(128)S(1)}, s32[128]{0:T(128)}, u32[]{:S(2)}) copy-start(s32[128]{0:T(128)} %param.15) | copy-start | bytes 1540
  34.8 29.7 %all-to-all-start.1 = ((bf16[32,32,256]{2,1,0:T(8,128)(2,1)}), bf16[32,32,256]{2,1,0:T(8,128)(2,1)S(1)}, u32[]{:S(2)}, u32[]{:S(2)}) async-start(bf16[32,32,256]{2,1,0:T(8,128)(2,1)} %bitcast.9), calls=%async_computation.1 | async-start | bytes 1048576 | tf_op jit(solution)/shard_map/dispatch/all_to_all | solution.py:35
  67.5 45.8 %copy-start = (bf16[144,4,2048]{2,1,0:T(4,128)(2,1)S(1)}, bf16[144,4,2048]{2,1,0:T(4,128)(2,1)}, u32[]{:S(2)}) copy-start(bf16[144,4,2048]{2,1,0:T(4,128)(2,1)} %features_ref.3) | copy-start | bytes 7077892
  67.5 45.8 %copy-start.1 = (bf16[576,192]{1,0:T(8,128)(2,1)S(1)}, bf16[576,192]{1,0:T(8,128)(2,1)}, u32[]{:S(2)}) copy-start(bf16[576,192]{1,0:T(8,128)(2,1)} %get-tuple-element.26.mask_ref) | copy-start | bytes 663556
  67.5 45.8 %copy-start.2 = (bf16[256,144]{1,0:T(8,128)(2,1)S(1)}, bf16[256,144]{1,0:T(8,128)(2,1)}, u32[]{:S(2)}) copy-start(bf16[256,144]{1,0:T(8,128)(2,1)} %get-tuple-element.24.placing_ref) | copy-start | bytes 221188
  114.9 5.2 %collective-permute-start = (bf16[16,104,128]{2,1,0:T(8,128)(2,1)S(1)}, bf16[16,104,128]{2,1,0:T(8,128)(2,1)S(1)}, u32[]{:S(2)}, u32[]{:S(2)}) collective-permute-start(bf16[16,104,128]{2,1,0:T(8,128)(2,1)S(1)} %other_half.1), channel_id=1, source_target_pairs={{0,4},{4,0},{1,5},{5,1},{2,6},{6,2},{3,7},{7,3},{8,12},{12,8},{9,1... | collective-permute-start | bytes 1277960 | tf_op jit(solution)/shard_map/encoder_grad/ppermute | solution.py:591

commit v6 on v5

--- a/solution.py
+++ b/solution.py
@@ -202,7 +202,9 @@
     for part in range(groups):
         pooled = fine(grad_logits, cls_ref[part], (1, 0)) * (1.0 / groups)
         grad = inv_std * (scaled_parts[part] - mean - normed[part] * slope)
-        grad_ref[part] = fold_rows(live * pooled + grad, grad_ref.shape[1]).astype(bf16)
+        folded = fold_rows(live * pooled + grad, grad_ref.shape[0]).astype(bf16)
+        for near in range(grad_ref.shape[0]):
+            grad_ref[near, part] = folded[near]
 
 
 def as_column(row):
@@ -368,9 +370,9 @@
 
 
 def fold_kernel(parts_ref, back_ref):
-    groups = parts_ref.shape[0]
+    groups = parts_ref.shape[1]
     far_count = back_ref.shape[0]
-    total = sum(parts_ref[group].astype(f32) for group in range(groups))
+    total = sum(parts_ref[:, group].astype(f32) for group in range(groups))
     wide, narrow = unfold_rows(total, far_count * SLOTS)
     total = jnp.concatenate([wide, narrow], axis=1).astype(bf16)
     order = slot_order(far_count.bit_length() - 1, total.shape[0])
@@ -551,7 +553,7 @@
             "backward",
             (
                 shape((1, CLASSES), f32),
-                shape((groups, near_count, far_count * SLOTS * 3 // 2, LANES), bf16),
+                shape((near_count, groups, far_count * SLOTS * 3 // 2, LANES), bf16),
             ),
             (
                 place,
@@ -570,7 +572,7 @@
 
     with jax.named_scope("give_back"):
         from_near = swap(
-            grad_parts.reshape((groups * near_count,) + grad_parts.shape[2:]), ("x",) + NEAR
+            grad_parts.reshape((groups * near_count,) + grad_parts.shape[2:]), NEAR + ("x",)
         ).reshape(grad_parts.shape)
         (folded,) = run(
             fold_kernel, "fold", (shape((far_count, 24, LANES), bf16),), (from_near,), "v"

time: 175 us -> 175 us (level)
  no operation moved by 1% of the time
where the time goes in v6:
time: 175 us; the launch traced here: 174 us
  blocking collectives  111 us (63%)
  starting transfers between devices  33.1 us (19%)
  Pallas kernels  16.6 us (9%)
  waiting for transfers between devices  12.4 us (7%)
    all_to_all x3, blocking collectives, swap(): return lax.all_to_all(blocks, axes, split_axis=0, concat_axis=0, tiled=True)  48.4 us
    all_to_all x2, blocking collectives, swap_plane(): lax.all_to_all(blocks, ENC, split_axis=0, concat_axis=0, axis_index_group...  30.9 us
    all_to_all x2, starting transfers between devices, swap(): return lax.all_to_all(blocks, axes, split_axis=0, concat_axis=0, tiled=True)  28.4 us
    all_gather x1, blocking collectives, on_device(): weights = lax.all_gather(far_held, NEAR, axis=0)  16.9 us
    pallas_call x8, Pallas kernels, run(): pl.pallas_call(kernel, out_shape=out_shape, in_specs=[kinds[spec] for spe...  16.6 us
    all_to_all x2, waiting for transfers between devices, swap(): return lax.all_to_all(blocks, axes, split_axis=0, concat_axis=0, tiled=True)  12.4 us
    all_gather x1, blocking collectives, on_device(): all_logits = lax.all_gather(part_logits, 'x', axis=0)  9.78 us
    ppermute x1, starting transfers between devices, on_device(): other = lax.ppermute(sent, 'c', [(0, 1), (1, 0)])  4.65 us
  transfers between devices with their start and end apart: 3, of which 1 were waited for; matrix products, arithmetic and copies ran while one was open for 0% of the time, Pallas kernels for 1%

profile of v6, /device:TPU:1, one launch (start us, length us, event | category | flops | bytes accessed | tf_op | source)
XLA Modules:
  0.0 174.1 jit_solution(6138890544030484570)
XLA Ops:
  0.7 4.5 %send.1 = (bf16[16,56,128]{2,1,0:T(8,128)(2,1)}, bf16[576,192]{1,0:T(8,128)(2,1)}, bf16[256,144]{1,0:T(8,128)(2,1)}) custom-call(s32[1]{0:T(128)} %bitcast.place_ref, s32[1,144]{1,0:T(1,128)} %bitcast.37, s32[1,144]{1,0:T(1,128)} %bitcast.38, s32[1,128]{1,0:T(1,128)} %bitcast.30, bf16[6,2304]{1,0:T(8,128)(2,1)} %refs_3_.1, bf16[6,768]{1,0:T(8,128)(2,1)} %refs_4_.1, ...), custom_call_target="tpu_custom_call" | custom-call | tf_op jit(solution)/shard_map/encode/send/pallas_call | solution.py:451
  5.1 15.8 %all-to-all-start = ((bf16[16,56,128]{2,1,0:T(8,128)(2,1)}), bf16[16,56,128]{2,1,0:T(8,128)(2,1)S(1)}, u32[]{:S(2)}, u32[]{:S(2)}) async-start(bf16[16,56,128]{2,1,0:T(8,128)(2,1)} %get-tuple-element.16), calls=%async_computation | async-start | bytes 458752 | tf_op jit(solution)/shard_map/dispatch/all_to_all | solution.py:35
  20.9 0.1 reshape.33
  21.1 0.1 reshape.32.gain_ref
  21.2 12.4 %all-to-all-done.received_ref = bf16[16,56,128]{2,1,0:T(8,128)(2,1)S(1)} async-done(((bf16[16,56,128]{2,1,0:T(8,128)(2,1)}), bf16[16,56,128]{2,1,0:T(8,128)(2,1)S(1)}, u32[]{:S(2)}, u32[]{:S(2)}) %all-to-all-start) | async-done | bytes 229408 | tf_op jit(solution)/shard_map/dispatch/all_to_all | solution.py:35
  33.7 1.2 turn.1
  34.8 12.7 %all-to-all-start.1 = ((bf16[32,32,256]{2,1,0:T(8,128)(2,1)}), bf16[32,32,256]{2,1,0:T(8,128)(2,1)S(1)}, u32[]{:S(2)}, u32[]{:S(2)}) async-start(bf16[32,32,256]{2,1,0:T(8,128)(2,1)} %bitcast.9), calls=%async_computation.1 | async-start | bytes 1048576 | tf_op jit(solution)/shard_map/dispatch/all_to_all | solution.py:35
  47.5 0.1 pad_add_fusion.place_ref
  47.6 16.9 %all-gather = bf16[3840,128]{1,0:T(8,128)(2,1)S(1)} all-gather(bf16[480,128]{1,0:T(8,128)(2,1)S(1)} %get-tuple-element.18), channel_id=2, replica_groups=mesh['y'=4,'zh'=4,'zl'=4,'c'=2,'x'=4] {'y','c'}, dimensions={0}, use_global_device_ids=true | all-gather | bytes 1105920 | tf_op jit(solution)/shard_map/weights/all_gather | solution.py:533
  64.5 3.0 %forward.1 = (f32[1,32]{1,0:T(1,128)S(1)}, f32[3,256,256]{2,1,0:T(8,128)S(1)}, bf16[256,576]{1,0:T(8,128)(2,1)S(1)}, bf16[4,192,640]{2,1,0:T(8,128)(2,1)S(1)}) custom-call(s32[3]{0:T(128)S(1)} %pad_add_fusion.place_ref, bf16[4,256,256]{2,1,0:T(8,128)(2,1)S(1)} %bitcast.22, bf16[8,480,128]{2,1,0:T(8,128)(2,1)S(1)} %bitcast.24, ...), custom_call_target="tpu_custom_call" | custom-call | tf_op jit(solution)/shard_map/attend/forward/pallas_call | solution.py:451
  67.5 9.8 %all-gather.3.part_logits_ref = f32[4,1,32]{2,1,0:T(1,128)S(1)} all-gather(f32[1,1,32]{2,1,0:T(1,128)S(1)} %bitcast.33), channel_id=3, replica_groups=mesh['y'=4,'zh'=4,'zl'=4,'c'=2,'x'=4] {'x'}, dimensions={0}, use_global_device_ids=true | all-gather | bytes 640 | tf_op jit(solution)/shard_map/attend/all_gather | solution.py:550
  77.3 3.2 %backward.1 = (f32[1,32]{1,0:T(1,128)}, bf16[8,4,48,128]{3,2,1,0:T(8,128)(2,1)S(1)}) custom-call(s32[3]{0:T(128)S(1)} %pad_add_fusion.place_ref, f32[4,1,32]{2,1,0:T(1,128)S(1)} %all-gather.3.part_logits_ref, s32[1,128]{1,0:T(1,128)S(1)} %bitcast.31, s32[1,128]{1,0:T(1,128)S(1)} %bitcast.32, bf16[4,256,256]{2,1,0:T(8,128)(2,1)S(1)} %bitcast.23, ...), custom_call_target="tpu_custom_call" | custom-call | tf_op jit(solution)/shard_map/attend/backward/pallas_call | solution.py:451
  80.5 15.3 %all_to_all.35 = bf16[32,48,128]{2,1,0:T(8,128)(2,1)S(1)} all-to-all(bf16[32,48,128]{2,1,0:T(8,128)(2,1)S(1)} %bitcast.29), channel_id=1, replica_groups=mesh['y'=4,'zh'=4,'zl'=4,'c'=2,'x'=4] {'y','c','x'}, dimensions={0} | all-to-all | bytes 786432 | tf_op jit(solution)/shard_map/give_back/all_to_all | solution.py:35
  95.9 0.3 fold.1
  96.2 16.8 %all_to_all.36.back_ref = bf16[16,24,128]{2,1,0:T(8,128)(2,1)S(1)} all-to-all(bf16[16,24,128]{2,1,0:T(8,128)(2,1)S(1)} %fold.1), channel_id=1, replica_groups=mesh['y'=4,'zh'=4,'zl'=4,'c'=2,'x'=4] {'zh','zl'}, dimensions={0} | all-to-all | bytes 196608 | tf_op jit(solution)/shard_map/give_back/all_to_all | solution.py:35
  113.0 1.6 other_half.1
  114.6 4.7 %collective-permute-start = (bf16[16,104,128]{2,1,0:T(8,128)(2,1)S(1)}, bf16[16,104,128]{2,1,0:T(8,128)(2,1)S(1)}, u32[]{:S(2)}, u32[]{:S(2)}) collective-permute-start(bf16[16,104,128]{2,1,0:T(8,128)(2,1)S(1)} %other_half.1), channel_id=1, source_target_pairs={{0,4},{4,0},{1,5},{5,1},{2,6},{6,2},{3,7},{7,3},{8,12},{12,8},{9,1... | collective-permute-start | bytes 1277960 | tf_op jit(solution)/shard_map/encoder_grad/ppermute | solution.py:593
  119.2 1.6 own_half.1
  120.8 0.1 add_convert_fusion
  120.9 14.4 %all_to_all.37 = bf16[16,104,128]{2,1,0:T(8,128)(2,1)S(1)} all-to-all(bf16[16,104,128]{2,1,0:T(8,128)(2,1)S(1)} %add_convert_fusion), channel_id=1, replica_groups={{0,8,16,24,128,136,144,152,256,264,272,280,384,392,400,408},{32,40,48,5..., dimensions={0} | all-to-all | bytes 851968 | tf_op jit(solution)/shard_map/reduce/all_to_all | solution.py:52
  135.5 16.3 %all_to_all.38 = bf16[4,104,128]{2,1,0:T(8,128)(2,1)S(1)} all-to-all(bf16[4,104,128]{2,1,0:T(8,128)(2,1)S(1)} %broadcast_in_dim.30), channel_id=1, replica_groups=mesh['y'=4,'zh'=4,'zl'=4,'c'=2,'x'=4] {'zh'}, dimensions={0} | all-to-all | bytes 212992 | tf_op jit(solution)/shard_map/reduce/all_to_all | solution.py:35
  151.8 16.4 %all_to_all.39 = bf16[16,104,128]{2,1,0:T(8,128)(2,1)S(1)} all-to-all(bf16[16,104,128]{2,1,0:T(8,128)(2,1)S(1)} %broadcast_in_dim.31), channel_id=1, replica_groups={{0,8,16,24,128,136,144,152,256,264,272,280,384,392,400,408},{32,40,48,5..., dimensions={0} | all-to-all | bytes 851968 | tf_op jit(solution)/shard_map/reduce/all_to_all | solution.py:52
  168.3 4.5 %all-gather.2 = bf16[32,104,128]{2,1,0:T(8,128)(2,1)S(1)} all-gather(bf16[16,104,128]{2,1,0:T(8,128)(2,1)S(1)} %all_to_all.39), channel_id=4, replica_groups=mesh['y'=4,'zh'=4,'zl'=4,'c'=2,'x'=4] {'c'}, dimensions={0}, use_global_device_ids=true | all-gather | bytes 1277952 | tf_op jit(solution)/shard_map/reduce/all_gather | solution.py:607
  172.8 1.3 unpack.1
  (21 shorter events, 0.2 us)
Async XLA Ops:
  0.6 20.3 %copy-start.5 = (f32[768,32]{0,1:T(8,128)S(1)}, f32[768,32]{0,1:T(8,128)}, u32[]{:S(2)}) copy-start(f32[768,32]{0,1:T(8,128)} %param.21) | copy-start | bytes 294916
  0.6 20.4 %copy-start.6 = (f32[768]{0:T(1024)S(1)}, f32[768]{0:T(1024)}, u32[]{:S(2)}) copy-start(f32[768]{0:T(1024)} %param.18) | copy-start | bytes 9220
  5.1 28.5 %all-to-all-start = ((bf16[16,56,128]{2,1,0:T(8,128)(2,1)}), bf16[16,56,128]{2,1,0:T(8,128)(2,1)S(1)}, u32[]{:S(2)}, u32[]{:S(2)}) async-start(bf16[16,56,128]{2,1,0:T(8,128)(2,1)} %get-tuple-element.16), calls=%async_computation | async-start | bytes 458752 | tf_op jit(solution)/shard_map/dispatch/all_to_all | solution.py:35
  20.9 56.4 %copy-start.3 = (s32[128]{0:T(128)S(1)}, s32[128]{0:T(128)}, u32[]{:S(2)}) copy-start(s32[128]{0:T(128)} %param.14) | copy-start | bytes 1540
  20.9 56.4 %copy-start.4 = (s32[128]{0:T(128)S(1)}, s32[128]{0:T(128)}, u32[]{:S(2)}) copy-start(s32[128]{0:T(128)} %param.15) | copy-start | bytes 1540
  34.8 29.7 %all-to-all-start.1 = ((bf16[32,32,256]{2,1,0:T(8,128)(2,1)}), bf16[32,32,256]{2,1,0:T(8,128)(2,1)S(1)}, u32[]{:S(2)}, u32[]{:S(2)}) async-start(bf16[32,32,256]{2,1,0:T(8,128)(2,1)} %bitcast.9), calls=%async_computation.1 | async-start | bytes 1048576 | tf_op jit(solution)/shard_map/dispatch/all_to_all | solution.py:35
  67.5 45.5 %copy-start = (bf16[144,4,2048]{2,1,0:T(4,128)(2,1)S(1)}, bf16[144,4,2048]{2,1,0:T(4,128)(2,1)}, u32[]{:S(2)}) copy-start(bf16[144,4,2048]{2,1,0:T(4,128)(2,1)} %features_ref.3) | copy-start | bytes 7077892
  67.5 45.5 %copy-start.1 = (bf16[576,192]{1,0:T(8,128)(2,1)S(1)}, bf16[576,192]{1,0:T(8,128)(2,1)}, u32[]{:S(2)}) copy-start(bf16[576,192]{1,0:T(8,128)(2,1)} %get-tuple-element.26.mask_ref) | copy-start | bytes 663556
  67.5 45.5 %copy-start.2 = (bf16[256,144]{1,0:T(8,128)(2,1)S(1)}, bf16[256,144]{1,0:T(8,128)(2,1)}, u32[]{:S(2)}) copy-start(bf16[256,144]{1,0:T(8,128)(2,1)} %get-tuple-element.24.placing_ref) | copy-start | bytes 221188
  114.6 6.2 %collective-permute-start = (bf16[16,104,128]{2,1,0:T(8,128)(2,1)S(1)}, bf16[16,104,128]{2,1,0:T(8,128)(2,1)S(1)}, u32[]{:S(2)}, u32[]{:S(2)}) collective-permute-start(bf16[16,104,128]{2,1,0:T(8,128)(2,1)S(1)} %other_half.1), channel_id=1, source_target_pairs={{0,4},{4,0},{1,5},{5,1},{2,6},{6,2},{3,7},{7,3},{8,12},{12,8},{9,1... | collective-permute-start | bytes 1277960 | tf_op jit(solution)/shard_map/encoder_grad/ppermute | solution.py:593

commit v7 on v5

--- a/solution.py
+++ b/solution.py
@@ -43,7 +43,7 @@
         for first in range(0, far_count, length):
             stretch = [(first + core * length // 2 + at) % far_count for at in range(length)]
             groups.append(
-                [(line * far_count + far) * cores + core for line in range(lines) for far in stretch]
+                [(line * far_count + far) * cores + core for far in stretch for line in range(lines)]
             )
     return groups
 

time: 175 us -> 178 us (1.017)
  blocking collectives: 112 us -> 115 us
    all_gather x1, blocking collectives: 3.83 us -> 6.02 us  [on_device(): all_parts = lax.all_gather(swap_plane(copies), 'c', axis=0)]
where the time goes in v7:
time: 178 us; the launch traced here: 177 us
  blocking collectives  115 us (65%)
  starting transfers between devices  32 us (18%)
  Pallas kernels  16.6 us (9%)
  waiting for transfers between devices  12.4 us (7%)
    all_to_all x3, blocking collectives, swap(): return lax.all_to_all(blocks, axes, split_axis=0, concat_axis=0, tiled=True)  48.4 us
    all_to_all x2, blocking collectives, swap_plane(): lax.all_to_all(blocks, ENC, split_axis=0, concat_axis=0, axis_index_group...  33.4 us
    all_to_all x2, starting transfers between devices, swap(): return lax.all_to_all(blocks, axes, split_axis=0, concat_axis=0, tiled=True)  28.4 us
    all_gather x1, blocking collectives, on_device(): weights = lax.all_gather(far_held, NEAR, axis=0)  16.9 us
    pallas_call x8, Pallas kernels, run(): pl.pallas_call(kernel, out_shape=out_shape, in_specs=[kinds[spec] for spe...  16.6 us
    all_to_all x2, waiting for transfers between devices, swap(): return lax.all_to_all(blocks, axes, split_axis=0, concat_axis=0, tiled=True)  12.4 us
    all_gather x1, blocking collectives, on_device(): all_logits = lax.all_gather(part_logits, 'x', axis=0)  9.78 us
    all_gather x1, blocking collectives, on_device(): all_parts = lax.all_gather(swap_plane(copies), 'c', axis=0)  6.02 us
  transfers between devices with their start and end apart: 3, of which 1 were waited for; matrix products, arithmetic and copies ran while one was open for 0% of the time, Pallas kernels for 1%

profile of v7, /device:TPU:1, one launch (start us, length us, event | category | flops | bytes accessed | tf_op | source)
XLA Modules:
  0.0 177.0 jit_solution(11645111688616576606)
XLA Ops:
  0.7 4.5 %send.1 = (bf16[16,56,128]{2,1,0:T(8,128)(2,1)}, bf16[576,192]{1,0:T(8,128)(2,1)}, bf16[256,144]{1,0:T(8,128)(2,1)}) custom-call(s32[1]{0:T(128)} %bitcast.place_ref, s32[1,144]{1,0:T(1,128)} %bitcast.37, s32[1,144]{1,0:T(1,128)} %bitcast.38, s32[1,128]{1,0:T(1,128)} %bitcast.30, bf16[6,2304]{1,0:T(8,128)(2,1)} %refs_3_.1, bf16[6,768]{1,0:T(8,128)(2,1)} %refs_4_.1, ...), custom_call_target="tpu_custom_call" | custom-call | tf_op jit(solution)/shard_map/encode/send/pallas_call | solution.py:449
  5.1 15.8 %all-to-all-start = ((bf16[16,56,128]{2,1,0:T(8,128)(2,1)}), bf16[16,56,128]{2,1,0:T(8,128)(2,1)S(1)}, u32[]{:S(2)}, u32[]{:S(2)}) async-start(bf16[16,56,128]{2,1,0:T(8,128)(2,1)} %get-tuple-element.16), calls=%async_computation | async-start | bytes 458752 | tf_op jit(solution)/shard_map/dispatch/all_to_all | solution.py:35
  20.9 0.1 reshape.33
  21.1 0.1 reshape.32.gain_ref
  21.2 12.4 %all-to-all-done.received_ref = bf16[16,56,128]{2,1,0:T(8,128)(2,1)S(1)} async-done(((bf16[16,56,128]{2,1,0:T(8,128)(2,1)}), bf16[16,56,128]{2,1,0:T(8,128)(2,1)S(1)}, u32[]{:S(2)}, u32[]{:S(2)}) %all-to-all-start) | async-done | bytes 229408 | tf_op jit(solution)/shard_map/dispatch/all_to_all | solution.py:35
  33.7 1.2 turn.1
  34.8 12.7 %all-to-all-start.1 = ((bf16[32,32,256]{2,1,0:T(8,128)(2,1)}), bf16[32,32,256]{2,1,0:T(8,128)(2,1)S(1)}, u32[]{:S(2)}, u32[]{:S(2)}) async-start(bf16[32,32,256]{2,1,0:T(8,128)(2,1)} %bitcast.9), calls=%async_computation.1 | async-start | bytes 1048576 | tf_op jit(solution)/shard_map/dispatch/all_to_all | solution.py:35
  47.5 0.1 pad_add_fusion.place_ref
  47.6 16.9 %all-gather = bf16[3840,128]{1,0:T(8,128)(2,1)S(1)} all-gather(bf16[480,128]{1,0:T(8,128)(2,1)S(1)} %get-tuple-element.18), channel_id=2, replica_groups=mesh['y'=4,'zh'=4,'zl'=4,'c'=2,'x'=4] {'y','c'}, dimensions={0}, use_global_device_ids=true | all-gather | bytes 1105920 | tf_op jit(solution)/shard_map/weights/all_gather | solution.py:531
  64.5 3.0 %forward.1 = (f32[1,32]{1,0:T(1,128)S(1)}, f32[3,256,256]{2,1,0:T(8,128)S(1)}, bf16[256,576]{1,0:T(8,128)(2,1)S(1)}, bf16[4,192,640]{2,1,0:T(8,128)(2,1)S(1)}) custom-call(s32[3]{0:T(128)S(1)} %pad_add_fusion.place_ref, bf16[4,256,256]{2,1,0:T(8,128)(2,1)S(1)} %bitcast.22, bf16[8,480,128]{2,1,0:T(8,128)(2,1)S(1)} %bitcast.24, ...), custom_call_target="tpu_custom_call" | custom-call | tf_op jit(solution)/shard_map/attend/forward/pallas_call | solution.py:449
  67.5 9.8 %all-gather.3.part_logits_ref = f32[4,1,32]{2,1,0:T(1,128)S(1)} all-gather(f32[1,1,32]{2,1,0:T(1,128)S(1)} %bitcast.33), channel_id=3, replica_groups=mesh['y'=4,'zh'=4,'zl'=4,'c'=2,'x'=4] {'x'}, dimensions={0}, use_global_device_ids=true | all-gather | bytes 640 | tf_op jit(solution)/shard_map/attend/all_gather | solution.py:548
  77.3 3.2 %backward.1 = (f32[1,32]{1,0:T(1,128)}, bf16[4,8,48,128]{3,2,1,0:T(8,128)(2,1)S(1)}) custom-call(s32[3]{0:T(128)S(1)} %pad_add_fusion.place_ref, f32[4,1,32]{2,1,0:T(1,128)S(1)} %all-gather.3.part_logits_ref, s32[1,128]{1,0:T(1,128)S(1)} %bitcast.31, s32[1,128]{1,0:T(1,128)S(1)} %bitcast.32, bf16[4,256,256]{2,1,0:T(8,128)(2,1)S(1)} %bitcast.23, ...), custom_call_target="tpu_custom_call" | custom-call | tf_op jit(solution)/shard_map/attend/backward/pallas_call | solution.py:449
  80.5 15.5 %all_to_all.35 = bf16[32,48,128]{2,1,0:T(8,128)(2,1)S(1)} all-to-all(bf16[32,48,128]{2,1,0:T(8,128)(2,1)S(1)} %bitcast.29), channel_id=1, replica_groups=mesh['y'=4,'zh'=4,'zl'=4,'c'=2,'x'=4] {'x','y','c'}, dimensions={0} | all-to-all | bytes 786432 | tf_op jit(solution)/shard_map/give_back/all_to_all | solution.py:35
  96.0 0.3 fold.1
  96.3 17.0 %all_to_all.36.back_ref = bf16[16,24,128]{2,1,0:T(8,128)(2,1)S(1)} all-to-all(bf16[16,24,128]{2,1,0:T(8,128)(2,1)S(1)} %fold.1), channel_id=1, replica_groups=mesh['y'=4,'zh'=4,'zl'=4,'c'=2,'x'=4] {'zh','zl'}, dimensions={0} | all-to-all | bytes 196608 | tf_op jit(solution)/shard_map/give_back/all_to_all | solution.py:35
  113.3 1.6 other_half.1
  114.9 3.6 %collective-permute-start = (bf16[16,104,128]{2,1,0:T(8,128)(2,1)S(1)}, bf16[16,104,128]{2,1,0:T(8,128)(2,1)S(1)}, u32[]{:S(2)}, u32[]{:S(2)}) collective-permute-start(bf16[16,104,128]{2,1,0:T(8,128)(2,1)S(1)} %other_half.1), channel_id=1, source_target_pairs={{0,4},{4,0},{1,5},{5,1},{2,6},{6,2},{3,7},{7,3},{8,12},{12,8},{9,1... | collective-permute-start | bytes 1277960 | tf_op jit(solution)/shard_map/encoder_grad/ppermute | solution.py:591
  118.5 1.6 own_half.1
  120.1 0.1 add_convert_fusion
  120.2 16.0 %all_to_all.37 = bf16[16,104,128]{2,1,0:T(8,128)(2,1)S(1)} all-to-all(bf16[16,104,128]{2,1,0:T(8,128)(2,1)S(1)} %add_convert_fusion), channel_id=1, replica_groups={{0,128,256,384,8,136,264,392,16,144,272,400,24,152,280,408},{32,160,288..., dimensions={0} | all-to-all | bytes 851968 | tf_op jit(solution)/shard_map/reduce/all_to_all | solution.py:52
  136.3 15.9 %all_to_all.38 = bf16[4,104,128]{2,1,0:T(8,128)(2,1)S(1)} all-to-all(bf16[4,104,128]{2,1,0:T(8,128)(2,1)S(1)} %broadcast_in_dim.30), channel_id=1, replica_groups=mesh['y'=4,'zh'=4,'zl'=4,'c'=2,'x'=4] {'zh'}, dimensions={0} | all-to-all | bytes 212992 | tf_op jit(solution)/shard_map/reduce/all_to_all | solution.py:35
  152.3 17.4 %all_to_all.39 = bf16[16,104,128]{2,1,0:T(8,128)(2,1)S(1)} all-to-all(bf16[16,104,128]{2,1,0:T(8,128)(2,1)S(1)} %broadcast_in_dim.31), channel_id=1, replica_groups={{0,128,256,384,8,136,264,392,16,144,272,400,24,152,280,408},{32,160,288..., dimensions={0} | all-to-all | bytes 851968 | tf_op jit(solution)/shard_map/reduce/all_to_all | solution.py:52
  169.7 6.0 %all-gather.2 = bf16[32,104,128]{2,1,0:T(8,128)(2,1)S(1)} all-gather(bf16[16,104,128]{2,1,0:T(8,128)(2,1)S(1)} %all_to_all.39), channel_id=4, replica_groups=mesh['y'=4,'zh'=4,'zl'=4,'c'=2,'x'=4] {'c'}, dimensions={0}, use_global_device_ids=true | all-gather | bytes 1277952 | tf_op jit(solution)/shard_map/reduce/all_gather | solution.py:605
  175.7 1.3 unpack.1
  (21 shorter events, 0.2 us)
Async XLA Ops:
  0.6 20.3 %copy-start.5 = (f32[768,32]{0,1:T(8,128)S(1)}, f32[768,32]{0,1:T(8,128)}, u32[]{:S(2)}) copy-start(f32[768,32]{0,1:T(8,128)} %param.21) | copy-start | bytes 294916
  0.6 20.4 %copy-start.6 = (f32[768]{0:T(1024)S(1)}, f32[768]{0:T(1024)}, u32[]{:S(2)}) copy-start(f32[768]{0:T(1024)} %param.18) | copy-start | bytes 9220
  5.1 28.5 %all-to-all-start = ((bf16[16,56,128]{2,1,0:T(8,128)(2,1)}), bf16[16,56,128]{2,1,0:T(8,128)(2,1)S(1)}, u32[]{:S(2)}, u32[]{:S(2)}) async-start(bf16[16,56,128]{2,1,0:T(8,128)(2,1)} %get-tuple-element.16), calls=%async_computation | async-start | bytes 458752 | tf_op jit(solution)/shard_map/dispatch/all_to_all | solution.py:35
  20.9 56.4 %copy-start.3 = (s32[128]{0:T(128)S(1)}, s32[128]{0:T(128)}, u32[]{:S(2)}) copy-start(s32[128]{0:T(128)} %param.14) | copy-start | bytes 1540
  20.9 56.4 %copy-start.4 = (s32[128]{0:T(128)S(1)}, s32[128]{0:T(128)}, u32[]{:S(2)}) copy-start(s32[128]{0:T(128)} %param.15) | copy-start | bytes 1540
  34.8 29.7 %all-to-all-start.1 = ((bf16[32,32,256]{2,1,0:T(8,128)(2,1)}), bf16[32,32,256]{2,1,0:T(8,128)(2,1)S(1)}, u32[]{:S(2)}, u32[]{:S(2)}) async-start(bf16[32,32,256]{2,1,0:T(8,128)(2,1)} %bitcast.9), calls=%async_computation.1 | async-start | bytes 1048576 | tf_op jit(solution)/shard_map/dispatch/all_to_all | solution.py:35
  67.5 45.8 %copy-start = (bf16[144,4,2048]{2,1,0:T(4,128)(2,1)S(1)}, bf16[144,4,2048]{2,1,0:T(4,128)(2,1)}, u32[]{:S(2)}) copy-start(bf16[144,4,2048]{2,1,0:T(4,128)(2,1)} %features_ref.3) | copy-start | bytes 7077892
  67.5 45.8 %copy-start.1 = (bf16[576,192]{1,0:T(8,128)(2,1)S(1)}, bf16[576,192]{1,0:T(8,128)(2,1)}, u32[]{:S(2)}) copy-start(bf16[576,192]{1,0:T(8,128)(2,1)} %get-tuple-element.26.mask_ref) | copy-start | bytes 663556
  67.5 45.8 %copy-start.2 = (bf16[256,144]{1,0:T(8,128)(2,1)S(1)}, bf16[256,144]{1,0:T(8,128)(2,1)}, u32[]{:S(2)}) copy-start(bf16[256,144]{1,0:T(8,128)(2,1)} %get-tuple-element.24.placing_ref) | copy-start | bytes 221188
  114.9 5.2 %collective-permute-start = (bf16[16,104,128]{2,1,0:T(8,128)(2,1)S(1)}, bf16[16,104,128]{2,1,0:T(8,128)(2,1)S(1)}, u32[]{:S(2)}, u32[]{:S(2)}) collective-permute-start(bf16[16,104,128]{2,1,0:T(8,128)(2,1)S(1)} %other_half.1), channel_id=1, source_target_pairs={{0,4},{4,0},{1,5},{5,1},{2,6},{6,2},{3,7},{7,3},{8,12},{12,8},{9,1... | collective-permute-start | bytes 1277960 | tf_op jit(solution)/shard_map/encoder_grad/ppermute | solution.py:591
